TPU v7x, 128 devices: a whole 4x4x4 slice. The times are simulated.
128 devices in a mesh: row: 8 (over x, core), col: 16 (over z, y).
Axes of the slice: x: 4, y: 4, z: 4, core: 2. Of those that a mesh axis runs over, the one named last changes fastest.
Arguments:
- features: bfloat16 [128, 512, 192], P('row', 'col'), may hold values from -6 to 6
- selectors: bfloat16 [128, 512, 4, 16], P('row', 'col'), may hold values from -2 to 2
- log_decay: bfloat16 [128, 512, 2, 6], P('row', 'col'), may hold values from -0.8 to 0, as said below
- in_weight: bfloat16 [192, 768], replicated, may hold values from -0.4375 to 0.4375
- out_weight: bfloat16 [384, 192], replicated, may hold values from -0.3125 to 0.3125
- cotangent: bfloat16 [128, 512, 192], P('row', 'col'), may hold values from -6 to 6
Outputs:
- block_out: bfloat16 [128, 512, 192], P('row', 'col')
- input_grad: bfloat16 [128, 512, 192], P('row', 'col')
- in_weight_grad: float32 [192, 768], replicated
- out_weight_grad: float32 [384, 192], replicated
Inputs may be any that keep to these rules, and one draw needn't show every extreme that they name: `log_decay`: log-decays are negative.
All inputs are finite; a program needn't handle non-finite values.
Results may differ from a plain program's by a relative error of at most 0.012.
Values may be sent and summed in bfloat16 or wider, within the bound.
No kernel may reach another device: no remote copies, remote signals or barrier semaphores. Data moves between devices by JAX's collectives and lax.ppermute only.
A program may use at most 128 MiB of HBM per device.

v0:
```python
import jax
import jax.numpy as jnp
from jax import lax
from jax.sharding import PartitionSpec as P

HIGHEST_PRECISION = lax.Precision.HIGHEST


def prefix(value, axis, join, neutral, backward):
    count, mine = (lax.axis_size(axis), lax.axis_index(axis))
    pieces = jax.tree.map(lambda part: lax.all_gather(part, axis), value)
    if backward:
        pieces = jax.tree.map(lambda part: part[::-1], pieces)
        mine = count - 1 - mine
    so_far = jax.tree.map(
        lambda part, zero: jnp.full_like(part, 0) + jnp.asarray(zero, part.dtype), value, neutral
    )

    def turn(position, so_far):
        longer = join(so_far, jax.tree.map(lambda part: part[position], pieces))
        return jax.tree.map(lambda new, old: jnp.where(position < mine, new, old), longer, so_far)

    return lax.fori_loop(0, count - 1, turn, so_far)


def forward_local(values, b_sel, c_sel, log_step):
    batch_size, length, channels = values.shape
    head_count = log_step.shape[2]
    head_dim = channels // head_count
    cumlog = jnp.cumsum(log_step.astype(jnp.float32), axis=1)
    totals = cumlog[:, -1]
    scores = jnp.einsum("btn,bsn->bts", c_sel, b_sel, preferred_element_type=jnp.float32)
    positions = jnp.arange(length)
    causal = positions[:, None] >= positions[None, :]
    spread = cumlog[:, :, None, :] - cumlog[:, None, :, :]
    weights = jnp.exp(jnp.where(causal[None, :, :, None], spread, -jnp.inf)) * scores[:, :, :, None]
    per_head = values.astype(jnp.float32).reshape(batch_size, length, head_count, head_dim)
    output = jnp.einsum("btsh,bshp->bthp", weights, per_head, precision=HIGHEST_PRECISION)
    fading = jnp.exp(totals[:, None, :] - cumlog)
    states = jnp.einsum(
        "bsh,bshp,bsn->bhpn",
        fading,
        per_head,
        b_sel.astype(jnp.float32),
        precision=HIGHEST_PRECISION,
    )
    return (output.reshape(batch_size, length, channels), totals, states, cumlog)


def add_incoming(output, c_sel, cumlog, incoming):
    batch_size, length, channels = output.shape
    carried_term = jnp.exp(cumlog)[:, :, :, None] * jnp.einsum(
        "bhpn,btn->bthp", incoming, c_sel.astype(jnp.float32), precision=HIGHEST_PRECISION
    )
    return output + carried_term.reshape(batch_size, length, channels)


def backward_local(adjoint, b_sel, c_sel, log_step):
    batch_size, length, channels = adjoint.shape
    head_count = log_step.shape[2]
    head_dim = channels // head_count
    cumlog = jnp.cumsum(log_step.astype(jnp.float32), axis=1)
    totals = cumlog[:, -1]
    scores = jnp.einsum("bsn,btn->bst", b_sel, c_sel, preferred_element_type=jnp.float32)
    positions = jnp.arange(length)
    onward = positions[:, None] <= positions[None, :]
    spread = cumlog[:, None, :, :] - cumlog[:, :, None, :]
    weights = jnp.exp(jnp.where(onward[None, :, :, None], spread, -jnp.inf)) * scores[:, :, :, None]
    per_head = adjoint.astype(jnp.float32).reshape(batch_size, length, head_count, head_dim)
    output = jnp.einsum("bsth,bthp->bshp", weights, per_head, precision=HIGHEST_PRECISION)
    rising = jnp.exp(cumlog)
    states = jnp.einsum(
        "bth,bthp,btn->bhpn",
        rising,
        per_head,
        c_sel.astype(jnp.float32),
        precision=HIGHEST_PRECISION,
    )
    return (output.reshape(batch_size, length, channels), totals, states, cumlog)


def add_outgoing(output, b_sel, cumlog, totals, incoming):
    batch_size, length, channels = output.shape
    carried_term = jnp.exp(totals[:, None, :] - cumlog)[:, :, :, None] * jnp.einsum(
        "bhpn,bsn->bshp", incoming, b_sel.astype(jnp.float32), precision=HIGHEST_PRECISION
    )
    return output + carried_term.reshape(batch_size, length, channels)


def combine_parts(first_part, second_part):
    return (
        first_part[0] + second_part[0],
        jnp.exp(second_part[0])[:, :, None, None] * first_part[1] + second_part[1],
    )


def on_device(features, selectors, log_decay, in_weight, out_weight, cotangent):
    rows_dev, cols_dev, model_dim = features.shape
    channels = out_weight.shape[0]
    head_count = log_decay.shape[3]
    state_dim = selectors.shape[3]
    tokens_dev = rows_dev * cols_dev
    col_count = lax.axis_size("col")
    row_count = lax.axis_size("row")

    def carry_zero(batch_size):
        return (
            jnp.zeros((batch_size, head_count), jnp.float32),
            jnp.zeros((batch_size, head_count, channels // head_count, state_dim), jnp.float32),
        )

    projected = jnp.dot(
        features.reshape(tokens_dev, model_dim), in_weight, preferred_element_type=jnp.float32
    )
    scan_values = projected[:, :channels].astype(jnp.bfloat16).reshape(rows_dev, cols_dev, channels)
    gates = projected[:, channels:].astype(jnp.bfloat16).reshape(rows_dev, cols_dev, channels)
    row_sel = selectors[:, :, 0:2]
    row_log = log_decay[:, :, 0]
    col_sel = selectors[:, :, 2:4]
    col_log = log_decay[:, :, 1]
    output, totals, states, cumlog = forward_local(
        scan_values, row_sel[:, :, 0], row_sel[:, :, 1], row_log
    )
    incoming = prefix((totals, states), "col", combine_parts, carry_zero(rows_dev), False)
    row_out = add_incoming(output, row_sel[:, :, 1], cumlog, incoming[1]).astype(jnp.bfloat16)
    turned_sel = jnp.swapaxes(col_sel, 0, 1)
    turned_log = jnp.swapaxes(col_log, 0, 1)
    output, totals, states, cumlog = forward_local(
        jnp.swapaxes(row_out, 0, 1), turned_sel[:, :, 0], turned_sel[:, :, 1], turned_log
    )
    incoming = prefix((totals, states), "row", combine_parts, carry_zero(cols_dev), False)
    col_out = jnp.swapaxes(
        add_incoming(output, turned_sel[:, :, 1], cumlog, incoming[1]), 0, 1
    ).astype(jnp.bfloat16)
    col_float = col_out.astype(jnp.float32)
    gate_float = gates.astype(jnp.float32)
    sigmoid_gate = jax.nn.sigmoid(gate_float)
    hidden = (col_float * gate_float * sigmoid_gate).astype(jnp.bfloat16)
    hidden_flat = hidden.reshape(tokens_dev, channels)
    mixed = jnp.dot(hidden_flat, out_weight, preferred_element_type=jnp.float32).reshape(
        rows_dev, cols_dev, model_dim
    )
    block_out = (features.astype(jnp.float32) + mixed).astype(jnp.bfloat16)
    cot_flat = cotangent.reshape(tokens_dev, model_dim)
    hidden_grad = jnp.dot(cot_flat, out_weight.T, preferred_element_type=jnp.float32).reshape(
        rows_dev, cols_dev, channels
    )
    col_grad = (hidden_grad * gate_float * sigmoid_gate).astype(jnp.bfloat16)
    gate_grad = (
        hidden_grad * col_float * sigmoid_gate * (1.0 + gate_float * (1.0 - sigmoid_gate))
    ).astype(jnp.bfloat16)
    turned_sel = jnp.swapaxes(col_sel, 0, 1)
    turned_log = jnp.swapaxes(col_log, 0, 1)
    output, totals, states, cumlog = backward_local(
        jnp.swapaxes(col_grad, 0, 1), turned_sel[:, :, 0], turned_sel[:, :, 1], turned_log
    )
    incoming = prefix((totals, states), "row", combine_parts, carry_zero(cols_dev), True)
    row_grad = jnp.swapaxes(
        add_outgoing(output, turned_sel[:, :, 0], cumlog, totals, incoming[1]), 0, 1
    ).astype(jnp.bfloat16)
    output, totals, states, cumlog = backward_local(
        row_grad, row_sel[:, :, 0], row_sel[:, :, 1], row_log
    )
    incoming = prefix((totals, states), "col", combine_parts, carry_zero(rows_dev), True)
    value_grad = add_outgoing(output, row_sel[:, :, 0], cumlog, totals, incoming[1]).astype(
        jnp.bfloat16
    )
    joined = jnp.concatenate([value_grad, gate_grad], axis=-1).reshape(tokens_dev, 2 * channels)
    pulled = jnp.dot(joined, in_weight.T, preferred_element_type=jnp.float32).reshape(
        rows_dev, cols_dev, model_dim
    )
    input_grad = (cotangent.astype(jnp.float32) + pulled).astype(jnp.bfloat16)
    in_part = jnp.dot(
        features.reshape(tokens_dev, model_dim).T, joined, preferred_element_type=jnp.float32
    )
    out_part = jnp.dot(hidden_flat.T, cot_flat, preferred_element_type=jnp.float32)
    in_total, out_total = lax.psum((in_part, out_part), ("row", "col"))
    total_tokens = tokens_dev * row_count * col_count
    scale = float(total_tokens) ** (-0.5)
    return (block_out, input_grad, in_total * scale, out_total * scale)


def solution(mesh):
    in_specs = (
        P("row", "col", None),
        P("row", "col", None, None),
        P("row", "col", None, None),
        P(),
        P(),
        P("row", "col", None),
    )
    out_specs = (P("row", "col", None), P("row", "col", None), P(), P())
    return jax.shard_map(
        on_device, mesh=mesh, in_specs=in_specs, out_specs=out_specs, check_vma=False
    )
```

profile of v0, /device:TPU:1, one launch (start us, length us, event | category | flops | bytes accessed | tf_op | source)
XLA Modules:
  0.0 623.2 jit_solution(1029519418428057804)
XLA Ops:
  8.4 1.9 fusion.140
  13.1 1.7 fusion.54
  15.7 21.8 %all-gather = f32[256,1,6]{2,0,1:T(8,128)S(1)} all-gather(f32[16,1,6]{2,0,1:T(8,128)S(1)} %get-tuple-element.527), channel_id=2, replica_groups=mesh['row'=8,'col'=16] {'col'}, dimensions={0}, use_global_device_ids=true | all-gather | bytes 6528 | tf_op jit(solution)/shard_map/all_gather | solution.py:11
  41.4 1.8 copy.108
  43.5 2.4 fusion.33
  45.9 62.7 %all-gather.11.cloned.1.call-done = f32[256,6,64,16]{2,3,1,0:T(8,128)} async-done(((f32[16,6,64,16]{2,3,1,0:T(8,128)}), f32[256,6,64,16]{2,3,1,0:T(8,128)}) %all-gather.11.cloned.1.call-update) | async-done | bytes 6291472 | tf_op jit(solution)/shard_map/all_gather | solution.py:11
  108.6 33.3 %while.56 = (s32[]{:T(128)}, f32[16,6,64,16]{2,3,1,0:T(8,128)S(1)}, s32[]{:T(128)}, f32[16,16,6]{1,2,0:T(8,128)}, f32[16,16,6,64,16]{3,4,2,1,0:T(8,128)}, /*index=5*/s32[]{:T(128)}, s32[]{:T(128)}) while((s32[]{:T(128)}, f32[16,6,64,16]{2,3,1,0:T(8,128)S(1)}, s32[]{:T(128)}, f32[16,16,6]{1,2,0:T(8,128)}, ...), condition=%wide.region_2.3_spmd.clone, body=%wide.region_1.2_spmd.clone.sunk | while | flops 393220 | bytes 1181673 | solution.py:23
  111.6 1.4 fusion.159
  118.3 1.4 fusion.159
  124.9 1.4 fusion.159
  142.0 2.4 fusion.15
  145.9 2.4 fusion.12
  150.5 13.7 %all-gather.2 = f32[256,1,6]{2,0,1:T(8,128)S(1)} all-gather(f32[32,1,6]{2,0,1:T(8,128)S(1)} %get-tuple-element.529), channel_id=4, replica_groups=mesh['row'=8,'col'=16] {'row'}, dimensions={0}, use_global_device_ids=true | all-gather | bytes 6912 | tf_op jit(solution)/shard_map/all_gather | solution.py:11
  164.4 3.8 fusion.28
  168.2 47.6 %all-gather.13.cloned.1.call-done = f32[256,6,64,16]{2,3,1,0:T(8,128)} async-done(((f32[32,6,64,16]{2,3,1,0:T(8,128)}), f32[256,6,64,16]{2,3,1,0:T(8,128)}) %all-gather.13.cloned.1.call-update) | async-done | bytes 6291472 | tf_op jit(solution)/shard_map/all_gather | solution.py:11
  215.9 14.1 %while.57 = (s32[]{:T(128)}, f32[32,6,64,16]{2,3,1,0:T(8,128)S(1)}, s32[]{:T(128)}, f32[8,32,6]{2,1,0:T(8,128)S(1)}, f32[8,32,6,64,16]{3,4,2,1,0:T(8,128)}, /*index=5*/s32[]{:T(128)}, s32[]{:T(128)}) while((s32[]{:T(128)}, f32[32,6,64,16]{2,3,1,0:T(8,128)S(1)}, s32[]{:T(128)}, f32[8,32,6]{2,1,0:T(8,128)S(1)}, ...), condition=%wide.region_5.6_spmd.clone, body=%wide.region_4.5_spmd.clone.sunk | while | flops 786436 | bytes 2361705 | solution.py:23
  215.9 2.0 fusion.160
  217.9 2.0 fusion.160
  219.9 2.0 fusion.160
  221.9 2.0 fusion.160
  223.9 2.0 fusion.160
  226.0 2.0 fusion.160
  228.0 2.0 fusion.160
  230.0 2.5 fusion.38
  234.4 2.7 fusion.94
  238.1 2.4 fusion.8
  241.1 3.9 fusion.22
  245.0 63.4 %all-gather.15.cloned.1.call-done = f32[256,6,64,16]{2,3,1,0:T(8,128)} async-done(((f32[32,6,64,16]{2,3,1,0:T(8,128)}), f32[256,6,64,16]{2,3,1,0:T(8,128)}) %all-gather.15.cloned.1.call-update) | async-done | bytes 6291472 | tf_op jit(solution)/shard_map/all_gather | solution.py:11
  308.4 10.4 %rev.13 = f32[8,32,6,64,16]{3,4,2,1,0:T(8,128)} reverse(f32[8,32,6,64,16]{3,4,2,1,0:T(8,128)} %bitcast.213), dimensions={0} | reverse | bytes 12582912 | tf_op jit(solution)/shard_map/rev | solution.py:13
  318.8 14.1 %while.58 = (s32[]{:T(128)}, f32[32,6,64,16]{2,3,1,0:T(8,128)S(1)}, s32[]{:T(128)}, f32[8,32,6]{2,1,0:T(8,128)S(1)}, f32[8,32,6,64,16]{3,4,2,1,0:T(8,128)}, /*index=5*/s32[]{:T(128)}, s32[]{:T(128)}) while((s32[]{:T(128)}, f32[32,6,64,16]{2,3,1,0:T(8,128)S(1)}, s32[]{:T(128)}, f32[8,32,6]{2,1,0:T(8,128)S(1)}, ...), condition=%wide.region_7.8_spmd.clone, body=%wide.region_6.7_spmd.clone.sunk | while | flops 786436 | bytes 2361705 | solution.py:23
  318.8 2.0 fusion.161
  320.8 2.0 fusion.161
  322.8 2.0 fusion.161
  324.8 2.0 fusion.161
  326.9 2.0 fusion.161
  328.9 2.0 fusion.161
  330.9 2.0 fusion.161
  332.9 2.4 fusion.7
  336.8 2.1 fusion.51
  339.5 2.0 convolution_bitcast_fusion.1
  341.5 2.7 fusion.16
  344.2 85.0 %all-gather.17.cloned.1.call-done = f32[256,6,64,16]{2,3,1,0:T(8,128)} async-done(((f32[16,6,64,16]{2,3,1,0:T(8,128)}), f32[256,6,64,16]{2,3,1,0:T(8,128)}) %all-gather.17.cloned.1.call-update) | async-done | bytes 6291472 | tf_op jit(solution)/shard_map/all_gather | solution.py:11
  429.2 10.8 %rev.15 = f32[16,16,6,64,16]{3,4,2,1,0:T(8,128)} reverse(f32[16,16,6,64,16]{3,4,2,1,0:T(8,128)} %bitcast.212), dimensions={0} | reverse | bytes 12582912 | tf_op jit(solution)/shard_map/rev | solution.py:13
  440.0 23.3 %while.59 = (s32[]{:T(128)}, f32[16,6,64,16]{2,3,1,0:T(8,128)S(1)}, s32[]{:T(128)}, f32[16,16,6]{1,2,0:T(8,128)S(1)}, f32[16,16,6,64,16]{3,4,2,1,0:T(8,128)}, /*index=5*/s32[]{:T(128)}, s32[]{:T(128)}) while((s32[]{:T(128)}, f32[16,6,64,16]{2,3,1,0:T(8,128)S(1)}, s32[]{:T(128)}, f32[16,16,6]{1,2,0:T(8,128)S(1)}, ...), condition=%wide.region_9.10_spmd.clone, body=%wide.region_8.9_spmd.clone.sunk | while | flops 393220 | bytes 1181673 | solution.py:23
  440.1 1.5 fusion.162
  468.7 144.3 %all-reduce.3.cloned.1.call-done = (f32[192,768]{1,0:T(8,128)}, f32[384,192]{0,1:T(8,128)}) async-done(((f32[192,768]{1,0:T(8,128)}, f32[384,192]{0,1:T(8,128)}), (f32[192,768]{1,0:T(8,128)}, f32[384,192]{0,1:T(8,128)})) %all-reduce.3.cloned.1.call-update) | async-done | bytes 884752 | tf_op jit(solution)/shard_map/psum | solution.py:177
  613.1 1.9 broadcast_multiply_fusion
  615.0 1.7 broadcast_multiply_fusion.1
  (212 shorter events, 73.6 us)
Async XLA Ops:
  7.2 3.4 copy-start
  7.2 3.4 copy-start.8
  7.2 101.4 %all-gather.11.cloned.1.call-start = ((), (), s32[]{:S(2)}) async-start(), calls=%async_computation | async-start | bytes 13369344 | tf_op jit(solution)/shard_map/all_gather | solution.py:11
  11.0 1.4 copy-start.3
  14.8 201.1 %all-gather.13.cloned.1.call-start = ((), (), s32[]{:S(2)}) async-start(), calls=%async_computation.1 | async-start | bytes 14155776 | tf_op jit(solution)/shard_map/all_gather | solution.py:11
  15.7 24.7 %slice-start = ((bf16[16,32,4,16]{1,3,2,0:T(8,128)(2,1)}), bf16[16,32,2,16]{1,3,2,0:T(8,128)(2,1)S(1)}, s32[]{:S(2)}) async-start(bf16[16,32,4,16]{1,3,2,0:T(8,128)(2,1)} %param.15), calls=%async_computation.5 | async-start | bytes 262144 | tf_op jit(solution)/shard_map/slice | solution.py:119
  40.6 2.9 copy-start.21
  108.6 33.3 %copy-start.14 = (f32[16,32,6]{1,2,0:T(8,128)S(1)}, f32[16,32,6]{1,2,0:T(8,128)}, u32[]{:S(2)}) copy-start(f32[16,32,6]{1,2,0:T(8,128)} %copy.92) | copy-start | bytes 36868
  144.7 1.2 copy-start.11
  145.9 2.5 copy-start.1
  148.3 1.3 copy-start.7
  148.4 160.0 %all-gather.15.cloned.1.call-start = ((), (), s32[]{:S(2)}) async-start(), calls=%async_computation.2 | async-start | bytes 14155776 | tf_op jit(solution)/shard_map/all_gather | solution.py:11
  149.4 15.0 %copy-start.20 = (f32[32,16,6]{1,2,0:T(8,128)S(1)}, f32[32,16,6]{1,2,0:T(8,128)}, u32[]{:S(2)}) copy-start(f32[32,16,6]{1,2,0:T(8,128)} %copy.102) | copy-start | bytes 36868
  149.6 80.3 %copy-start.5 = (f32[32,16,6]{1,2,0:T(8,128)}, f32[32,16,6]{1,2,0:T(8,128)S(1)}, u32[]{:S(2)}) copy-start(f32[32,16,6]{1,2,0:T(8,128)S(1)} %copy.106) | copy-start | bytes 36868
  230.0 2.5 copy-start.12
  234.4 3.3 copy-start.6
  237.2 0.9 copy-start.10
  238.1 2.5 copy-start.2
  238.1 2.7 copy-start.13
  240.6 188.6 %all-gather.17.cloned.1.call-start = ((), (), s32[]{:S(2)}) async-start(), calls=%async_computation.3 | async-start | bytes 13369344 | tf_op jit(solution)/shard_map/all_gather | solution.py:11
  335.6 1.2 copy-start.15
  335.6 1.2 copy-start.16
  336.8 2.4 copy-start.17
  338.9 2.6 copy-start.22
  338.9 274.1 %all-reduce.3.cloned.1.call-start = ((), (), s32[]{:S(2)}) async-start(), calls=%async_computation.4 | async-start | bytes 1769472 | tf_op jit(solution)/shard_map/psum | solution.py:177
  440.0 23.3 %copy-start.4 = (f32[16,6,64,32]{2,3,1,0:T(8,128)S(1)}, f32[16,6,64,32]{2,3,1,0:T(8,128)}, u32[]{:S(2)}) copy-start(f32[16,6,64,32]{2,3,1,0:T(8,128)} %fusion.16) | copy-start | bytes 2359300
  464.3 1.0 copy-start.9
  464.3 1.1 copy-start.23
  465.3 1.3 copy-start.19
  465.4 2.2 copy-start.18
Sparse Core Ops, SparseCore 0:
  14.9 93.6 all-gather.10
  148.5 67.3 all-gather.12
  240.7 67.6 all-gather.14
  339.1 90.1 all-gather.16
  466.7 146.3 all-reduce.2
where the time goes:
time: 626 us; the launch traced here: 623 us
  waiting for transfers between devices  403 us (64%)
  other arithmetic  78.4 us (13%)
  local copies, waits for them, and re-layouts  51 us (8%)
  matrix products  38.9 us (6%)
  blocking collectives  35.5 us (6%)
  between operations  14.4 us (2%)
    all_gather x4, waiting for transfers between devices, prefix(): pieces = jax.tree.map(lambda part: lax.all_gather(part, axis), value)  259 us
    psum x1, waiting for transfers between devices, on_device(): in_total, out_total = lax.psum((in_part, out_part), ('row', 'col'))  144 us
    select_n x44, other arithmetic, turn(): jnp.where(position < mine, new, old)  70.5 us
    all_gather x2, blocking collectives, prefix(): pieces = jax.tree.map(lambda part: lax.all_gather(part, axis), value)  35.5 us
    rev x4, local copies, waits for them, and re-layouts, prefix(): pieces = jax.tree.map(lambda part: part[::-1], pieces)  21.2 us
    exp x74, local copies, waits for them, and re-layouts, combine_parts(): jnp.exp(second_part[0])[:, :, None, None] * first_part[1] + second_part[1]  13.1 us
  transfers between devices with their start and end apart: 5, of which 5 were waited for; matrix products, arithmetic and copies ran while one was open for 4% of the time, Pallas kernels for 0%

commit v1 on v0

v1 whole, which is shorter than its diff:
```python
import jax
import jax.numpy as jnp
from jax import lax
from jax.experimental import pallas as pl
from jax.experimental.pallas import tpu as pltpu
from jax.sharding import PartitionSpec as P

BF = jnp.bfloat16
F32 = jnp.float32
MODEL = 192
CHAN = 384
TOK = 512
GROUP = 256
VMEM_LIMIT = 48 * 1024 * 1024


def iota(shape, dim):
    return lax.broadcasted_iota(jnp.int32, shape, dim)


def mm(a, b):
    return jnp.dot(a, b, preferred_element_type=F32)


def mm_t(a, b):
    return lax.dot_general(a, b, (((1,), (1,)), ((), ())), preferred_element_type=F32)


def t_mm(a, b):
    return lax.dot_general(a, b, (((0,), (0,)), ((), ())), preferred_element_type=F32)


def spread(aux, first):
    pick = (iota((256, 128), 0) - first == iota((256, 128), 1) % 16).astype(F32).astype(BF)
    return mm(aux, pick)


def scan_tokens(aux, values, by_row, forward):
    token = iota((TOK, 128), 0)
    chunk = token // 64 if by_row else (token // GROUP) * 4 + token % 4
    member = (iota((TOK, 128), 1) // 16 == chunk).astype(F32)
    b_part = (spread(aux, 192) * member).astype(BF)
    c_part = (spread(aux, 208) * member).astype(BF)
    heads = (iota((256, CHAN), 0) - 224 == iota((256, CHAN), 1) // 64).astype(F32).astype(BF)
    log_step = mm(aux, heads).astype(BF)
    here, there = iota((GROUP, GROUP), 0), iota((GROUP, GROUP), 1)
    same = (here // 64 == there // 64) if by_row else (here % 4 == there % 4)
    if forward:
        order, counted, src, out = there <= here, there <= here, b_part, c_part
    else:
        order, counted, src, out = there >= here, there > here, c_part, b_part
    add_up = (same & counted).astype(F32).astype(BF)
    halves = [slice(0, GROUP), slice(GROUP, TOK)]
    run = [mm(add_up, log_step[h]) for h in halves]
    raised = [(jnp.exp(-run[i]) * values[h]).astype(BF) for i, h in enumerate(halves)]
    states = t_mm(src[halves[0]], raised[0]) + t_mm(src[halves[1]], raised[1])
    decay = jnp.exp(t_mm(member.astype(BF), log_step))
    zero = jnp.zeros((16, CHAN), F32)
    carried = [zero] * 8
    part = lambda array, k: array[16 * k : 16 * k + 16]
    if by_row:
        steps = [(k, k + 1) for k in range(7)] if forward else [(k, k - 1) for k in range(7, 0, -1)]
    else:
        steps = [(j, j + 4) for j in range(4)] if forward else [(j + 4, j) for j in range(4)]
    for old, new in steps:
        carried[new] = part(decay, old) * (carried[old] + part(states, old))
    coming = jnp.concatenate(carried, axis=0).astype(BF)
    result = []
    for i, h in enumerate(halves):
        scores = jnp.where(order, mm_t(out[h], src[h]), 0.0).astype(BF)
        result.append(jnp.exp(run[i]) * (mm(scores, raised[i]) + mm(out[h], coming)))
    return jnp.concatenate(result, axis=0)


def to_columns(scratch, slot, token_rows):
    for l in range(CHAN // 128):
        for r in range(8):
            for j in range(4):
                scratch[l, pl.ds(r * 128 + slot + j, 16, stride=8), :] = token_rows[
                    l, pl.ds(4 * r + j, 16, stride=32), :
                ]


def split_lanes(ref, value):
    for l in range(value.shape[1] // 128):
        ref[l] = value[:, 128 * l : 128 * l + 128]


def send_rows_kernel(place, packed, cot, *outs):
    x, core = place[0] // 2, place[0] % 2
    slot = iota((TOK, 1), 0)
    q, row, j = slot // 64, (slot % 64) // 4, slot % 4
    dest = ((x + q // 2) % 4) * 2 + (core + q % 2) % 2
    pick = ((row * 32 + 4 * dest + j) == iota((TOK, TOK), 1)).astype(F32).astype(BF)
    left = mm(pick, packed[...]).astype(BF)
    right = mm(pick, cot[...]).astype(BF)
    for k in range(8):
        outs[k][:, 0:256] = left[64 * k : 64 * k + 64]
        outs[k][:, 256 : 256 + MODEL] = right[64 * k : 64 * k + 64]
        outs[k][:, 256 + MODEL :] = jnp.zeros((64, 64), BF)


def row_forward_kernel(packed, w_in, out):
    aux = packed[...]
    values = mm(aux[:, :MODEL], w_in[:, :CHAN]).astype(BF).astype(F32)
    out[...] = scan_tokens(aux, values, True, True).astype(BF)


def gate_terms(aux, cot, w_in, w_out):
    gate = mm(aux[:, :MODEL], w_in[:, CHAN:]).astype(BF).astype(F32)
    sig = 1.0 / (1.0 + jnp.exp(-gate))
    return gate, sig, mm_t(cot, w_out[...])


def col_adjoint_kernel(place, row_out, w_in, w_out, *refs):
    pieces, (out, whole, tokens, scratch) = refs[:8], refs[8:]
    x, core = place[0] // 2, place[0] % 2
    for k in range(8):
        source = ((x + 4 - k // 2) % 4) * 2 + (core + k % 2) % 2
        whole[pl.ds(pl.multiple_of(source * 64, 64), 64), :] = pieces[k][...]
    aux = whole[:, :256]
    cot = whole[:, 256 : 256 + MODEL]
    gate, sig, hidden_grad = gate_terms(aux, cot, w_in, w_out)
    col_grad = (hidden_grad * gate * sig).astype(BF).astype(F32)
    row_grad = scan_tokens(aux, col_grad, False, False)
    split_lanes(tokens, row_out[...].astype(F32))
    to_columns(scratch, 0, tokens)
    split_lanes(tokens, row_grad)
    for l in range(3):
        for j in range(4):
            scratch[l, pl.ds(4 + j, 128, stride=8), :] = tokens[l, pl.ds(j, 128, stride=4), :]
    for l in range(3):
        out[:, 128 * l : 128 * l + 128] = scratch[l].astype(BF)


def second_kernel(came, whole, packed, w_in, w_out, block, partial, out, tokens, scratch):
    split_lanes(scratch, came[...].astype(F32))
    for l in range(3):
        for j in range(4):
            tokens[l, pl.ds(j, 128, stride=4), :] = scratch[l, pl.ds(j, 128, stride=8), :]
    row_out = jnp.concatenate([tokens[l] for l in range(3)], axis=1)
    for l in range(3):
        for r in range(8):
            for j in range(4):
                tokens[l, pl.ds(4 * r + j, 16, stride=32), :] = scratch[
                    l, pl.ds(r * 128 + 4 + j, 16, stride=8), :
                ]
    row_grad = jnp.concatenate([tokens[l] for l in range(3)], axis=1)

    aux = whole[:, :256]
    feat = whole[:, :MODEL]
    cot = whole[:, 256 : 256 + MODEL]
    col_out = scan_tokens(aux, row_out, False, True).astype(BF).astype(F32)
    gate, sig, hidden_grad = gate_terms(aux, cot, w_in, w_out)
    hidden = (col_out * gate * sig).astype(BF)
    block[...] = (feat.astype(F32) + mm(hidden, w_out[...])).astype(BF)
    gate_grad = (hidden_grad * col_out * sig * (1.0 + gate * (1.0 - sig))).astype(BF)
    partial[...] = cot.astype(F32) + mm_t(gate_grad, w_in[:, CHAN:])
    shifted = jnp.concatenate([jnp.zeros((TOK, MODEL), F32), cot.astype(F32)], axis=1).astype(BF)
    out_part = t_mm(hidden, shifted)
    gate_part = t_mm(feat, gate_grad)

    row_aux = packed[...]
    value_grad = scan_tokens(row_aux, row_grad, True, False).astype(BF)
    pull = mm_t(value_grad, w_in[:, :CHAN])
    pull = jnp.concatenate([pull, jnp.zeros((TOK, MODEL), F32)], axis=1)
    value_part = t_mm(row_aux[:, :MODEL], value_grad)

    split_lanes(tokens, pull)
    to_columns(scratch, 0, tokens)
    in_part = jnp.concatenate([value_part, gate_part], axis=0)
    for l in range(3):
        lanes = slice(128 * l, 128 * l + 128)
        for k in range(3):
            rows = slice(128 * k, 128 * k + 128)
            scratch[l, pl.ds(4 + k, 128, stride=8), :] = in_part[rows, lanes]
            if l > 0:
                scratch[l, pl.ds(k, 128, stride=8), :] += out_part[rows, lanes]
        scratch[l, pl.ds(7, 128, stride=8), :] = jnp.zeros((128, 128), F32)
    for l in range(3):
        out[:, 128 * l : 128 * l + 128] = scratch[l].astype(BF)


def third_kernel(place, came, partial, block, sums, *refs):
    outs, scratch, grad = refs[:8], refs[8], refs[9]
    x, core = place[0] // 2, place[0] % 2
    total = jnp.sum(came[...].astype(F32), axis=0) * (65536.0**-0.5)
    tiles = [total[4 + k : 5 + k, 128 * l : 128 * l + 128] for k in range(3) for l in range(3)]
    tiles += [total[k : k + 1, 128 * l : 128 * l + 128] for k in range(3) for l in (1, 2)]
    tiles.append(jnp.zeros((1, 128), F32))
    slice_ = jnp.concatenate(tiles, axis=0).astype(BF)
    sums[...] = jnp.broadcast_to(slice_[None], (128, 16, 128))
    for l in range(2):
        scratch[l] = came[:, :, 128 * l : 128 * l + 128].astype(F32).reshape(1024, 128)
    for l in range(2):
        for j in range(4):
            grad[l, pl.ds(j, 128, stride=4), :] = scratch[l, pl.ds(j, 128, stride=8), :]
    pull = jnp.concatenate([grad[0], grad[1][:, :64]], axis=1)
    whole = (partial[...] + pull).astype(BF)
    scratch[0, 0:TOK, :] = whole[:, 0:128].astype(F32)
    scratch[1, 0:TOK, 0:64] = whole[:, 128:192].astype(F32)
    for k in range(8):
        dest = ((x + k // 2) % 4) * 2 + (core + k % 2) % 2
        rows = pl.ds(pl.multiple_of(dest * 64, 64), 64)
        outs[k][:, 0:MODEL] = block[rows, :]
        outs[k][:, MODEL:256] = jnp.zeros((64, 64), BF)
        outs[k][:, 256:384] = scratch[0, rows, :].astype(BF)
        outs[k][:, 384:512] = scratch[1, rows, :].astype(BF)


def last_kernel(place, sums, *refs):
    pieces, (block, grad, in_grad, out_grad, piece, whole, weights) = refs[:8], refs[8:]
    x, core = place[0] // 2, place[0] % 2
    for k in range(8):
        source = ((x + 4 - k // 2) % 4) * 2 + (core + k % 2) % 2
        for l in range(4):
            piece[l] = pieces[k][:, 128 * l : 128 * l + 128].astype(F32)
            for j in range(4):
                whole[l, pl.ds(4 * source + j, 16, stride=32), :] = piece[
                    l, pl.ds(j, 16, stride=4), :
                ]
    block[:, 0:128] = whole[0].astype(BF)
    block[:, 128:192] = whole[1, :, 0:64].astype(BF)
    grad[:, 0:128] = whole[2].astype(BF)
    grad[:, 128:192] = whole[3, :, 0:64].astype(BF)
    weights[...] = sums[...].astype(F32)
    strided = lambda first: weights[pl.ds(first, 128, stride=16), :]
    for l in range(3):
        lanes = slice(128 * l, 128 * l + 128)
        gate_lanes = slice(CHAN + 128 * l, CHAN + 128 * l + 128)
        in_grad[0:128, lanes] = strided(l)
        middle = strided(3 + l)
        in_grad[128:192, lanes] = middle[0:64]
        in_grad[0:64, gate_lanes] = middle[64:128]
        in_grad[64:192, gate_lanes] = strided(6 + l)
    lane = iota((128, 128), 1)
    for k in range(3):
        first = pltpu.roll(strided(9 + 2 * k), 64, 1)
        second = pltpu.roll(strided(10 + 2 * k), 64, 1)
        out_grad[128 * k : 128 * k + 128, 0:128] = jnp.where(lane < 64, first, second)
        out_grad[128 * k : 128 * k + 128, 128:192] = second[:, 0:64]


def call(kernel, outs, ins, scratch=(), flops=10**8):
    specs = [pl.BlockSpec(memory_space=pltpu.VMEM)] * len(ins)
    if ins[0].shape == (1,):
        specs[0] = pl.BlockSpec(memory_space=pltpu.SMEM)
    return pl.pallas_call(
        kernel,
        out_shape=[jax.ShapeDtypeStruct(shape, dtype) for shape, dtype in outs],
        in_specs=specs,
        out_specs=[pl.BlockSpec(memory_space=pltpu.VMEM)] * len(outs),
        scratch_shapes=[pltpu.VMEM(shape, dtype) for shape, dtype in scratch],
        compiler_params=pltpu.CompilerParams(vmem_limit_bytes=VMEM_LIMIT),
        cost_estimate=pl.CostEstimate(flops=flops, bytes_accessed=10**6, transcendentals=10**5),
    )(*ins)


def row_pairs(k):
    return [(i, ((i // 2 + k // 2) % 4) * 2 + (i + k) % 2) for i in range(8)]


def swap_rows(pieces):
    return [pieces[0]] + [lax.ppermute(pieces[k], "row", row_pairs(k)) for k in range(1, 8)]


def on_device(features, selectors, log_decay, in_weight, out_weight, cotangent):
    place = lax.axis_index("row").astype(jnp.int32).reshape(1)
    pad = jnp.zeros((16, 32, 26), BF)
    flat_sel = selectors.reshape(16, 32, 64)
    row_packed = jnp.concatenate(
        [features, flat_sel[:, :, 0:32], log_decay[:, :, 0], pad], axis=-1
    )
    col_packed = jnp.concatenate(
        [features, flat_sel[:, :, 32:64], log_decay[:, :, 1], pad], axis=-1
    )
    row_packed = lax.all_to_all(row_packed, "col", 0, 0).reshape(TOK, 256)
    piece = ((64, 512), BF)
    pieces = call(
        send_rows_kernel,
        [piece] * 8,
        [place, col_packed.reshape(TOK, 256), cotangent.reshape(TOK, MODEL)],
    )
    pieces = swap_rows(pieces)
    (row_out,) = call(row_forward_kernel, [((TOK, CHAN), BF)], [row_packed, in_weight])
    wide = ((3, 1024, 128), F32)
    tall = ((3, TOK, 128), F32)
    sent, whole = call(
        col_adjoint_kernel,
        [((1024, CHAN), BF), ((TOK, 512), BF)],
        [place, row_out, in_weight, out_weight, *pieces],
        [tall, wide],
    )
    came = lax.all_to_all(sent.reshape(128, 8, CHAN), ("row", "col"), 0, 0)
    block, partial, sent = call(
        second_kernel,
        [((TOK, MODEL), BF), ((TOK, MODEL), F32), ((1024, CHAN), BF)],
        [came.reshape(1024, CHAN), whole, row_packed, in_weight, out_weight],
        [tall, wide],
    )
    came = lax.all_to_all(sent.reshape(128, 8, CHAN), ("row", "col"), 0, 0)
    sums, *pieces = call(
        third_kernel,
        [((128, 16, 128), BF)] + [piece] * 8,
        [place, came, partial, block],
        [((2, 1024, 128), F32), ((2, TOK, 128), F32)],
    )
    sums = lax.all_to_all(sums, ("row", "col"), 0, 0).reshape(2048, 128)
    pieces = swap_rows(pieces)
    block, grad, in_grad, out_grad = call(
        last_kernel,
        [((TOK, MODEL), BF), ((TOK, MODEL), BF), ((MODEL, 2 * CHAN), F32), ((CHAN, MODEL), F32)],
        [place, sums, *pieces],
        [((4, 64, 128), F32), ((4, TOK, 128), F32), ((2048, 128), F32)],
    )
    return (block.reshape(16, 32, MODEL), grad.reshape(16, 32, MODEL), in_grad, out_grad)


def solution(mesh):
    in_specs = (
        P("row", "col", None),
        P("row", "col", None, None),
        P("row", "col", None, None),
        P(),
        P(),
        P("row", "col", None),
    )
    out_specs = (P("row", "col", None), P("row", "col", None), P(), P())
    return jax.shard_map(
        on_device, mesh=mesh, in_specs=in_specs, out_specs=out_specs, check_vma=False
    )
```

time: 626 us -> 105 us (0.17)
  waiting for transfers between devices: 403 us -> 7.39 us
  other arithmetic: 78.4 us -> 1 us
  local copies, waits for them, and re-layouts: 51 us -> 4.25 us
  matrix products: 38.9 us -> 0 us
  starting transfers between devices: 0.69 us -> 31.4 us
  Pallas kernels: 0 us -> 13.9 us
  between operations: 14.4 us -> 0.8 us
  blocking collectives: 35.5 us -> 46.2 us
    all_gather x4 -> x0, waiting for transfers between devices: 259 us -> none  [prefix(): pieces = jax.tree.map(lambda part: lax.all_gather(part, axis), value)]
    psum x1 -> x0, waiting for transfers between devices: 144 us -> none  [on_device(): in_total, out_total = lax.psum((in_part, out_part), ('row', 'col'))]
    select_n x44 -> x0, other arithmetic: 70.5 us -> none  [turn(): jnp.where(position < mine, new, old)]
    all_to_all x0 -> x2, blocking collectives: none -> 46.2 us  [on_device(): came = lax.all_to_all(sent.reshape(128, 8, CHAN), ('row', 'col'), 0, 0)]
    dot_general x22 -> x0, matrix products: 38.9 us -> none  [the longest x2 6.6 us: backward_local(): jnp.einsum('bsth,bthp->bshp', weights, per_head, precision=HIGHEST_PRECIS...]
    all_gather x2 -> x0, blocking collectives: 35.5 us -> none  [prefix(): pieces = jax.tree.map(lambda part: lax.all_gather(part, axis), value)]
    rev x4 -> x0, local copies, waits for them, and re-layouts: 21.2 us -> none  [prefix(): pieces = jax.tree.map(lambda part: part[::-1], pieces)]
    ppermute x0 -> x14, starting transfers between devices: none -> 18.7 us  [swap_rows(): lax.ppermute(pieces[k], 'row', row_pairs(k))]
  transfers between devices with their start and end apart: 5 -> 16, of which waited for: 5 -> 7; matrix products, arithmetic and copies ran while one was open for 4% -> 1% of each run, Pallas kernels for 0% -> 2%
where the time goes in v1:
time: 105 us
  blocking collectives  46.2 us (44%)
  starting transfers between devices  31.4 us (30%)
  Pallas kernels  13.9 us (13%)
  waiting for transfers between devices  7.39 us (7%)
  local copies, waits for them, and re-layouts  4.25 us (4%)
    all_to_all x2, blocking collectives, on_device(): came = lax.all_to_all(sent.reshape(128, 8, CHAN), ('row', 'col'), 0, 0)  46.2 us
    ppermute x14, starting transfers between devices, swap_rows(): lax.ppermute(pieces[k], 'row', row_pairs(k))  18.7 us
    pallas_call x6, Pallas kernels, call(): pl.pallas_call(kernel, out_shape=[jax.ShapeDtypeStruct(shape, dtype) for...  13.9 us
    all_to_all x1, starting transfers between devices, on_device(): row_packed = lax.all_to_all(row_packed, 'col', 0, 0).reshape(TOK, 256)  8.6 us
    ppermute x14, waiting for transfers between devices, swap_rows(): lax.ppermute(pieces[k], 'row', row_pairs(k))  7.39 us
    all_to_all x1, starting transfers between devices, on_device(): sums = lax.all_to_all(sums, ('row', 'col'), 0, 0).reshape(2048, 128)  4.15 us
    unnamed x14, local copies, waits for them, and re-layouts  2.78 us
  transfers between devices with their start and end apart: 16, of which 7 were waited for; matrix products, arithmetic and copies ran while one was open for 1% of the time, Pallas kernels for 2%

profile of v1, /device:TPU:1, one launch (start us, length us, event | category | flops | bytes accessed | tf_op | source)
XLA Modules:
  0.0 104.9 jit_solution(16979840923949166491)
XLA Ops:
  0.6 1.0 fusion.1
  1.6 0.2 copy.28
  1.8 0.0 copy-start.2
  1.8 0.1 copy.25
  2.0 0.1 pad.7.clone
  2.1 0.7 copy-done.2
  2.8 0.8 maximum_maximum_fusion
  3.6 8.6 %all-to-all-start = ((bf16[16,32,256]{2,1,0:T(8,128)(2,1)}), bf16[16,32,256]{2,1,0:T(8,128)(2,1)S(1)}, u32[]{:S(2)}, u32[]{:S(2)}) async-start(bf16[16,32,256]{2,1,0:T(8,128)(2,1)} %maximum_maximum_fusion), calls=%async_computation | async-start | bytes 524288 | tf_op jit(solution)/shard_map/all_to_all | solution.py:277
  12.2 0.2 copy.21
  12.5 0.1 copy.27
  12.6 0.0 copy-start.1
  12.6 0.2 maximum_maximum_fusion.1.packed
  12.8 0.8 copy-done.1
  13.5 0.6 shard_map.94
  14.2 0.0 copy-start
  14.2 1.0 collective-permute-start
  15.2 1.2 %collective-permute-start.1 = (bf16[64,512]{1,0:T(8,128)(2,1)S(1)}, bf16[64,512]{1,0:T(8,128)(2,1)S(1)}, u32[]{:S(2)}, u32[]{:S(2)}) collective-permute-start(bf16[64,512]{1,0:T(8,128)(2,1)S(1)} %get-tuple-element.32), channel_id=1, source_target_pairs={{0,32},{16,48},{32,64},{48,80},{64,96},{80,112},{96,0},{112,16},{1... | collective-permute-start | bytes 196616 | tf_op jit(solution)/shard_map/ppermute | solution.py:264
  16.4 1.4 %collective-permute-start.2 = (bf16[64,512]{1,0:T(8,128)(2,1)S(1)}, bf16[64,512]{1,0:T(8,128)(2,1)S(1)}, u32[]{:S(2)}, u32[]{:S(2)}) collective-permute-start(bf16[64,512]{1,0:T(8,128)(2,1)S(1)} %get-tuple-element.33), channel_id=1, source_target_pairs={{0,48},{16,32},{32,80},{48,64},{64,112},{80,96},{96,16},{112,0},{1... | collective-permute-start | bytes 196616 | tf_op jit(solution)/shard_map/ppermute | solution.py:264
  17.9 1.4 %collective-permute-start.3 = (bf16[64,512]{1,0:T(8,128)(2,1)S(1)}, bf16[64,512]{1,0:T(8,128)(2,1)S(1)}, u32[]{:S(2)}, u32[]{:S(2)}) collective-permute-start(bf16[64,512]{1,0:T(8,128)(2,1)S(1)} %get-tuple-element.34), channel_id=1, source_target_pairs={{0,64},{16,80},{32,96},{48,112},{64,0},{80,16},{96,32},{112,48},{1... | collective-permute-start | bytes 196616 | tf_op jit(solution)/shard_map/ppermute | solution.py:264
  19.3 1.9 %collective-permute-start.4 = (bf16[64,512]{1,0:T(8,128)(2,1)S(1)}, bf16[64,512]{1,0:T(8,128)(2,1)S(1)}, u32[]{:S(2)}, u32[]{:S(2)}) collective-permute-start(bf16[64,512]{1,0:T(8,128)(2,1)S(1)} %get-tuple-element.35), channel_id=1, source_target_pairs={{0,80},{16,64},{32,112},{48,96},{64,16},{80,0},{96,48},{112,32},{1... | collective-permute-start | bytes 196616 | tf_op jit(solution)/shard_map/ppermute | solution.py:264
  21.2 1.5 %collective-permute-start.5 = (bf16[64,512]{1,0:T(8,128)(2,1)S(1)}, bf16[64,512]{1,0:T(8,128)(2,1)S(1)}, u32[]{:S(2)}, u32[]{:S(2)}) collective-permute-start(bf16[64,512]{1,0:T(8,128)(2,1)S(1)} %get-tuple-element.36), channel_id=1, source_target_pairs={{0,96},{16,112},{32,0},{48,16},{64,32},{80,48},{96,64},{112,80},{1... | collective-permute-start | bytes 196616 | tf_op jit(solution)/shard_map/ppermute | solution.py:264
  22.7 0.0 collective-permute-done.1.refs_2_
  22.7 0.5 collective-permute-start.6
  23.1 0.1 copy.22.w_out
  23.3 0.0 all-to-all-done
  23.3 1.6 %shard_map.93.row_out = bf16[512,384]{1,0:T(8,128)(2,1)S(1)} custom-call(bf16[512,256]{1,0:T(8,128)(2,1)S(1)} %bitcast.16, bf16[192,768]{1,0:T(8,128)(2,1)S(1)} %copy-done), custom_call_target="tpu_custom_call" | custom-call | flops 100000000 | bytes 1000000 | tf_op jit(solution)/shard_map/pallas_call | solution.py:248
  24.9 0.5 collective-permute-done.4.refs_5_
  25.5 0.4 collective-permute-done.5.refs_6_
  25.9 1.4 %collective-permute-done.6.refs_7_ = bf16[64,512]{1,0:T(8,128)(2,1)S(1)} collective-permute-done((bf16[64,512]{1,0:T(8,128)(2,1)S(1)}, bf16[64,512]{1,0:T(8,128)(2,1)S(1)}, u32[]{:S(2)}, u32[]{:S(2)}) %collective-permute-start.6) | collective-permute-done | bytes 65568 | tf_op jit(solution)/shard_map/ppermute | solution.py:264
  27.3 2.7 %shard_map.95 = (bf16[1024,384]{1,0:T(8,128)(2,1)S(1)}, bf16[512,512]{1,0:T(8,128)(2,1)S(1)}) custom-call(s32[1]{0:T(128)} %bitcast.place, bf16[512,384]{1,0:T(8,128)(2,1)S(1)} %shard_map.93.row_out, bf16[192,768]{1,0:T(8,128)(2,1)S(1)} %copy-done, bf16[384,192]{1,0:T(8,128)(2,1)S(1)} %copy.22.w_out, bf16[64,512]{1,0:T(8,128)(2,1)S(1)} %get-tuple-element.30.refs_0_, ...), custom_call_target="tpu_custom_call" | custom-call | flops 100000000 | bytes 1000000 | tf_op jit(solution)/shard_map/pallas_call | solution.py:248
  30.0 25.8 %all_to_all.20 = bf16[128,8,384]{2,1,0:T(8,128)(2,1)S(1)} all-to-all(bf16[128,8,384]{2,1,0:T(8,128)(2,1)S(1)} %bitcast.19), channel_id=1, replica_groups=mesh['row'=8,'col'=16] {'row','col'}, dimensions={0} | all-to-all | bytes 1572864 | tf_op jit(solution)/shard_map/all_to_all | solution.py:294
  55.8 5.5 %shard_map.96 = (bf16[512,192]{1,0:T(8,128)(2,1)S(1)}, f32[512,192]{1,0:T(8,128)S(1)}, bf16[1024,384]{1,0:T(8,128)(2,1)S(1)}) custom-call(bf16[1024,384]{1,0:T(8,128)(2,1)S(1)} %bitcast.15, bf16[512,512]{1,0:T(8,128)(2,1)S(1)} %get-tuple-element.39.whole, bf16[512,256]{1,0:T(8,128)(2,1)S(1)} %bitcast.17, bf16[192,768]{1,0:T(8,128)(2,1)S(1)} %copy-done, ...), custom_call_target="tpu_custom_call" | custom-call | flops 100000000 | bytes 1000000 | tf_op jit(solution)/shard_map/pallas_call | solution.py:248
  61.4 20.3 %all_to_all.21.came = bf16[128,8,384]{2,1,0:T(8,128)(2,1)S(1)} all-to-all(bf16[128,8,384]{2,1,0:T(8,128)(2,1)S(1)} %bitcast.20), channel_id=1, replica_groups=mesh['row'=8,'col'=16] {'row','col'}, dimensions={0} | all-to-all | bytes 1572864 | tf_op jit(solution)/shard_map/all_to_all | solution.py:301
  81.7 1.2 %shard_map.97 = (bf16[128,16,128]{2,1,0:T(8,128)(2,1)}, bf16[64,512]{1,0:T(8,128)(2,1)S(1)}, bf16[64,512]{1,0:T(8,128)(2,1)S(1)}, bf16[64,512]{1,0:T(8,128)(2,1)...) custom-call(s32[1]{0:T(128)} %bitcast.place, ...), custom_call_target="tpu_custom_call" | custom-call | flops 100000000 | bytes 1000000 | tf_op jit(solution)/shard_map/pallas_call | solution.py:248
  82.9 4.2 %all-to-all-start.3 = ((bf16[128,16,128]{2,1,0:T(8,128)(2,1)}), bf16[128,16,128]{2,1,0:T(8,128)(2,1)S(1)}, u32[]{:S(2)}, u32[]{:S(2)}) async-start(bf16[128,16,128]{2,1,0:T(8,128)(2,1)} %get-tuple-element.43), calls=%async_computation.3 | async-start | bytes 1048576 | tf_op jit(solution)/shard_map/all_to_all | solution.py:308
  87.0 1.3 %collective-permute-start.7 = (bf16[64,512]{1,0:T(8,128)(2,1)S(1)}, bf16[64,512]{1,0:T(8,128)(2,1)S(1)}, u32[]{:S(2)}, u32[]{:S(2)}) collective-permute-start(bf16[64,512]{1,0:T(8,128)(2,1)S(1)} %get-tuple-element.45), channel_id=1, source_target_pairs={{0,16},{16,0},{32,48},{48,32},{64,80},{80,64},{96,112},{112,96},{1... | collective-permute-start | bytes 196616 | tf_op jit(solution)/shard_map/ppermute | solution.py:264
  88.3 0.5 collective-permute-start.8
  88.9 1.5 %collective-permute-start.9 = (bf16[64,512]{1,0:T(8,128)(2,1)S(1)}, bf16[64,512]{1,0:T(8,128)(2,1)S(1)}, u32[]{:S(2)}, u32[]{:S(2)}) collective-permute-start(bf16[64,512]{1,0:T(8,128)(2,1)S(1)} %get-tuple-element.47), channel_id=1, source_target_pairs={{0,48},{16,32},{32,80},{48,64},{64,112},{80,96},{96,16},{112,0},{1... | collective-permute-start | bytes 196616 | tf_op jit(solution)/shard_map/ppermute | solution.py:264
  90.4 2.0 %collective-permute-start.10 = (bf16[64,512]{1,0:T(8,128)(2,1)S(1)}, bf16[64,512]{1,0:T(8,128)(2,1)S(1)}, u32[]{:S(2)}, u32[]{:S(2)}) collective-permute-start(bf16[64,512]{1,0:T(8,128)(2,1)S(1)} %get-tuple-element.48), channel_id=1, source_target_pairs={{0,64},{16,80},{32,96},{48,112},{64,0},{80,16},{96,32},{112,48},{1... | collective-permute-start | bytes 196616 | tf_op jit(solution)/shard_map/ppermute | solution.py:264
  92.4 1.2 %collective-permute-start.11 = (bf16[64,512]{1,0:T(8,128)(2,1)S(1)}, bf16[64,512]{1,0:T(8,128)(2,1)S(1)}, u32[]{:S(2)}, u32[]{:S(2)}) collective-permute-start(bf16[64,512]{1,0:T(8,128)(2,1)S(1)} %get-tuple-element.49), channel_id=1, source_target_pairs={{0,80},{16,64},{32,112},{48,96},{64,16},{80,0},{96,48},{112,32},{1... | collective-permute-start | bytes 196616 | tf_op jit(solution)/shard_map/ppermute | solution.py:264
  93.6 1.5 %collective-permute-start.12 = (bf16[64,512]{1,0:T(8,128)(2,1)S(1)}, bf16[64,512]{1,0:T(8,128)(2,1)S(1)}, u32[]{:S(2)}, u32[]{:S(2)}) collective-permute-start(bf16[64,512]{1,0:T(8,128)(2,1)S(1)} %get-tuple-element.50), channel_id=1, source_target_pairs={{0,96},{16,112},{32,0},{48,16},{64,32},{80,48},{96,64},{112,80},{1... | collective-permute-start | bytes 196616 | tf_op jit(solution)/shard_map/ppermute | solution.py:264
  95.1 1.8 %collective-permute-done.8.refs_2_ = bf16[64,512]{1,0:T(8,128)(2,1)S(1)} collective-permute-done((bf16[64,512]{1,0:T(8,128)(2,1)S(1)}, bf16[64,512]{1,0:T(8,128)(2,1)S(1)}, u32[]{:S(2)}, u32[]{:S(2)}) %collective-permute-start.8) | collective-permute-done | bytes 65568 | tf_op jit(solution)/shard_map/ppermute | solution.py:264
  96.9 1.7 %collective-permute-start.13 = (bf16[64,512]{1,0:T(8,128)(2,1)S(1)}, bf16[64,512]{1,0:T(8,128)(2,1)S(1)}, u32[]{:S(2)}, u32[]{:S(2)}) collective-permute-start(bf16[64,512]{1,0:T(8,128)(2,1)S(1)} %get-tuple-element.51), channel_id=1, source_target_pairs={{0,112},{16,96},{32,16},{48,0},{64,48},{80,32},{96,80},{112,64},{1... | collective-permute-start | bytes 196616 | tf_op jit(solution)/shard_map/ppermute | solution.py:264
  98.6 0.3 collective-permute-done.9.refs_3_
  98.9 1.0 collective-permute-done.10.refs_4_
  99.9 1.9 %collective-permute-done.11.refs_5_ = bf16[64,512]{1,0:T(8,128)(2,1)S(1)} collective-permute-done((bf16[64,512]{1,0:T(8,128)(2,1)S(1)}, bf16[64,512]{1,0:T(8,128)(2,1)S(1)}, u32[]{:S(2)}, u32[]{:S(2)}) %collective-permute-start.11) | collective-permute-done | bytes 65568 | tf_op jit(solution)/shard_map/ppermute | solution.py:264
  101.8 2.3 %shard_map.98 = (bf16[512,192]{1,0:T(8,128)(2,1)}, bf16[512,192]{1,0:T(8,128)(2,1)}, f32[192,768]{1,0:T(8,128)}, f32[384,192]{1,0:T(8,128)S(1)}) custom-call(s32[1]{0:T(128)} %bitcast.place, bf16[2048,128]{1,0:T(8,128)(2,1)S(1)} %bitcast.18, bf16[64,512]{1,0:T(8,128)(2,1)S(1)} %get-tuple-element.44.refs_0_, ...), custom_call_target="tpu_custom_call" | custom-call | flops 100000000 | bytes 1000000 | tf_op jit(solution)/shard_map/pallas_call | solution.py:248
  104.1 0.9 copy.24
  (14 shorter events, 0.0 us)
Async XLA Ops:
  0.6 1.2 %copy-start.3 = (bf16[16,32,4,16]{1,3,2,0:T(8,128)(2,1)S(1)}, bf16[16,32,4,16]{1,3,2,0:T(8,128)(2,1)}, u32[]{:S(2)}) copy-start(bf16[16,32,4,16]{1,3,2,0:T(8,128)(2,1)} %param.7) | copy-start | bytes 196612
  1.8 1.0 copy-start.2
  3.6 19.7 %all-to-all-start = ((bf16[16,32,256]{2,1,0:T(8,128)(2,1)}), bf16[16,32,256]{2,1,0:T(8,128)(2,1)S(1)}, u32[]{:S(2)}, u32[]{:S(2)}) async-start(bf16[16,32,256]{2,1,0:T(8,128)(2,1)} %maximum_maximum_fusion), calls=%async_computation | async-start | bytes 524288 | tf_op jit(solution)/shard_map/all_to_all | solution.py:277
  12.6 1.0 copy-start.1
  13.5 9.6 %copy-start.4 = (bf16[384,192]{0,1:T(8,128)(2,1)S(1)}, bf16[384,192]{0,1:T(8,128)(2,1)}, u32[]{:S(2)}) copy-start(bf16[384,192]{0,1:T(8,128)(2,1)} %param.10) | copy-start | bytes 442372
  14.2 9.1 %copy-start = (bf16[192,768]{1,0:T(8,128)(2,1)S(1)}, bf16[192,768]{1,0:T(8,128)(2,1)}, u32[]{:S(2)}) copy-start(bf16[192,768]{1,0:T(8,128)(2,1)} %w_in.5) | copy-start | bytes 884740
  14.2 7.0 %collective-permute-start = (bf16[64,512]{1,0:T(8,128)(2,1)S(1)}, bf16[64,512]{1,0:T(8,128)(2,1)S(1)}, u32[]{:S(2)}, u32[]{:S(2)}) collective-permute-start(bf16[64,512]{1,0:T(8,128)(2,1)S(1)} %get-tuple-element.31), channel_id=1, source_target_pairs={{0,16},{16,0},{32,48},{48,32},{64,80},{80,64},{96,112},{112,96},{1... | collective-permute-start | bytes 196616 | tf_op jit(solution)/shard_map/ppermute | solution.py:264
  15.2 7.4 %collective-permute-start.1 = (bf16[64,512]{1,0:T(8,128)(2,1)S(1)}, bf16[64,512]{1,0:T(8,128)(2,1)S(1)}, u32[]{:S(2)}, u32[]{:S(2)}) collective-permute-start(bf16[64,512]{1,0:T(8,128)(2,1)S(1)} %get-tuple-element.32), channel_id=1, source_target_pairs={{0,32},{16,48},{32,64},{48,80},{64,96},{80,112},{96,0},{112,16},{1... | collective-permute-start | bytes 196616 | tf_op jit(solution)/shard_map/ppermute | solution.py:264
  16.4 8.5 %collective-permute-start.2 = (bf16[64,512]{1,0:T(8,128)(2,1)S(1)}, bf16[64,512]{1,0:T(8,128)(2,1)S(1)}, u32[]{:S(2)}, u32[]{:S(2)}) collective-permute-start(bf16[64,512]{1,0:T(8,128)(2,1)S(1)} %get-tuple-element.33), channel_id=1, source_target_pairs={{0,48},{16,32},{32,80},{48,64},{64,112},{80,96},{96,16},{112,0},{1... | collective-permute-start | bytes 196616 | tf_op jit(solution)/shard_map/ppermute | solution.py:264
  17.9 7.0 %collective-permute-start.3 = (bf16[64,512]{1,0:T(8,128)(2,1)S(1)}, bf16[64,512]{1,0:T(8,128)(2,1)S(1)}, u32[]{:S(2)}, u32[]{:S(2)}) collective-permute-start(bf16[64,512]{1,0:T(8,128)(2,1)S(1)} %get-tuple-element.34), channel_id=1, source_target_pairs={{0,64},{16,80},{32,96},{48,112},{64,0},{80,16},{96,32},{112,48},{1... | collective-permute-start | bytes 196616 | tf_op jit(solution)/shard_map/ppermute | solution.py:264
  19.3 6.1 %collective-permute-start.4 = (bf16[64,512]{1,0:T(8,128)(2,1)S(1)}, bf16[64,512]{1,0:T(8,128)(2,1)S(1)}, u32[]{:S(2)}, u32[]{:S(2)}) collective-permute-start(bf16[64,512]{1,0:T(8,128)(2,1)S(1)} %get-tuple-element.35), channel_id=1, source_target_pairs={{0,80},{16,64},{32,112},{48,96},{64,16},{80,0},{96,48},{112,32},{1... | collective-permute-start | bytes 196616 | tf_op jit(solution)/shard_map/ppermute | solution.py:264
  21.2 4.7 %collective-permute-start.5 = (bf16[64,512]{1,0:T(8,128)(2,1)S(1)}, bf16[64,512]{1,0:T(8,128)(2,1)S(1)}, u32[]{:S(2)}, u32[]{:S(2)}) collective-permute-start(bf16[64,512]{1,0:T(8,128)(2,1)S(1)} %get-tuple-element.36), channel_id=1, source_target_pairs={{0,96},{16,112},{32,0},{48,16},{64,32},{80,48},{96,64},{112,80},{1... | collective-permute-start | bytes 196616 | tf_op jit(solution)/shard_map/ppermute | solution.py:264
  22.7 4.6 %collective-permute-start.6 = (bf16[64,512]{1,0:T(8,128)(2,1)S(1)}, bf16[64,512]{1,0:T(8,128)(2,1)S(1)}, u32[]{:S(2)}, u32[]{:S(2)}) collective-permute-start(bf16[64,512]{1,0:T(8,128)(2,1)S(1)} %get-tuple-element.37), channel_id=1, source_target_pairs={{0,112},{16,96},{32,16},{48,0},{64,48},{80,32},{96,80},{112,64},{1... | collective-permute-start | bytes 196616 | tf_op jit(solution)/shard_map/ppermute | solution.py:264
  82.9 18.9 %all-to-all-start.3 = ((bf16[128,16,128]{2,1,0:T(8,128)(2,1)}), bf16[128,16,128]{2,1,0:T(8,128)(2,1)S(1)}, u32[]{:S(2)}, u32[]{:S(2)}) async-start(bf16[128,16,128]{2,1,0:T(8,128)(2,1)} %get-tuple-element.43), calls=%async_computation.3 | async-start | bytes 1048576 | tf_op jit(solution)/shard_map/all_to_all | solution.py:308
  87.0 6.6 %collective-permute-start.7 = (bf16[64,512]{1,0:T(8,128)(2,1)S(1)}, bf16[64,512]{1,0:T(8,128)(2,1)S(1)}, u32[]{:S(2)}, u32[]{:S(2)}) collective-permute-start(bf16[64,512]{1,0:T(8,128)(2,1)S(1)} %get-tuple-element.45), channel_id=1, source_target_pairs={{0,16},{16,0},{32,48},{48,32},{64,80},{80,64},{96,112},{112,96},{1... | collective-permute-start | bytes 196616 | tf_op jit(solution)/shard_map/ppermute | solution.py:264
  88.3 8.6 %collective-permute-start.8 = (bf16[64,512]{1,0:T(8,128)(2,1)S(1)}, bf16[64,512]{1,0:T(8,128)(2,1)S(1)}, u32[]{:S(2)}, u32[]{:S(2)}) collective-permute-start(bf16[64,512]{1,0:T(8,128)(2,1)S(1)} %get-tuple-element.46), channel_id=1, source_target_pairs={{0,32},{16,48},{32,64},{48,80},{64,96},{80,112},{96,0},{112,16},{1... | collective-permute-start | bytes 196616 | tf_op jit(solution)/shard_map/ppermute | solution.py:264
  88.9 10.0 %collective-permute-start.9 = (bf16[64,512]{1,0:T(8,128)(2,1)S(1)}, bf16[64,512]{1,0:T(8,128)(2,1)S(1)}, u32[]{:S(2)}, u32[]{:S(2)}) collective-permute-start(bf16[64,512]{1,0:T(8,128)(2,1)S(1)} %get-tuple-element.47), channel_id=1, source_target_pairs={{0,48},{16,32},{32,80},{48,64},{64,112},{80,96},{96,16},{112,0},{1... | collective-permute-start | bytes 196616 | tf_op jit(solution)/shard_map/ppermute | solution.py:264
  90.4 9.5 %collective-permute-start.10 = (bf16[64,512]{1,0:T(8,128)(2,1)S(1)}, bf16[64,512]{1,0:T(8,128)(2,1)S(1)}, u32[]{:S(2)}, u32[]{:S(2)}) collective-permute-start(bf16[64,512]{1,0:T(8,128)(2,1)S(1)} %get-tuple-element.48), channel_id=1, source_target_pairs={{0,64},{16,80},{32,96},{48,112},{64,0},{80,16},{96,32},{112,48},{1... | collective-permute-start | bytes 196616 | tf_op jit(solution)/shard_map/ppermute | solution.py:264
  92.4 9.3 %collective-permute-start.11 = (bf16[64,512]{1,0:T(8,128)(2,1)S(1)}, bf16[64,512]{1,0:T(8,128)(2,1)S(1)}, u32[]{:S(2)}, u32[]{:S(2)}) collective-permute-start(bf16[64,512]{1,0:T(8,128)(2,1)S(1)} %get-tuple-element.49), channel_id=1, source_target_pairs={{0,80},{16,64},{32,112},{48,96},{64,16},{80,0},{96,48},{112,32},{1... | collective-permute-start | bytes 196616 | tf_op jit(solution)/shard_map/ppermute | solution.py:264
  93.6 8.1 %collective-permute-start.12 = (bf16[64,512]{1,0:T(8,128)(2,1)S(1)}, bf16[64,512]{1,0:T(8,128)(2,1)S(1)}, u32[]{:S(2)}, u32[]{:S(2)}) collective-permute-start(bf16[64,512]{1,0:T(8,128)(2,1)S(1)} %get-tuple-element.50), channel_id=1, source_target_pairs={{0,96},{16,112},{32,0},{48,16},{64,32},{80,48},{96,64},{112,80},{1... | collective-permute-start | bytes 196616 | tf_op jit(solution)/shard_map/ppermute | solution.py:264
  96.9 4.8 %collective-permute-start.13 = (bf16[64,512]{1,0:T(8,128)(2,1)S(1)}, bf16[64,512]{1,0:T(8,128)(2,1)S(1)}, u32[]{:S(2)}, u32[]{:S(2)}) collective-permute-start(bf16[64,512]{1,0:T(8,128)(2,1)S(1)} %get-tuple-element.51), channel_id=1, source_target_pairs={{0,112},{16,96},{32,16},{48,0},{64,48},{80,32},{96,80},{112,64},{1... | collective-permute-start | bytes 196616 | tf_op jit(solution)/shard_map/ppermute | solution.py:264

commit v2 on v1

v2 whole, which is shorter than its diff:
```python
import jax
import jax.numpy as jnp
from jax import lax
from jax.experimental import pallas as pl
from jax.experimental.pallas import tpu as pltpu
from jax.sharding import PartitionSpec as P

BF = jnp.bfloat16
F32 = jnp.float32
MODEL = 192
CHAN = 384
TOK = 512
GROUP = 256
VMEM_LIMIT = 48 * 1024 * 1024


def iota(shape, dim):
    return lax.broadcasted_iota(jnp.int32, shape, dim)


def mm(a, b):
    return jnp.dot(a, b, preferred_element_type=F32)


def mm_t(a, b):
    return lax.dot_general(a, b, (((1,), (1,)), ((), ())), preferred_element_type=F32)


def t_mm(a, b):
    return lax.dot_general(a, b, (((0,), (0,)), ((), ())), preferred_element_type=F32)


def spread(aux, first):
    pick = (iota((256, 128), 0) - first == iota((256, 128), 1) % 16).astype(F32).astype(BF)
    return mm(aux, pick)


HALVES = (slice(0, GROUP), slice(GROUP, TOK))


def prepare_scan(aux, by_row, forward):
    token = iota((TOK, 128), 0)
    chunk = token // 64 if by_row else (token // GROUP) * 4 + token % 4
    member = (iota((TOK, 128), 1) // 16 == chunk).astype(F32)
    b_part = (spread(aux, 192) * member).astype(BF)
    c_part = (spread(aux, 208) * member).astype(BF)
    heads = (iota((256, CHAN), 0) - 224 == iota((256, CHAN), 1) // 64).astype(F32).astype(BF)
    log_step = mm(aux, heads).astype(BF)
    here, there = iota((GROUP, GROUP), 0), iota((GROUP, GROUP), 1)
    same = (here // 64 == there // 64) if by_row else (here % 4 == there % 4)
    if forward:
        order, counted, src, out = there <= here, there <= here, b_part, c_part
    else:
        order, counted, src, out = there >= here, there > here, c_part, b_part
    add_up = (same & counted).astype(F32).astype(BF)
    run = jnp.concatenate([mm(add_up, log_step[h]) for h in HALVES], axis=0)
    decay = jnp.exp(t_mm(member.astype(BF), log_step))
    scores = [jnp.where(order, mm_t(out[h], src[h]), 0.0).astype(BF) for h in HALVES]
    return jnp.concatenate(scores, axis=0), src, out, jnp.exp(-run), jnp.exp(run), decay


def apply_scan(prepared, values, by_row, forward):
    scores, src, out, up, down, decay = prepared
    raised = (up[...] * values).astype(BF)
    states = t_mm(src[...], raised)
    zero = jnp.zeros((16, CHAN), F32)
    carried = [zero] * 8
    part = lambda array, k: array[16 * k : 16 * k + 16]
    if by_row:
        steps = [(k, k + 1) for k in range(7)] if forward else [(k, k - 1) for k in range(7, 0, -1)]
    else:
        steps = [(j, j + 4) for j in range(4)] if forward else [(j + 4, j) for j in range(4)]
    for old, new in steps:
        carried[new] = part(decay, old) * (carried[old] + part(states, old))
    coming = jnp.concatenate(carried, axis=0).astype(BF)
    inner = jnp.concatenate([mm(scores[h, :], raised[h]) for h in HALVES], axis=0)
    return down[...] * (inner + mm(out[...], coming))


def scan_tokens(aux, values, by_row, forward):
    return apply_scan(prepare_scan(aux, by_row, forward), values, by_row, forward)


def to_columns(scratch, slot, token_rows):
    for l in range(CHAN // 128):
        for r in range(8):
            for j in range(4):
                scratch[l, pl.ds(r * 128 + slot + j, 16, stride=8), :] = token_rows[
                    l, pl.ds(4 * r + j, 16, stride=32), :
                ]


def split_lanes(ref, value):
    for l in range(value.shape[1] // 128):
        ref[l] = value[:, 128 * l : 128 * l + 128]


def peers(place, k):
    x, core = place[0] // 2, place[0] % 2
    return ((x + k // 2) % 4) * 2 + (core + k % 2) % 2


def with_aux(feat, sel, log, slot):
    index, lane = iota((48, 128), 0), iota((48, 128), 1)
    pick = ((lane == index + 64) & (index < 38)).astype(F32).astype(BF)
    blank = jnp.zeros((10, 32), F32)
    aux = []
    for i in range(16):
        chosen = sel[i, 32 * slot : 32 * slot + 32, :].astype(F32)
        decay = log[i].astype(F32)[:, slot, :]
        aux.append(t_mm(jnp.concatenate([chosen, decay, blank], axis=0).astype(BF), pick))
    upper = feat[:, 128:MODEL].astype(F32)
    upper = jnp.concatenate([upper, jnp.zeros((TOK, 64), F32)], axis=1)
    return (upper + jnp.concatenate(aux, axis=0)).astype(BF)


def pack_rows_kernel(feat, sel, log, packed):
    packed[:, 0:128] = feat[:, 0:128]
    packed[:, 128:256] = with_aux(feat, sel, log, 0)


def pack_columns_kernel(place, feat, cot, sel, log, *outs):
    slot = iota((TOK, 1), 0)
    row, j = (slot % 64) // 4, slot % 4
    dest = peers(place, slot // 64)
    choose = ((row * 32 + 4 * dest + j) == iota((TOK, TOK), 1)).astype(F32).astype(BF)
    left = mm(choose, feat[:, 0:128]).astype(BF)
    middle = mm(choose, with_aux(feat, sel, log, 1)).astype(BF)
    right = mm(choose, cot[...]).astype(BF)
    for k in range(8):
        rows = slice(64 * k, 64 * k + 64)
        outs[k][:, 0:128] = left[rows]
        outs[k][:, 128:256] = middle[rows]
        outs[k][:, 256 : 256 + MODEL] = right[rows]
        outs[k][:, 256 + MODEL :] = jnp.zeros((64, 64), BF)


def row_forward_kernel(packed, w_in, out):
    aux = packed[...]
    values = mm(aux[:, :MODEL], w_in[:, :CHAN]).astype(BF).astype(F32)
    out[...] = scan_tokens(aux, values, True, True).astype(BF)


def gate_terms(aux, cot, w_in, w_out):
    gate = mm(aux[:, :MODEL], w_in[:, CHAN:]).astype(BF).astype(F32)
    sig = 1.0 / (1.0 + jnp.exp(-gate))
    return gate, sig, mm(cot, w_out[...])


def sender(place, k):
    x, core = place[0] // 2, place[0] % 2
    return ((x + 4 - k // 2) % 4) * 2 + (core + k % 2) % 2


def col_adjoint_kernel(place, row_out, w_in, w_out, *refs):
    pieces, (out, whole, tokens, scratch) = refs[:8], refs[8:]
    for k in range(8):
        whole[pl.ds(pl.multiple_of(sender(place, k) * 64, 64), 64), :] = pieces[k][...]
    aux = whole[:, :256]
    cot = whole[:, 256 : 256 + MODEL]
    gate, sig, hidden_grad = gate_terms(aux, cot, w_in, w_out)
    col_grad = (hidden_grad * gate * sig).astype(BF).astype(F32)
    row_grad = scan_tokens(aux, col_grad, False, False)
    split_lanes(tokens, row_out[...].astype(F32))
    to_columns(scratch, 0, tokens)
    split_lanes(tokens, row_grad)
    for l in range(3):
        for j in range(4):
            scratch[l, pl.ds(4 + j, 128, stride=8), :] = tokens[l, pl.ds(j, 128, stride=4), :]
    for l in range(3):
        out[:, 128 * l : 128 * l + 128] = scratch[l].astype(BF)


def second_kernel(came, whole, packed, w_in, w_out, block, partial, out, tokens, scratch):
    split_lanes(scratch, came[...].astype(F32))
    for l in range(3):
        for j in range(4):
            tokens[l, pl.ds(j, 128, stride=4), :] = scratch[l, pl.ds(j, 128, stride=8), :]
    row_out = jnp.concatenate([tokens[l] for l in range(3)], axis=1)
    feat = whole[:, :MODEL]
    cot = whole[:, 256 : 256 + MODEL]
    col_out = scan_tokens(whole[:, :256], row_out, False, True).astype(BF).astype(F32)
    gate, sig, hidden_grad = gate_terms(feat, cot, w_in, w_out)
    hidden = (col_out * gate * sig).astype(BF)
    block[...] = feat.astype(F32) + mm_t(hidden, w_out[...])
    gate_grad = (hidden_grad * col_out * sig * (1.0 + gate * (1.0 - sig))).astype(BF)
    partial[...] = cot.astype(F32) + mm_t(gate_grad, w_in[:, CHAN:])
    shifted = jnp.concatenate([jnp.zeros((TOK, MODEL), F32), cot.astype(F32)], axis=1).astype(BF)
    out_part = t_mm(hidden, shifted)
    gate_part = t_mm(feat, gate_grad)

    for l in range(3):
        for r in range(8):
            for j in range(4):
                tokens[l, pl.ds(4 * r + j, 16, stride=32), :] = scratch[
                    l, pl.ds(r * 128 + 4 + j, 16, stride=8), :
                ]
    row_grad = jnp.concatenate([tokens[l] for l in range(3)], axis=1)
    value_grad = scan_tokens(packed[...], row_grad, True, False).astype(BF)
    pull = mm_t(value_grad, w_in[:, :CHAN])
    pull = jnp.concatenate([pull, jnp.zeros((TOK, MODEL), F32)], axis=1)
    value_part = t_mm(packed[:, :MODEL], value_grad)

    split_lanes(tokens, pull)
    to_columns(scratch, 0, tokens)
    in_part = jnp.concatenate([value_part, gate_part], axis=0)
    for l in range(3):
        lanes = slice(128 * l, 128 * l + 128)
        for k in range(3):
            rows = slice(128 * k, 128 * k + 128)
            scratch[l, pl.ds(4 + k, 128, stride=8), :] = in_part[rows, lanes]
            if l > 0:
                scratch[l, pl.ds(k, 128, stride=8), :] += out_part[rows, lanes]
        scratch[l, pl.ds(7, 128, stride=8), :] = jnp.zeros((128, 128), F32)
    for l in range(3):
        out[:, 128 * l : 128 * l + 128] = scratch[l].astype(BF)


def sum_kernel(came, sums):
    total = jnp.sum(came[...].astype(F32), axis=0) * (65536.0**-0.5)
    tiles = [total[4 + k : 5 + k, 128 * l : 128 * l + 128] for k in range(3) for l in range(3)]
    tiles += [total[k : k + 1, 128 * l : 128 * l + 128] for k in range(3) for l in (1, 2)]
    tiles.append(jnp.zeros((1, 128), F32))
    slice_ = jnp.concatenate(tiles, axis=0).astype(BF)
    sums[...] = jnp.broadcast_to(slice_[None], (128, 16, 128))


def return_kernel(place, came, partial, block, *refs):
    outs, (scratch, grad, whole) = refs[:8], refs[8:]
    for l in range(2):
        scratch[l] = came[:, :, 128 * l : 128 * l + 128].astype(F32).reshape(1024, 128)
    for l in range(2):
        for j in range(4):
            grad[l, pl.ds(j, 128, stride=4), :] = scratch[l, pl.ds(j, 128, stride=8), :]
    pull = jnp.concatenate([grad[0], grad[1][:, :64]], axis=1)
    whole[...] = jnp.concatenate([block[...], partial[...] + pull], axis=1).astype(BF)
    for k in range(8):
        rows = pl.ds(pl.multiple_of(peers(place, k) * 64, 64), 64)
        outs[k][...] = whole[rows, :]


def tokens_kernel(place, *refs):
    pieces, (block, grad, part, whole) = refs[:8], refs[8:]
    for k in range(8):
        first = 4 * sender(place, k)
        split_lanes(part, pieces[k][...].astype(F32))
        for l in range(3):
            for j in range(4):
                whole[l, pl.ds(first + j, 16, stride=32), :] = part[l, pl.ds(j, 16, stride=4), :]
    middle = whole[1]
    block[...] = jnp.concatenate([whole[0], middle[:, :64]], axis=1).astype(BF)
    grad[...] = jnp.concatenate([middle[:, 64:], whole[2]], axis=1).astype(BF)


def weights_kernel(sums, in_grad, out_grad, weights):
    weights[...] = sums[...].astype(F32)
    strided = lambda first: weights[pl.ds(first, 128, stride=16), :]
    for l in range(3):
        lanes = slice(128 * l, 128 * l + 128)
        gate_lanes = slice(CHAN + 128 * l, CHAN + 128 * l + 128)
        in_grad[0:128, lanes] = strided(l)
        middle = strided(3 + l)
        in_grad[128:192, lanes] = middle[0:64]
        in_grad[0:64, gate_lanes] = middle[64:128]
        in_grad[64:192, gate_lanes] = strided(6 + l)
    for k in range(3):
        lanes = slice(128 * k, 128 * k + 128)
        out_grad[0:64, lanes] = strided(9 + 2 * k).T[64:128]
        out_grad[64:192, lanes] = strided(10 + 2 * k).T


def call(kernel, outs, ins, scratch=(), flops=10**8, vmem=VMEM_LIMIT):
    specs = [pl.BlockSpec()] * len(ins)
    if ins[0].shape == (1,):
        specs[0] = pl.BlockSpec(memory_space=pltpu.SMEM)
    return pl.pallas_call(
        kernel,
        out_shape=[jax.ShapeDtypeStruct(shape, dtype) for shape, dtype in outs],
        in_specs=specs,
        out_specs=[pl.BlockSpec()] * len(outs),
        scratch_shapes=[pltpu.VMEM(shape, dtype) for shape, dtype in scratch],
        compiler_params=pltpu.CompilerParams(vmem_limit_bytes=vmem),
        cost_estimate=pl.CostEstimate(flops=flops, bytes_accessed=10**6, transcendentals=10**5),
    )(*ins)


def swap_rows(pieces):
    pairs = lambda k: [(i, ((i // 2 + k // 2) % 4) * 2 + (i + k) % 2) for i in range(8)]
    return [pieces[0]] + [lax.ppermute(pieces[k], "row", pairs(k)) for k in range(1, 8)]


def on_device(features, selectors, log_decay, in_weight, out_weight, cotangent):
    place = lax.axis_index("row").astype(jnp.int32).reshape(1)
    out_turned = out_weight.T
    feat = features.reshape(TOK, MODEL)
    sel = selectors.transpose(0, 2, 3, 1).reshape(16, 64, 32)
    log = log_decay.transpose(0, 3, 2, 1)
    wide = ((3, 1024, 128), F32)
    tall = ((3, TOK, 128), F32)
    (row_packed,) = call(
        pack_rows_kernel, [((TOK, 256), BF)], [feat, sel, log], vmem=60 * 1024 * 1024
    )
    row_packed = lax.all_to_all(row_packed.reshape(16, 32, 256), "col", 0, 0).reshape(TOK, 256)
    pieces = call(
        pack_columns_kernel,
        [((64, 512), BF)] * 8,
        [place, feat, cotangent.reshape(TOK, MODEL), sel, log],
    )
    pieces = swap_rows(pieces)
    (row_out,) = call(row_forward_kernel, [((TOK, CHAN), BF)], [row_packed, in_weight])
    sent, whole = call(
        col_adjoint_kernel,
        [((1024, CHAN), BF), ((TOK, 512), BF)],
        [place, row_out, in_weight, out_turned, *pieces],
        [tall, wide],
    )
    came = lax.all_to_all(sent.reshape(128, 8, CHAN), ("row", "col"), 0, 0)
    block, partial, sent = call(
        second_kernel,
        [((TOK, MODEL), F32), ((TOK, MODEL), F32), ((1024, CHAN), BF)],
        [came.reshape(1024, CHAN), whole, row_packed, in_weight, out_turned],
        [tall, wide],
    )
    came = lax.all_to_all(sent.reshape(128, 8, CHAN), ("row", "col"), 0, 0)
    (sums,) = call(sum_kernel, [((128, 16, 128), BF)], [came])
    sums = lax.all_to_all(sums, ("row", "col"), 0, 0).reshape(2048, 128)
    pieces = call(
        return_kernel,
        [((64, CHAN), BF)] * 8,
        [place, came, partial, block],
        [((2, 1024, 128), F32), ((2, TOK, 128), F32), ((TOK, CHAN), BF)],
    )
    block, grad = call(
        tokens_kernel,
        [((TOK, MODEL), BF)] * 2,
        [place, *swap_rows(pieces)],
        [((3, 64, 128), F32), tall],
    )
    in_grad, out_grad = call(
        weights_kernel,
        [((MODEL, 2 * CHAN), F32), ((MODEL, CHAN), F32)],
        [sums],
        [((2048, 128), F32)],
    )
    return (block.reshape(16, 32, MODEL), grad.reshape(16, 32, MODEL), in_grad, out_grad.T)


def solution(mesh):
    in_specs = (
        P("row", "col", None),
        P("row", "col", None, None),
        P("row", "col", None, None),
        P(),
        P(),
        P("row", "col", None),
    )
    out_specs = (P("row", "col", None), P("row", "col", None), P(), P())
    return jax.shard_map(
        on_device, mesh=mesh, in_specs=in_specs, out_specs=out_specs, check_vma=False
    )
```

time: 105 us -> 101 us (0.962)
  local copies, waits for them, and re-layouts: 4.25 us -> 0.03 us
  Pallas kernels: 13.9 us -> 15.5 us
    unnamed x14 -> x12, local copies, waits for them, and re-layouts: 2.78 us -> 0.03 us
    pallas_call x6 -> x9, Pallas kernels: 13.9 us -> 15.5 us  [call(): pl.pallas_call(kernel, out_shape=[jax.ShapeDtypeStruct(shape, dtype) for...]
    slice x3 -> x0, local copies, waits for them, and re-layouts: 1.18 us -> none  [the longest x2 1.16 us: on_device(): log_decay[:, :, 1]]
  transfers between devices with their start and end apart: 16 -> 16, of which waited for: 7 -> 7; matrix products, arithmetic and copies ran while one was open for 1% -> 0% of each run, Pallas kernels for 2% -> 4%
where the time goes in v2:
time: 101 us; the launch traced here: 100 us
  blocking collectives  46.2 us (46%)
  starting transfers between devices  31.5 us (31%)
  Pallas kernels  15.5 us (15%)
  waiting for transfers between devices  6.46 us (6%)
    all_to_all x2, blocking collectives, on_device(): came = lax.all_to_all(sent.reshape(128, 8, CHAN), ('row', 'col'), 0, 0)  46.2 us
    ppermute x14, starting transfers between devices, swap_rows(): lax.ppermute(pieces[k], 'row', pairs(k))  18.7 us
    pallas_call x9, Pallas kernels, call(): pl.pallas_call(kernel, out_shape=[jax.ShapeDtypeStruct(shape, dtype) for...  15.5 us
    all_to_all x1, starting transfers between devices, on_device(): lax.all_to_all(row_packed.reshape(16, 32, 256), 'col', 0, 0)  8.73 us
    ppermute x14, waiting for transfers between devices, swap_rows(): lax.ppermute(pieces[k], 'row', pairs(k))  6.45 us
    all_to_all x1, starting transfers between devices, on_device(): sums = lax.all_to_all(sums, ('row', 'col'), 0, 0).reshape(2048, 128)  4.15 us
  transfers between devices with their start and end apart: 16, of which 7 were waited for; matrix products, arithmetic and copies ran while one was open for 0% of the time, Pallas kernels for 4%

profile of v2, /device:TPU:1, one launch (start us, length us, event | category | flops | bytes accessed | tf_op | source)
XLA Modules:
  0.0 100.5 jit_solution(5987969850143672434)
XLA Ops:
  0.6 0.0 copy-start.4
  0.6 0.0 copy-start.5
  0.7 2.0 %shard_map.93 = bf16[512,256]{1,0:T(8,128)(2,1)} custom-call(bf16[512,192]{1,0:T(8,128)(2,1)} %bitcast.21, bf16[16,64,32]{2,1,0:T(8,128)(2,1)} %bitcast.23, bf16[16,6,2,32]{3,2,1,0:T(2,128)(2,1)} %bitcast.30), custom_call_target="tpu_custom_call" | custom-call | flops 100000000 | bytes 1000000 | tf_op jit(solution)/shard_map/pallas_call | solution.py:276
  2.7 8.7 %all-to-all-start = ((bf16[16,32,256]{2,1,0:T(8,128)(2,1)}), bf16[16,32,256]{2,1,0:T(8,128)(2,1)S(1)}, u32[]{:S(2)}, u32[]{:S(2)}) async-start(bf16[16,32,256]{2,1,0:T(8,128)(2,1)} %bitcast.32), calls=%async_computation | async-start | bytes 524288 | tf_op jit(solution)/shard_map/all_to_all | solution.py:303
  11.4 0.0 copy-done.4
  11.4 0.0 copy-done.5
  11.5 0.0 copy-start
  11.5 1.0 shard_map.95
  12.4 1.0 %collective-permute-start = (bf16[64,512]{1,0:T(8,128)(2,1)S(1)}, bf16[64,512]{1,0:T(8,128)(2,1)S(1)}, u32[]{:S(2)}, u32[]{:S(2)}) collective-permute-start(bf16[64,512]{1,0:T(8,128)(2,1)S(1)} %get-tuple-element.30), channel_id=1, source_target_pairs={{0,16},{16,0},{32,48},{48,32},{64,80},{80,64},{96,112},{112,96},{1... | collective-permute-start | bytes 196616 | tf_op jit(solution)/shard_map/ppermute | solution.py:289
  13.5 1.2 %collective-permute-start.1 = (bf16[64,512]{1,0:T(8,128)(2,1)S(1)}, bf16[64,512]{1,0:T(8,128)(2,1)S(1)}, u32[]{:S(2)}, u32[]{:S(2)}) collective-permute-start(bf16[64,512]{1,0:T(8,128)(2,1)S(1)} %get-tuple-element.31), channel_id=1, source_target_pairs={{0,32},{16,48},{32,64},{48,80},{64,96},{80,112},{96,0},{112,16},{1... | collective-permute-start | bytes 196616 | tf_op jit(solution)/shard_map/ppermute | solution.py:289
  14.7 1.4 %collective-permute-start.2 = (bf16[64,512]{1,0:T(8,128)(2,1)S(1)}, bf16[64,512]{1,0:T(8,128)(2,1)S(1)}, u32[]{:S(2)}, u32[]{:S(2)}) collective-permute-start(bf16[64,512]{1,0:T(8,128)(2,1)S(1)} %get-tuple-element.32), channel_id=1, source_target_pairs={{0,48},{16,32},{32,80},{48,64},{64,112},{80,96},{96,16},{112,0},{1... | collective-permute-start | bytes 196616 | tf_op jit(solution)/shard_map/ppermute | solution.py:289
  16.1 1.4 %collective-permute-start.3 = (bf16[64,512]{1,0:T(8,128)(2,1)S(1)}, bf16[64,512]{1,0:T(8,128)(2,1)S(1)}, u32[]{:S(2)}, u32[]{:S(2)}) collective-permute-start(bf16[64,512]{1,0:T(8,128)(2,1)S(1)} %get-tuple-element.33), channel_id=1, source_target_pairs={{0,64},{16,80},{32,96},{48,112},{64,0},{80,16},{96,32},{112,48},{1... | collective-permute-start | bytes 196616 | tf_op jit(solution)/shard_map/ppermute | solution.py:289
  17.6 1.9 %collective-permute-start.4 = (bf16[64,512]{1,0:T(8,128)(2,1)S(1)}, bf16[64,512]{1,0:T(8,128)(2,1)S(1)}, u32[]{:S(2)}, u32[]{:S(2)}) collective-permute-start(bf16[64,512]{1,0:T(8,128)(2,1)S(1)} %get-tuple-element.34), channel_id=1, source_target_pairs={{0,80},{16,64},{32,112},{48,96},{64,16},{80,0},{96,48},{112,32},{1... | collective-permute-start | bytes 196616 | tf_op jit(solution)/shard_map/ppermute | solution.py:289
  19.4 0.0 collective-permute-done.refs_1_
  19.4 1.5 %collective-permute-start.5 = (bf16[64,512]{1,0:T(8,128)(2,1)S(1)}, bf16[64,512]{1,0:T(8,128)(2,1)S(1)}, u32[]{:S(2)}, u32[]{:S(2)}) collective-permute-start(bf16[64,512]{1,0:T(8,128)(2,1)S(1)} %get-tuple-element.35), channel_id=1, source_target_pairs={{0,96},{16,112},{32,0},{48,16},{64,32},{80,48},{96,64},{112,80},{1... | collective-permute-start | bytes 196616 | tf_op jit(solution)/shard_map/ppermute | solution.py:289
  20.9 0.0 collective-permute-done.1.refs_2_
  20.9 0.5 collective-permute-start.6
  21.4 0.0 all-to-all-done
  21.4 1.2 %shard_map.94.row_out = bf16[512,384]{1,0:T(8,128)(2,1)S(1)} custom-call(bf16[512,256]{1,0:T(8,128)(2,1)S(1)} %bitcast.18, bf16[192,768]{1,0:T(8,128)(2,1)S(1)} %copy-done), custom_call_target="tpu_custom_call" | custom-call | flops 100000000 | bytes 1000000 | tf_op jit(solution)/shard_map/pallas_call | solution.py:276
  22.6 0.0 collective-permute-done.2.refs_3_
  22.6 0.0 collective-permute-done.3.refs_4_
  22.6 1.1 %collective-permute-done.4.refs_5_ = bf16[64,512]{1,0:T(8,128)(2,1)S(1)} collective-permute-done((bf16[64,512]{1,0:T(8,128)(2,1)S(1)}, bf16[64,512]{1,0:T(8,128)(2,1)S(1)}, u32[]{:S(2)}, u32[]{:S(2)}) %collective-permute-start.4) | collective-permute-done | bytes 65568 | tf_op jit(solution)/shard_map/ppermute | solution.py:289
  23.7 0.4 collective-permute-done.5.refs_6_
  24.1 1.4 %collective-permute-done.6.refs_7_ = bf16[64,512]{1,0:T(8,128)(2,1)S(1)} collective-permute-done((bf16[64,512]{1,0:T(8,128)(2,1)S(1)}, bf16[64,512]{1,0:T(8,128)(2,1)S(1)}, u32[]{:S(2)}, u32[]{:S(2)}) %collective-permute-start.6) | collective-permute-done | bytes 65568 | tf_op jit(solution)/shard_map/ppermute | solution.py:289
  25.6 2.3 %shard_map.96 = (bf16[1024,384]{1,0:T(8,128)(2,1)S(1)}, bf16[512,512]{1,0:T(8,128)(2,1)S(1)}) custom-call(s32[1]{0:T(128)} %bitcast.place, bf16[512,384]{1,0:T(8,128)(2,1)S(1)} %shard_map.94.row_out, bf16[192,768]{1,0:T(8,128)(2,1)S(1)} %copy-done, bf16[192,384]{1,0:T(8,128)(2,1)S(1)} %bitcast.27, bf16[64,512]{1,0:T(8,128)(2,1)S(1)} %get-tuple-element.29.refs_0_, ...), custom_call_target="tpu_custom_call" | custom-call | flops 100000000 | bytes 1000000 | tf_op jit(solution)/shard_map/pallas_call | solution.py:276
  27.9 25.8 %all_to_all.20 = bf16[128,8,384]{2,1,0:T(8,128)(2,1)S(1)} all-to-all(bf16[128,8,384]{2,1,0:T(8,128)(2,1)S(1)} %bitcast.25), channel_id=1, replica_groups=mesh['row'=8,'col'=16] {'row','col'}, dimensions={0} | all-to-all | bytes 1572864 | tf_op jit(solution)/shard_map/all_to_all | solution.py:317
  53.7 5.1 %shard_map.97 = (f32[512,192]{1,0:T(8,128)S(1)}, f32[512,192]{1,0:T(8,128)S(1)}, bf16[1024,384]{1,0:T(8,128)(2,1)S(1)}) custom-call(bf16[1024,384]{1,0:T(8,128)(2,1)S(1)} %bitcast.17, bf16[512,512]{1,0:T(8,128)(2,1)S(1)} %get-tuple-element.38.whole, bf16[512,256]{1,0:T(8,128)(2,1)S(1)} %bitcast.19, bf16[192,768]{1,0:T(8,128)(2,1)S(1)} %copy-done, ...), custom_call_target="tpu_custom_call" | custom-call | flops 100000000 | bytes 1000000 | tf_op jit(solution)/shard_map/pallas_call | solution.py:276
  58.8 20.3 %all_to_all.21.came = bf16[128,8,384]{2,1,0:T(8,128)(2,1)S(1)} all-to-all(bf16[128,8,384]{2,1,0:T(8,128)(2,1)S(1)} %bitcast.26), channel_id=1, replica_groups=mesh['row'=8,'col'=16] {'row','col'}, dimensions={0} | all-to-all | bytes 1572864 | tf_op jit(solution)/shard_map/all_to_all | solution.py:324
  79.1 1.0 shard_map.100
  80.1 4.2 %all-to-all-start.3 = ((bf16[128,16,128]{2,1,0:T(8,128)(2,1)}), bf16[128,16,128]{2,1,0:T(8,128)(2,1)S(1)}, u32[]{:S(2)}, u32[]{:S(2)}) async-start(bf16[128,16,128]{2,1,0:T(8,128)(2,1)} %shard_map.100), calls=%async_computation.3 | async-start | bytes 1048576 | tf_op jit(solution)/shard_map/all_to_all | solution.py:326
  84.3 0.3 shard_map.98
  84.6 1.3 %collective-permute-start.7 = (bf16[64,384]{1,0:T(8,128)(2,1)S(1)}, bf16[64,384]{1,0:T(8,128)(2,1)S(1)}, u32[]{:S(2)}, u32[]{:S(2)}) collective-permute-start(bf16[64,384]{1,0:T(8,128)(2,1)S(1)} %get-tuple-element.43), channel_id=1, source_target_pairs={{0,16},{16,0},{32,48},{48,32},{64,80},{80,64},{96,112},{112,96},{1... | collective-permute-start | bytes 147464 | tf_op jit(solution)/shard_map/ppermute | solution.py:289
  85.9 0.5 collective-permute-start.8
  86.4 1.5 %collective-permute-start.9 = (bf16[64,384]{1,0:T(8,128)(2,1)S(1)}, bf16[64,384]{1,0:T(8,128)(2,1)S(1)}, u32[]{:S(2)}, u32[]{:S(2)}) collective-permute-start(bf16[64,384]{1,0:T(8,128)(2,1)S(1)} %get-tuple-element.45), channel_id=1, source_target_pairs={{0,48},{16,32},{32,80},{48,64},{64,112},{80,96},{96,16},{112,0},{1... | collective-permute-start | bytes 147464 | tf_op jit(solution)/shard_map/ppermute | solution.py:289
  88.0 2.0 %collective-permute-start.10 = (bf16[64,384]{1,0:T(8,128)(2,1)S(1)}, bf16[64,384]{1,0:T(8,128)(2,1)S(1)}, u32[]{:S(2)}, u32[]{:S(2)}) collective-permute-start(bf16[64,384]{1,0:T(8,128)(2,1)S(1)} %get-tuple-element.46), channel_id=1, source_target_pairs={{0,64},{16,80},{32,96},{48,112},{64,0},{80,16},{96,32},{112,48},{1... | collective-permute-start | bytes 147464 | tf_op jit(solution)/shard_map/ppermute | solution.py:289
  90.0 1.2 %collective-permute-start.11 = (bf16[64,384]{1,0:T(8,128)(2,1)S(1)}, bf16[64,384]{1,0:T(8,128)(2,1)S(1)}, u32[]{:S(2)}, u32[]{:S(2)}) collective-permute-start(bf16[64,384]{1,0:T(8,128)(2,1)S(1)} %get-tuple-element.47), channel_id=1, source_target_pairs={{0,80},{16,64},{32,112},{48,96},{64,16},{80,0},{96,48},{112,32},{1... | collective-permute-start | bytes 147464 | tf_op jit(solution)/shard_map/ppermute | solution.py:289
  91.2 0.0 collective-permute-done.7.refs_1_
  91.2 1.5 %collective-permute-start.12 = (bf16[64,384]{1,0:T(8,128)(2,1)S(1)}, bf16[64,384]{1,0:T(8,128)(2,1)S(1)}, u32[]{:S(2)}, u32[]{:S(2)}) collective-permute-start(bf16[64,384]{1,0:T(8,128)(2,1)S(1)} %get-tuple-element.48), channel_id=1, source_target_pairs={{0,96},{16,112},{32,0},{48,16},{64,32},{80,48},{96,64},{112,80},{1... | collective-permute-start | bytes 147464 | tf_op jit(solution)/shard_map/ppermute | solution.py:289
  92.7 1.2 %collective-permute-done.8.refs_2_ = bf16[64,384]{1,0:T(8,128)(2,1)S(1)} collective-permute-done((bf16[64,384]{1,0:T(8,128)(2,1)S(1)}, bf16[64,384]{1,0:T(8,128)(2,1)S(1)}, u32[]{:S(2)}, u32[]{:S(2)}) %collective-permute-start.8) | collective-permute-done | bytes 49184 | tf_op jit(solution)/shard_map/ppermute | solution.py:289
  93.8 1.7 %collective-permute-start.13 = (bf16[64,384]{1,0:T(8,128)(2,1)S(1)}, bf16[64,384]{1,0:T(8,128)(2,1)S(1)}, u32[]{:S(2)}, u32[]{:S(2)}) collective-permute-start(bf16[64,384]{1,0:T(8,128)(2,1)S(1)} %get-tuple-element.49), channel_id=1, source_target_pairs={{0,112},{16,96},{32,16},{48,0},{64,48},{80,32},{96,80},{112,64},{1... | collective-permute-start | bytes 147464 | tf_op jit(solution)/shard_map/ppermute | solution.py:289
  95.5 0.0 collective-permute-done.9.refs_3_
  95.5 0.6 collective-permute-done.10.refs_4_
  96.1 1.5 %collective-permute-done.11.refs_5_ = bf16[64,384]{1,0:T(8,128)(2,1)S(1)} collective-permute-done((bf16[64,384]{1,0:T(8,128)(2,1)S(1)}, bf16[64,384]{1,0:T(8,128)(2,1)S(1)}, u32[]{:S(2)}, u32[]{:S(2)}) %collective-permute-start.11) | collective-permute-done | bytes 49184 | tf_op jit(solution)/shard_map/ppermute | solution.py:289
  97.6 0.0 collective-permute-done.12.refs_6_
  97.6 0.2 collective-permute-done.13.refs_7_
  97.8 1.4 %shard_map.99 = (bf16[512,192]{1,0:T(8,128)(2,1)}, bf16[512,192]{1,0:T(8,128)(2,1)}) custom-call(s32[1]{0:T(128)} %bitcast.place, bf16[64,384]{1,0:T(8,128)(2,1)S(1)} %get-tuple-element.42.refs_0_, bf16[64,384]{1,0:T(8,128)(2,1)S(1)} %collective-permute-done.7.refs_1_, bf16[64,384]{1,0:T(8,128)(2,1)S(1)} %collective-permute-done.8.refs_2_, ...), custom_call_target="tpu_custom_call" | custom-call | flops 100000000 | bytes 1000000 | tf_op jit(solution)/shard_map/pallas_call | solution.py:276
  99.3 0.0 all-to-all-done.3
  99.3 1.2 %shard_map.101 = (f32[192,768]{1,0:T(8,128)}, f32[192,384]{1,0:T(8,128)}) custom-call(bf16[2048,128]{1,0:T(8,128)(2,1)S(1)} %bitcast.20), custom_call_target="tpu_custom_call" | custom-call | flops 100000000 | bytes 1000000 | tf_op jit(solution)/shard_map/pallas_call | solution.py:276
  (7 shorter events, 0.0 us)
Async XLA Ops:
  0.6 10.8 %copy-start.4 = (bf16[16,32,192]{2,1,0:T(8,128)(2,1)S(1)}, bf16[16,32,192]{2,1,0:T(8,128)(2,1)}, u32[]{:S(2)}) copy-start(bf16[16,32,192]{2,1,0:T(8,128)(2,1)} %param.11) | copy-start | bytes 589828
  0.6 10.8 %copy-start.5 = (bf16[16,32,2,6]{1,2,3,0:T(2,128)(2,1)S(1)}, bf16[16,32,2,6]{1,2,3,0:T(2,128)(2,1)}, u32[]{:S(2)}) copy-start(bf16[16,32,2,6]{1,2,3,0:T(2,128)(2,1)} %param.8) | copy-start | bytes 36868
  2.7 8.8 %copy-start.1 = (bf16[16,32,192]{2,1,0:T(8,128)(2,1)S(1)}, bf16[16,32,192]{2,1,0:T(8,128)(2,1)}, u32[]{:S(2)}) copy-start(bf16[16,32,192]{2,1,0:T(8,128)(2,1)} %param.6) | copy-start | bytes 589828
  2.7 8.8 %copy-start.2 = (bf16[16,32,4,16]{1,3,2,0:T(8,128)(2,1)S(1)}, bf16[16,32,4,16]{1,3,2,0:T(8,128)(2,1)}, u32[]{:S(2)}) copy-start(bf16[16,32,4,16]{1,3,2,0:T(8,128)(2,1)} %param.7) | copy-start | bytes 196612
  2.7 18.7 %all-to-all-start = ((bf16[16,32,256]{2,1,0:T(8,128)(2,1)}), bf16[16,32,256]{2,1,0:T(8,128)(2,1)S(1)}, u32[]{:S(2)}, u32[]{:S(2)}) async-start(bf16[16,32,256]{2,1,0:T(8,128)(2,1)} %bitcast.32), calls=%async_computation | async-start | bytes 524288 | tf_op jit(solution)/shard_map/all_to_all | solution.py:303
  11.5 9.9 %copy-start = (bf16[192,768]{1,0:T(8,128)(2,1)S(1)}, bf16[192,768]{1,0:T(8,128)(2,1)}, u32[]{:S(2)}) copy-start(bf16[192,768]{1,0:T(8,128)(2,1)} %w_in.5) | copy-start | bytes 884740
  12.4 7.0 %collective-permute-start = (bf16[64,512]{1,0:T(8,128)(2,1)S(1)}, bf16[64,512]{1,0:T(8,128)(2,1)S(1)}, u32[]{:S(2)}, u32[]{:S(2)}) collective-permute-start(bf16[64,512]{1,0:T(8,128)(2,1)S(1)} %get-tuple-element.30), channel_id=1, source_target_pairs={{0,16},{16,0},{32,48},{48,32},{64,80},{80,64},{96,112},{112,96},{1... | collective-permute-start | bytes 196616 | tf_op jit(solution)/shard_map/ppermute | solution.py:289
  13.5 7.4 %collective-permute-start.1 = (bf16[64,512]{1,0:T(8,128)(2,1)S(1)}, bf16[64,512]{1,0:T(8,128)(2,1)S(1)}, u32[]{:S(2)}, u32[]{:S(2)}) collective-permute-start(bf16[64,512]{1,0:T(8,128)(2,1)S(1)} %get-tuple-element.31), channel_id=1, source_target_pairs={{0,32},{16,48},{32,64},{48,80},{64,96},{80,112},{96,0},{112,16},{1... | collective-permute-start | bytes 196616 | tf_op jit(solution)/shard_map/ppermute | solution.py:289
  14.7 7.9 %collective-permute-start.2 = (bf16[64,512]{1,0:T(8,128)(2,1)S(1)}, bf16[64,512]{1,0:T(8,128)(2,1)S(1)}, u32[]{:S(2)}, u32[]{:S(2)}) collective-permute-start(bf16[64,512]{1,0:T(8,128)(2,1)S(1)} %get-tuple-element.32), channel_id=1, source_target_pairs={{0,48},{16,32},{32,80},{48,64},{64,112},{80,96},{96,16},{112,0},{1... | collective-permute-start | bytes 196616 | tf_op jit(solution)/shard_map/ppermute | solution.py:289
  16.1 6.5 %collective-permute-start.3 = (bf16[64,512]{1,0:T(8,128)(2,1)S(1)}, bf16[64,512]{1,0:T(8,128)(2,1)S(1)}, u32[]{:S(2)}, u32[]{:S(2)}) collective-permute-start(bf16[64,512]{1,0:T(8,128)(2,1)S(1)} %get-tuple-element.33), channel_id=1, source_target_pairs={{0,64},{16,80},{32,96},{48,112},{64,0},{80,16},{96,32},{112,48},{1... | collective-permute-start | bytes 196616 | tf_op jit(solution)/shard_map/ppermute | solution.py:289
  17.6 6.1 %collective-permute-start.4 = (bf16[64,512]{1,0:T(8,128)(2,1)S(1)}, bf16[64,512]{1,0:T(8,128)(2,1)S(1)}, u32[]{:S(2)}, u32[]{:S(2)}) collective-permute-start(bf16[64,512]{1,0:T(8,128)(2,1)S(1)} %get-tuple-element.34), channel_id=1, source_target_pairs={{0,80},{16,64},{32,112},{48,96},{64,16},{80,0},{96,48},{112,32},{1... | collective-permute-start | bytes 196616 | tf_op jit(solution)/shard_map/ppermute | solution.py:289
  19.4 4.7 %collective-permute-start.5 = (bf16[64,512]{1,0:T(8,128)(2,1)S(1)}, bf16[64,512]{1,0:T(8,128)(2,1)S(1)}, u32[]{:S(2)}, u32[]{:S(2)}) collective-permute-start(bf16[64,512]{1,0:T(8,128)(2,1)S(1)} %get-tuple-element.35), channel_id=1, source_target_pairs={{0,96},{16,112},{32,0},{48,16},{64,32},{80,48},{96,64},{112,80},{1... | collective-permute-start | bytes 196616 | tf_op jit(solution)/shard_map/ppermute | solution.py:289
  20.9 4.6 %collective-permute-start.6 = (bf16[64,512]{1,0:T(8,128)(2,1)S(1)}, bf16[64,512]{1,0:T(8,128)(2,1)S(1)}, u32[]{:S(2)}, u32[]{:S(2)}) collective-permute-start(bf16[64,512]{1,0:T(8,128)(2,1)S(1)} %get-tuple-element.36), channel_id=1, source_target_pairs={{0,112},{16,96},{32,16},{48,0},{64,48},{80,32},{96,80},{112,64},{1... | collective-permute-start | bytes 196616 | tf_op jit(solution)/shard_map/ppermute | solution.py:289
  21.4 4.2 %copy-start.3 = (bf16[384,192]{0,1:T(8,128)(2,1)S(1)}, bf16[384,192]{0,1:T(8,128)(2,1)}, u32[]{:S(2)}) copy-start(bf16[384,192]{0,1:T(8,128)(2,1)} %param.10) | copy-start | bytes 442372
  80.1 19.2 %all-to-all-start.3 = ((bf16[128,16,128]{2,1,0:T(8,128)(2,1)}), bf16[128,16,128]{2,1,0:T(8,128)(2,1)S(1)}, u32[]{:S(2)}, u32[]{:S(2)}) async-start(bf16[128,16,128]{2,1,0:T(8,128)(2,1)} %shard_map.100), calls=%async_computation.3 | async-start | bytes 1048576 | tf_op jit(solution)/shard_map/all_to_all | solution.py:326
  84.6 6.6 %collective-permute-start.7 = (bf16[64,384]{1,0:T(8,128)(2,1)S(1)}, bf16[64,384]{1,0:T(8,128)(2,1)S(1)}, u32[]{:S(2)}, u32[]{:S(2)}) collective-permute-start(bf16[64,384]{1,0:T(8,128)(2,1)S(1)} %get-tuple-element.43), channel_id=1, source_target_pairs={{0,16},{16,0},{32,48},{48,32},{64,80},{80,64},{96,112},{112,96},{1... | collective-permute-start | bytes 147464 | tf_op jit(solution)/shard_map/ppermute | solution.py:289
  85.9 7.9 %collective-permute-start.8 = (bf16[64,384]{1,0:T(8,128)(2,1)S(1)}, bf16[64,384]{1,0:T(8,128)(2,1)S(1)}, u32[]{:S(2)}, u32[]{:S(2)}) collective-permute-start(bf16[64,384]{1,0:T(8,128)(2,1)S(1)} %get-tuple-element.44), channel_id=1, source_target_pairs={{0,32},{16,48},{32,64},{48,80},{64,96},{80,112},{96,0},{112,16},{1... | collective-permute-start | bytes 147464 | tf_op jit(solution)/shard_map/ppermute | solution.py:289
  86.4 9.0 %collective-permute-start.9 = (bf16[64,384]{1,0:T(8,128)(2,1)S(1)}, bf16[64,384]{1,0:T(8,128)(2,1)S(1)}, u32[]{:S(2)}, u32[]{:S(2)}) collective-permute-start(bf16[64,384]{1,0:T(8,128)(2,1)S(1)} %get-tuple-element.45), channel_id=1, source_target_pairs={{0,48},{16,32},{32,80},{48,64},{64,112},{80,96},{96,16},{112,0},{1... | collective-permute-start | bytes 147464 | tf_op jit(solution)/shard_map/ppermute | solution.py:289
  88.0 8.1 %collective-permute-start.10 = (bf16[64,384]{1,0:T(8,128)(2,1)S(1)}, bf16[64,384]{1,0:T(8,128)(2,1)S(1)}, u32[]{:S(2)}, u32[]{:S(2)}) collective-permute-start(bf16[64,384]{1,0:T(8,128)(2,1)S(1)} %get-tuple-element.46), channel_id=1, source_target_pairs={{0,64},{16,80},{32,96},{48,112},{64,0},{80,16},{96,32},{112,48},{1... | collective-permute-start | bytes 147464 | tf_op jit(solution)/shard_map/ppermute | solution.py:289
  90.0 7.6 %collective-permute-start.11 = (bf16[64,384]{1,0:T(8,128)(2,1)S(1)}, bf16[64,384]{1,0:T(8,128)(2,1)S(1)}, u32[]{:S(2)}, u32[]{:S(2)}) collective-permute-start(bf16[64,384]{1,0:T(8,128)(2,1)S(1)} %get-tuple-element.47), channel_id=1, source_target_pairs={{0,80},{16,64},{32,112},{48,96},{64,16},{80,0},{96,48},{112,32},{1... | collective-permute-start | bytes 147464 | tf_op jit(solution)/shard_map/ppermute | solution.py:289
  91.2 6.4 %collective-permute-start.12 = (bf16[64,384]{1,0:T(8,128)(2,1)S(1)}, bf16[64,384]{1,0:T(8,128)(2,1)S(1)}, u32[]{:S(2)}, u32[]{:S(2)}) collective-permute-start(bf16[64,384]{1,0:T(8,128)(2,1)S(1)} %get-tuple-element.48), channel_id=1, source_target_pairs={{0,96},{16,112},{32,0},{48,16},{64,32},{80,48},{96,64},{112,80},{1... | collective-permute-start | bytes 147464 | tf_op jit(solution)/shard_map/ppermute | solution.py:289
  93.8 4.0 %collective-permute-start.13 = (bf16[64,384]{1,0:T(8,128)(2,1)S(1)}, bf16[64,384]{1,0:T(8,128)(2,1)S(1)}, u32[]{:S(2)}, u32[]{:S(2)}) collective-permute-start(bf16[64,384]{1,0:T(8,128)(2,1)S(1)} %get-tuple-element.49), channel_id=1, source_target_pairs={{0,112},{16,96},{32,16},{48,0},{64,48},{80,32},{96,80},{112,64},{1... | collective-permute-start | bytes 147464 | tf_op jit(solution)/shard_map/ppermute | solution.py:289

commit v3 on v2

--- a/solution.py
+++ b/solution.py
@@ -30,11 +30,6 @@
     return lax.dot_general(a, b, (((0,), (0,)), ((), ())), preferred_element_type=F32)
 
 
-def spread(aux, first):
-    pick = (iota((256, 128), 0) - first == iota((256, 128), 1) % 16).astype(F32).astype(BF)
-    return mm(aux, pick)
-
-
 HALVES = (slice(0, GROUP), slice(GROUP, TOK))
 
 
@@ -42,10 +37,13 @@
     token = iota((TOK, 128), 0)
     chunk = token // 64 if by_row else (token // GROUP) * 4 + token % 4
     member = (iota((TOK, 128), 1) // 16 == chunk).astype(F32)
-    b_part = (spread(aux, 192) * member).astype(BF)
-    c_part = (spread(aux, 208) * member).astype(BF)
-    heads = (iota((256, CHAN), 0) - 224 == iota((256, CHAN), 1) // 64).astype(F32).astype(BF)
-    log_step = mm(aux, heads).astype(BF)
+    lane = iota((256, 640), 1)
+    wanted = jnp.where(lane < 128, 192 + lane % 16, 208 + lane % 16)
+    wanted = jnp.where(lane < 256, wanted, 220 + lane // 64)
+    spread = mm(aux, (iota((256, 640), 0) == wanted).astype(F32).astype(BF))
+    b_part = (spread[:, 0:128] * member).astype(BF)
+    c_part = (spread[:, 128:256] * member).astype(BF)
+    log_step = spread[:, 256:].astype(BF)
     here, there = iota((GROUP, GROUP), 0), iota((GROUP, GROUP), 1)
     same = (here // 64 == there // 64) if by_row else (here % 4 == there % 4)
     if forward:
@@ -127,12 +125,12 @@
     left = mm(choose, feat[:, 0:128]).astype(BF)
     middle = mm(choose, with_aux(feat, sel, log, 1)).astype(BF)
     right = mm(choose, cot[...]).astype(BF)
-    for k in range(8):
-        rows = slice(64 * k, 64 * k + 64)
+    for k in range(4):
+        rows = slice(128 * k, 128 * k + 128)
         outs[k][:, 0:128] = left[rows]
         outs[k][:, 128:256] = middle[rows]
         outs[k][:, 256 : 256 + MODEL] = right[rows]
-        outs[k][:, 256 + MODEL :] = jnp.zeros((64, 64), BF)
+        outs[k][:, 256 + MODEL :] = jnp.zeros((128, 64), BF)
 
 
 def row_forward_kernel(packed, w_in, out):
@@ -155,7 +153,9 @@
 def col_adjoint_kernel(place, row_out, w_in, w_out, *refs):
     pieces, (out, whole, tokens, scratch) = refs[:8], refs[8:]
     for k in range(8):
-        whole[pl.ds(pl.multiple_of(sender(place, k) * 64, 64), 64), :] = pieces[k][...]
+        half, first = k % 2, 64 * (k % 2)
+        rows = pl.ds(pl.multiple_of(sender(place, k) * 64, 64), 64)
+        whole[rows, :] = pieces[4 * half + k // 2][first : first + 64, :]
     aux = whole[:, :256]
     cot = whole[:, 256 : 256 + MODEL]
     gate, sig, hidden_grad = gate_terms(aux, cot, w_in, w_out)
@@ -239,20 +239,8 @@
         outs[k][...] = whole[rows, :]
 
 
-def tokens_kernel(place, *refs):
-    pieces, (block, grad, part, whole) = refs[:8], refs[8:]
-    for k in range(8):
-        first = 4 * sender(place, k)
-        split_lanes(part, pieces[k][...].astype(F32))
-        for l in range(3):
-            for j in range(4):
-                whole[l, pl.ds(first + j, 16, stride=32), :] = part[l, pl.ds(j, 16, stride=4), :]
-    middle = whole[1]
-    block[...] = jnp.concatenate([whole[0], middle[:, :64]], axis=1).astype(BF)
-    grad[...] = jnp.concatenate([middle[:, 64:], whole[2]], axis=1).astype(BF)
-
-
-def weights_kernel(sums, in_grad, out_grad, weights):
+def last_kernel(place, sums, *refs):
+    pieces, (block, grad, in_grad, out_grad, part, whole, weights) = refs[:8], refs[8:]
     weights[...] = sums[...].astype(F32)
     strided = lambda first: weights[pl.ds(first, 128, stride=16), :]
     for l in range(3):
@@ -267,6 +255,15 @@
         lanes = slice(128 * k, 128 * k + 128)
         out_grad[0:64, lanes] = strided(9 + 2 * k).T[64:128]
         out_grad[64:192, lanes] = strided(10 + 2 * k).T
+    for k in range(8):
+        first = 4 * sender(place, k)
+        split_lanes(part.at[k], pieces[k][...].astype(F32))
+        for l in range(3):
+            for j in range(4):
+                whole[l, pl.ds(first + j, 16, stride=32), :] = part[k, l, pl.ds(j, 16, stride=4), :]
+    middle = whole[1]
+    block[...] = jnp.concatenate([whole[0], middle[:, :64]], axis=1).astype(BF)
+    grad[...] = jnp.concatenate([middle[:, 64:], whole[2]], axis=1).astype(BF)
 
 
 def call(kernel, outs, ins, scratch=(), flops=10**8, vmem=VMEM_LIMIT):
@@ -289,6 +286,12 @@
     return [pieces[0]] + [lax.ppermute(pieces[k], "row", pairs(k)) for k in range(1, 8)]
 
 
+def swap_rows_in_steps(pieces):
+    along = lambda s: [(i, (i + 2 * s) % 8) for i in range(8)]
+    mine = [pieces[0]] + [lax.ppermute(pieces[s], "row", along(s)) for s in (1, 2, 3)]
+    return mine + [lax.ppermute(piece, "row", [(i, i ^ 1) for i in range(8)]) for piece in mine]
+
+
 def on_device(features, selectors, log_decay, in_weight, out_weight, cotangent):
     place = lax.axis_index("row").astype(jnp.int32).reshape(1)
     out_turned = out_weight.T
@@ -303,11 +306,13 @@
     row_packed = lax.all_to_all(row_packed.reshape(16, 32, 256), "col", 0, 0).reshape(TOK, 256)
     pieces = call(
         pack_columns_kernel,
-        [((64, 512), BF)] * 8,
+        [((128, 512), BF)] * 4,
         [place, feat, cotangent.reshape(TOK, MODEL), sel, log],
     )
-    pieces = swap_rows(pieces)
-    (row_out,) = call(row_forward_kernel, [((TOK, CHAN), BF)], [row_packed, in_weight])
+    pieces = swap_rows_in_steps(pieces)
+    (row_out,) = call(
+        row_forward_kernel, [((TOK, CHAN), BF)], [row_packed, in_weight], flops=3 * 10**10
+    )
     sent, whole = call(
         col_adjoint_kernel,
         [((1024, CHAN), BF), ((TOK, 512), BF)],
@@ -330,17 +335,11 @@
         [place, came, partial, block],
         [((2, 1024, 128), F32), ((2, TOK, 128), F32), ((TOK, CHAN), BF)],
     )
-    block, grad = call(
-        tokens_kernel,
-        [((TOK, MODEL), BF)] * 2,
-        [place, *swap_rows(pieces)],
-        [((3, 64, 128), F32), tall],
-    )
-    in_grad, out_grad = call(
-        weights_kernel,
-        [((MODEL, 2 * CHAN), F32), ((MODEL, CHAN), F32)],
-        [sums],
-        [((2048, 128), F32)],
+    block, grad, in_grad, out_grad = call(
+        last_kernel,
+        [((TOK, MODEL), BF)] * 2 + [((MODEL, 2 * CHAN), F32), ((MODEL, CHAN), F32)],
+        [place, sums, *swap_rows(pieces)],
+        [((8, 3, 64, 128), F32), tall, ((2048, 128), F32)],
     )
     return (block.reshape(16, 32, MODEL), grad.reshape(16, 32, MODEL), in_grad, out_grad.T)
 

time: 101 us -> 99.1 us (0.981)
    ppermute x0 -> x7, starting transfers between devices: none -> 9.86 us  [the longest x4 4.98 us: swap_rows_in_steps(): lax.ppermute(piece, 'row', [(i, i ^ 1) for i in range(8)])]
    ppermute x14 -> x7, starting transfers between devices: 18.7 us -> 9.7 us  [swap_rows(): lax.ppermute(pieces[k], 'row', pairs(k))]
    ppermute x14 -> x7, waiting for transfers between devices: 6.45 us -> 3.53 us  [swap_rows(): lax.ppermute(pieces[k], 'row', pairs(k))]
    ppermute x0 -> x7, waiting for transfers between devices: none -> 1.27 us  [the longest x3 1.13 us: swap_rows_in_steps(): lax.ppermute(pieces[s], 'row', along(s))]
    pallas_call x9 -> x8, Pallas kernels: 15.5 us -> 14.5 us  [call(): pl.pallas_call(kernel, out_shape=[jax.ShapeDtypeStruct(shape, dtype) for...]
  transfers between devices with their start and end apart: 16 -> 16, of which waited for: 7 -> 7; matrix products, arithmetic and copies ran while one was open for 0% -> 0% of each run, Pallas kernels for 4% -> 2%
where the time goes in v3:
time: 99.1 us; the launch traced here: 98.8 us
  blocking collectives  45.4 us (46%)
  starting transfers between devices  32.4 us (33%)
  Pallas kernels  14.5 us (15%)
  waiting for transfers between devices  5.57 us (6%)
    all_to_all x2, blocking collectives, on_device(): came = lax.all_to_all(sent.reshape(128, 8, CHAN), ('row', 'col'), 0, 0)  45.4 us
    pallas_call x8, Pallas kernels, call(): pl.pallas_call(kernel, out_shape=[jax.ShapeDtypeStruct(shape, dtype) for...  14.5 us
    ppermute x7, starting transfers between devices, swap_rows(): lax.ppermute(pieces[k], 'row', pairs(k))  9.7 us
    all_to_all x1, starting transfers between devices, on_device(): lax.all_to_all(row_packed.reshape(16, 32, 256), 'col', 0, 0)  8.73 us
    ppermute x4, starting transfers between devices, swap_rows_in_steps(): lax.ppermute(piece, 'row', [(i, i ^ 1) for i in range(8)])  4.98 us
    ppermute x3, starting transfers between devices, swap_rows_in_steps(): lax.ppermute(pieces[s], 'row', along(s))  4.88 us
    all_to_all x1, starting transfers between devices, on_device(): sums = lax.all_to_all(sums, ('row', 'col'), 0, 0).reshape(2048, 128)  4.15 us
    ppermute x7, waiting for transfers between devices, swap_rows(): lax.ppermute(pieces[k], 'row', pairs(k))  3.53 us
  transfers between devices with their start and end apart: 16, of which 7 were waited for; matrix products, arithmetic and copies ran while one was open for 0% of the time, Pallas kernels for 2%

profile of v3, /device:TPU:1, one launch (start us, length us, event | category | flops | bytes accessed | tf_op | source)
XLA Modules:
  0.0 98.8 jit_solution(12728473992711098507)
XLA Ops:
  0.7 2.0 %shard_map.93 = bf16[512,256]{1,0:T(8,128)(2,1)} custom-call(bf16[512,192]{1,0:T(8,128)(2,1)} %bitcast.19, bf16[16,64,32]{2,1,0:T(8,128)(2,1)} %bitcast.21, bf16[16,6,2,32]{3,2,1,0:T(2,128)(2,1)} %bitcast.30), custom_call_target="tpu_custom_call" | custom-call | flops 100000000 | bytes 1000000 | tf_op jit(solution)/shard_map/pallas_call | solution.py:273
  2.7 8.7 %all-to-all-start = ((bf16[16,32,256]{2,1,0:T(8,128)(2,1)}), bf16[16,32,256]{2,1,0:T(8,128)(2,1)S(1)}, u32[]{:S(2)}, u32[]{:S(2)}) async-start(bf16[16,32,256]{2,1,0:T(8,128)(2,1)} %bitcast.32), calls=%async_computation | async-start | bytes 524288 | tf_op jit(solution)/shard_map/all_to_all | solution.py:306
  11.4 0.0 copy-done.4
  11.4 0.0 copy-done.5
  11.4 0.0 copy-done.1
  11.4 0.0 copy-done.2
  11.5 0.0 copy-start
  11.5 0.9 shard_map.95
  12.4 1.3 %collective-permute-start = (bf16[128,512]{1,0:T(8,128)(2,1)S(1)}, bf16[128,512]{1,0:T(8,128)(2,1)S(1)}, u32[]{:S(2)}, u32[]{:S(2)}) collective-permute-start(bf16[128,512]{1,0:T(8,128)(2,1)S(1)} %get-tuple-element.26), channel_id=1, source_target_pairs={{0,32},{16,48},{32,64},{48,80},{64,96},{80,112},{96,0},{112,16},{1... | collective-permute-start | bytes 393224 | tf_op jit(solution)/shard_map/ppermute | solution.py:291
  13.7 2.4 %collective-permute-start.1 = (bf16[128,512]{1,0:T(8,128)(2,1)S(1)}, bf16[128,512]{1,0:T(8,128)(2,1)S(1)}, u32[]{:S(2)}, u32[]{:S(2)}) collective-permute-start(bf16[128,512]{1,0:T(8,128)(2,1)S(1)} %get-tuple-element.27), channel_id=1, source_target_pairs={{0,64},{16,80},{32,96},{48,112},{64,0},{80,16},{96,32},{112,48},{1... | collective-permute-start | bytes 393224 | tf_op jit(solution)/shard_map/ppermute | solution.py:291
  16.2 1.2 %collective-permute-start.2 = (bf16[128,512]{1,0:T(8,128)(2,1)S(1)}, bf16[128,512]{1,0:T(8,128)(2,1)S(1)}, u32[]{:S(2)}, u32[]{:S(2)}) collective-permute-start(bf16[128,512]{1,0:T(8,128)(2,1)S(1)} %get-tuple-element.28), channel_id=1, source_target_pairs={{0,96},{16,112},{32,0},{48,16},{64,32},{80,48},{96,64},{112,80},{1... | collective-permute-start | bytes 393224 | tf_op jit(solution)/shard_map/ppermute | solution.py:291
  17.3 1.8 %collective-permute-start.3 = (bf16[128,512]{1,0:T(8,128)(2,1)S(1)}, bf16[128,512]{1,0:T(8,128)(2,1)S(1)}, u32[]{:S(2)}, u32[]{:S(2)}) collective-permute-start(bf16[128,512]{1,0:T(8,128)(2,1)S(1)} %get-tuple-element.25.refs_0_), channel_id=1, source_target_pairs={{0,16},{16,0},{32,48},{48,32},{64,80},{80,64},{96,112},{112,96},{1... | collective-permute-start | bytes 393224 | tf_op jit(solution)/shard_map/ppermute | solution.py:292
  19.1 0.0 collective-permute-done.refs_1_
  19.1 1.0 %collective-permute-start.4 = (bf16[128,512]{1,0:T(8,128)(2,1)S(1)}, bf16[128,512]{1,0:T(8,128)(2,1)S(1)}, u32[]{:S(2)}, u32[]{:S(2)}) collective-permute-start(bf16[128,512]{1,0:T(8,128)(2,1)S(1)} %collective-permute-done.refs_1_), channel_id=1, source_target_pairs={{0,16},{16,0},{32,48},{48,32},{64,80},{80,64},{96,112},{112,96},{1... | collective-permute-start | bytes 393224 | tf_op jit(solution)/shard_map/ppermute | solution.py:292
  20.1 1.1 %collective-permute-done.1.refs_2_ = bf16[128,512]{1,0:T(8,128)(2,1)S(1)} collective-permute-done((bf16[128,512]{1,0:T(8,128)(2,1)S(1)}, bf16[128,512]{1,0:T(8,128)(2,1)S(1)}, u32[]{:S(2)}, u32[]{:S(2)}) %collective-permute-start.1) | collective-permute-done | bytes 131104 | tf_op jit(solution)/shard_map/ppermute | solution.py:291
  21.2 2.2 %collective-permute-start.5 = (bf16[128,512]{1,0:T(8,128)(2,1)S(1)}, bf16[128,512]{1,0:T(8,128)(2,1)S(1)}, u32[]{:S(2)}, u32[]{:S(2)}) collective-permute-start(bf16[128,512]{1,0:T(8,128)(2,1)S(1)} %collective-permute-done.1.refs_2_), channel_id=1, source_target_pairs={{0,16},{16,0},{32,48},{48,32},{64,80},{80,64},{96,112},{112,96},{1... | collective-permute-start | bytes 393224 | tf_op jit(solution)/shard_map/ppermute | solution.py:292
  23.4 0.0 collective-permute-done.2.refs_3_
  23.4 0.0 collective-permute-start.6
  23.4 0.0 all-to-all-done
  23.4 0.0 copy-start.3
  23.4 1.1 %shard_map.94.row_out = bf16[512,384]{1,0:T(8,128)(2,1)S(1)} custom-call(bf16[512,256]{1,0:T(8,128)(2,1)S(1)} %bitcast.23, bf16[192,768]{1,0:T(8,128)(2,1)S(1)} %copy-done), custom_call_target="tpu_custom_call" | custom-call | flops 30000001024 | bytes 1000000 | tf_op jit(solution)/shard_map/pallas_call | solution.py:273
  24.6 0.0 collective-permute-done.3.refs_4_
  24.6 0.0 collective-permute-done.4.refs_5_
  24.6 0.0 collective-permute-done.5.refs_6_
  24.6 0.1 collective-permute-done.6.refs_7_
  24.8 2.3 %shard_map.96 = (bf16[1024,384]{1,0:T(8,128)(2,1)S(1)}, bf16[512,512]{1,0:T(8,128)(2,1)S(1)}) custom-call(s32[1]{0:T(128)} %bitcast.place, bf16[512,384]{1,0:T(8,128)(2,1)S(1)} %shard_map.94.row_out, bf16[192,768]{1,0:T(8,128)(2,1)S(1)} %copy-done, bf16[192,384]{1,0:T(8,128)(2,1)S(1)} %bitcast.27, bf16[128,512]{1,0:T(8,128)(2,1)S(1)} %get-tuple-element.25.refs_0_, ...), custom_call_target="tpu_custom_call" | custom-call | flops 100000000 | bytes 1000000 | tf_op jit(solution)/shard_map/pallas_call | solution.py:273
  27.0 25.0 %all_to_all.20 = bf16[128,8,384]{2,1,0:T(8,128)(2,1)S(1)} all-to-all(bf16[128,8,384]{2,1,0:T(8,128)(2,1)S(1)} %bitcast.25), channel_id=1, replica_groups=mesh['row'=8,'col'=16] {'row','col'}, dimensions={0} | all-to-all | bytes 1572864 | tf_op jit(solution)/shard_map/all_to_all | solution.py:322
  52.1 4.8 %shard_map.97 = (f32[512,192]{1,0:T(8,128)S(1)}, f32[512,192]{1,0:T(8,128)S(1)}, bf16[1024,384]{1,0:T(8,128)(2,1)S(1)}) custom-call(bf16[1024,384]{1,0:T(8,128)(2,1)S(1)} %bitcast.17, bf16[512,512]{1,0:T(8,128)(2,1)S(1)} %get-tuple-element.30.whole, bf16[512,256]{1,0:T(8,128)(2,1)S(1)} %bitcast.24, bf16[192,768]{1,0:T(8,128)(2,1)S(1)} %copy-done, ...), custom_call_target="tpu_custom_call" | custom-call | flops 100000000 | bytes 1000000 | tf_op jit(solution)/shard_map/pallas_call | solution.py:273
  56.9 20.4 %all_to_all.21.came = bf16[128,8,384]{2,1,0:T(8,128)(2,1)S(1)} all-to-all(bf16[128,8,384]{2,1,0:T(8,128)(2,1)S(1)} %bitcast.26), channel_id=1, replica_groups=mesh['row'=8,'col'=16] {'row','col'}, dimensions={0} | all-to-all | bytes 1572864 | tf_op jit(solution)/shard_map/all_to_all | solution.py:329
  77.2 1.0 shard_map.98
  78.2 4.2 %all-to-all-start.3 = ((bf16[128,16,128]{2,1,0:T(8,128)(2,1)}), bf16[128,16,128]{2,1,0:T(8,128)(2,1)S(1)}, u32[]{:S(2)}, u32[]{:S(2)}) async-start(bf16[128,16,128]{2,1,0:T(8,128)(2,1)} %shard_map.98), calls=%async_computation.3 | async-start | bytes 1048576 | tf_op jit(solution)/shard_map/all_to_all | solution.py:331
  82.3 0.3 shard_map.99
  82.7 1.3 %collective-permute-start.7 = (bf16[64,384]{1,0:T(8,128)(2,1)S(1)}, bf16[64,384]{1,0:T(8,128)(2,1)S(1)}, u32[]{:S(2)}, u32[]{:S(2)}) collective-permute-start(bf16[64,384]{1,0:T(8,128)(2,1)S(1)} %get-tuple-element.35), channel_id=1, source_target_pairs={{0,16},{16,0},{32,48},{48,32},{64,80},{80,64},{96,112},{112,96},{1... | collective-permute-start | bytes 147464 | tf_op jit(solution)/shard_map/ppermute | solution.py:286
  84.0 0.5 collective-permute-start.8
  84.5 1.5 %collective-permute-start.9 = (bf16[64,384]{1,0:T(8,128)(2,1)S(1)}, bf16[64,384]{1,0:T(8,128)(2,1)S(1)}, u32[]{:S(2)}, u32[]{:S(2)}) collective-permute-start(bf16[64,384]{1,0:T(8,128)(2,1)S(1)} %get-tuple-element.37), channel_id=1, source_target_pairs={{0,48},{16,32},{32,80},{48,64},{64,112},{80,96},{96,16},{112,0},{1... | collective-permute-start | bytes 147464 | tf_op jit(solution)/shard_map/ppermute | solution.py:286
  86.0 2.0 %collective-permute-start.10 = (bf16[64,384]{1,0:T(8,128)(2,1)S(1)}, bf16[64,384]{1,0:T(8,128)(2,1)S(1)}, u32[]{:S(2)}, u32[]{:S(2)}) collective-permute-start(bf16[64,384]{1,0:T(8,128)(2,1)S(1)} %get-tuple-element.38), channel_id=1, source_target_pairs={{0,64},{16,80},{32,96},{48,112},{64,0},{80,16},{96,32},{112,48},{1... | collective-permute-start | bytes 147464 | tf_op jit(solution)/shard_map/ppermute | solution.py:286
  88.1 1.2 %collective-permute-start.11 = (bf16[64,384]{1,0:T(8,128)(2,1)S(1)}, bf16[64,384]{1,0:T(8,128)(2,1)S(1)}, u32[]{:S(2)}, u32[]{:S(2)}) collective-permute-start(bf16[64,384]{1,0:T(8,128)(2,1)S(1)} %get-tuple-element.39), channel_id=1, source_target_pairs={{0,80},{16,64},{32,112},{48,96},{64,16},{80,0},{96,48},{112,32},{1... | collective-permute-start | bytes 147464 | tf_op jit(solution)/shard_map/ppermute | solution.py:286
  89.2 0.0 collective-permute-done.7.refs_1_
  89.2 1.5 %collective-permute-start.12 = (bf16[64,384]{1,0:T(8,128)(2,1)S(1)}, bf16[64,384]{1,0:T(8,128)(2,1)S(1)}, u32[]{:S(2)}, u32[]{:S(2)}) collective-permute-start(bf16[64,384]{1,0:T(8,128)(2,1)S(1)} %get-tuple-element.40), channel_id=1, source_target_pairs={{0,96},{16,112},{32,0},{48,16},{64,32},{80,48},{96,64},{112,80},{1... | collective-permute-start | bytes 147464 | tf_op jit(solution)/shard_map/ppermute | solution.py:286
  90.7 1.2 %collective-permute-done.8.refs_2_ = bf16[64,384]{1,0:T(8,128)(2,1)S(1)} collective-permute-done((bf16[64,384]{1,0:T(8,128)(2,1)S(1)}, bf16[64,384]{1,0:T(8,128)(2,1)S(1)}, u32[]{:S(2)}, u32[]{:S(2)}) %collective-permute-start.8) | collective-permute-done | bytes 49184 | tf_op jit(solution)/shard_map/ppermute | solution.py:286
  91.9 1.7 %collective-permute-start.13 = (bf16[64,384]{1,0:T(8,128)(2,1)S(1)}, bf16[64,384]{1,0:T(8,128)(2,1)S(1)}, u32[]{:S(2)}, u32[]{:S(2)}) collective-permute-start(bf16[64,384]{1,0:T(8,128)(2,1)S(1)} %get-tuple-element.41), channel_id=1, source_target_pairs={{0,112},{16,96},{32,16},{48,0},{64,48},{80,32},{96,80},{112,64},{1... | collective-permute-start | bytes 147464 | tf_op jit(solution)/shard_map/ppermute | solution.py:286
  93.5 0.0 collective-permute-done.9.refs_3_
  93.5 0.6 collective-permute-done.10.refs_4_
  94.1 1.5 %collective-permute-done.11.refs_5_ = bf16[64,384]{1,0:T(8,128)(2,1)S(1)} collective-permute-done((bf16[64,384]{1,0:T(8,128)(2,1)S(1)}, bf16[64,384]{1,0:T(8,128)(2,1)S(1)}, u32[]{:S(2)}, u32[]{:S(2)}) %collective-permute-start.11) | collective-permute-done | bytes 49184 | tf_op jit(solution)/shard_map/ppermute | solution.py:286
  95.7 0.0 collective-permute-done.12.refs_6_
  95.7 0.2 collective-permute-done.13.refs_7_
  95.9 0.8 all-to-all-done.3
  96.7 2.1 %shard_map.100 = (bf16[512,192]{1,0:T(8,128)(2,1)}, bf16[512,192]{1,0:T(8,128)(2,1)}, f32[192,768]{1,0:T(8,128)}, f32[192,384]{1,0:T(8,128)}) custom-call(s32[1]{0:T(128)} %bitcast.place, bf16[2048,128]{1,0:T(8,128)(2,1)S(1)} %bitcast.18, bf16[64,384]{1,0:T(8,128)(2,1)S(1)} %get-tuple-element.34.refs_0_, bf16[64,384]{1,0:T(8,128)(2,1)S(1)} %collective-permute-done.7.refs_1_, ...), custom_call_target="tpu_custom_call" | custom-call | flops 100000000 | bytes 1000000 | tf_op jit(solution)/shard_map/pallas_call | solution.py:273
  (6 shorter events, 0.0 us)
Async XLA Ops:
  0.6 10.8 %copy-start.4 = (bf16[16,32,192]{2,1,0:T(8,128)(2,1)S(1)}, bf16[16,32,192]{2,1,0:T(8,128)(2,1)}, u32[]{:S(2)}) copy-start(bf16[16,32,192]{2,1,0:T(8,128)(2,1)} %param.11) | copy-start | bytes 589828
  0.6 10.8 %copy-start.5 = (bf16[16,32,2,6]{1,2,3,0:T(2,128)(2,1)S(1)}, bf16[16,32,2,6]{1,2,3,0:T(2,128)(2,1)}, u32[]{:S(2)}) copy-start(bf16[16,32,2,6]{1,2,3,0:T(2,128)(2,1)} %param.8) | copy-start | bytes 36868
  2.7 8.8 %copy-start.1 = (bf16[16,32,192]{2,1,0:T(8,128)(2,1)S(1)}, bf16[16,32,192]{2,1,0:T(8,128)(2,1)}, u32[]{:S(2)}) copy-start(bf16[16,32,192]{2,1,0:T(8,128)(2,1)} %param.6) | copy-start | bytes 589828
  2.7 8.8 %copy-start.2 = (bf16[16,32,4,16]{1,3,2,0:T(8,128)(2,1)S(1)}, bf16[16,32,4,16]{1,3,2,0:T(8,128)(2,1)}, u32[]{:S(2)}) copy-start(bf16[16,32,4,16]{1,3,2,0:T(8,128)(2,1)} %param.7) | copy-start | bytes 196612
  2.7 20.7 %all-to-all-start = ((bf16[16,32,256]{2,1,0:T(8,128)(2,1)}), bf16[16,32,256]{2,1,0:T(8,128)(2,1)S(1)}, u32[]{:S(2)}, u32[]{:S(2)}) async-start(bf16[16,32,256]{2,1,0:T(8,128)(2,1)} %bitcast.32), calls=%async_computation | async-start | bytes 524288 | tf_op jit(solution)/shard_map/all_to_all | solution.py:306
  11.5 12.0 %copy-start = (bf16[192,768]{1,0:T(8,128)(2,1)S(1)}, bf16[192,768]{1,0:T(8,128)(2,1)}, u32[]{:S(2)}) copy-start(bf16[192,768]{1,0:T(8,128)(2,1)} %w_in.5) | copy-start | bytes 884740
  12.4 6.7 %collective-permute-start = (bf16[128,512]{1,0:T(8,128)(2,1)S(1)}, bf16[128,512]{1,0:T(8,128)(2,1)S(1)}, u32[]{:S(2)}, u32[]{:S(2)}) collective-permute-start(bf16[128,512]{1,0:T(8,128)(2,1)S(1)} %get-tuple-element.26), channel_id=1, source_target_pairs={{0,32},{16,48},{32,64},{48,80},{64,96},{80,112},{96,0},{112,16},{1... | collective-permute-start | bytes 393224 | tf_op jit(solution)/shard_map/ppermute | solution.py:291
  13.7 7.5 %collective-permute-start.1 = (bf16[128,512]{1,0:T(8,128)(2,1)S(1)}, bf16[128,512]{1,0:T(8,128)(2,1)S(1)}, u32[]{:S(2)}, u32[]{:S(2)}) collective-permute-start(bf16[128,512]{1,0:T(8,128)(2,1)S(1)} %get-tuple-element.27), channel_id=1, source_target_pairs={{0,64},{16,80},{32,96},{48,112},{64,0},{80,16},{96,32},{112,48},{1... | collective-permute-start | bytes 393224 | tf_op jit(solution)/shard_map/ppermute | solution.py:291
  16.2 7.3 %collective-permute-start.2 = (bf16[128,512]{1,0:T(8,128)(2,1)S(1)}, bf16[128,512]{1,0:T(8,128)(2,1)S(1)}, u32[]{:S(2)}, u32[]{:S(2)}) collective-permute-start(bf16[128,512]{1,0:T(8,128)(2,1)S(1)} %get-tuple-element.28), channel_id=1, source_target_pairs={{0,96},{16,112},{32,0},{48,16},{64,32},{80,48},{96,64},{112,80},{1... | collective-permute-start | bytes 393224 | tf_op jit(solution)/shard_map/ppermute | solution.py:291
  17.3 7.3 %collective-permute-start.3 = (bf16[128,512]{1,0:T(8,128)(2,1)S(1)}, bf16[128,512]{1,0:T(8,128)(2,1)S(1)}, u32[]{:S(2)}, u32[]{:S(2)}) collective-permute-start(bf16[128,512]{1,0:T(8,128)(2,1)S(1)} %get-tuple-element.25.refs_0_), channel_id=1, source_target_pairs={{0,16},{16,0},{32,48},{48,32},{64,80},{80,64},{96,112},{112,96},{1... | collective-permute-start | bytes 393224 | tf_op jit(solution)/shard_map/ppermute | solution.py:292
  19.1 5.5 %collective-permute-start.4 = (bf16[128,512]{1,0:T(8,128)(2,1)S(1)}, bf16[128,512]{1,0:T(8,128)(2,1)S(1)}, u32[]{:S(2)}, u32[]{:S(2)}) collective-permute-start(bf16[128,512]{1,0:T(8,128)(2,1)S(1)} %collective-permute-done.refs_1_), channel_id=1, source_target_pairs={{0,16},{16,0},{32,48},{48,32},{64,80},{80,64},{96,112},{112,96},{1... | collective-permute-start | bytes 393224 | tf_op jit(solution)/shard_map/ppermute | solution.py:292
  21.2 3.4 %collective-permute-start.5 = (bf16[128,512]{1,0:T(8,128)(2,1)S(1)}, bf16[128,512]{1,0:T(8,128)(2,1)S(1)}, u32[]{:S(2)}, u32[]{:S(2)}) collective-permute-start(bf16[128,512]{1,0:T(8,128)(2,1)S(1)} %collective-permute-done.1.refs_2_), channel_id=1, source_target_pairs={{0,16},{16,0},{32,48},{48,32},{64,80},{80,64},{96,112},{112,96},{1... | collective-permute-start | bytes 393224 | tf_op jit(solution)/shard_map/ppermute | solution.py:292
  23.4 1.3 %collective-permute-start.6 = (bf16[128,512]{1,0:T(8,128)(2,1)S(1)}, bf16[128,512]{1,0:T(8,128)(2,1)S(1)}, u32[]{:S(2)}, u32[]{:S(2)}) collective-permute-start(bf16[128,512]{1,0:T(8,128)(2,1)S(1)} %collective-permute-done.2.refs_3_), channel_id=1, source_target_pairs={{0,16},{16,0},{32,48},{48,32},{64,80},{80,64},{96,112},{112,96},{1... | collective-permute-start | bytes 393224 | tf_op jit(solution)/shard_map/ppermute | solution.py:292
  23.4 1.3 %copy-start.3 = (bf16[384,192]{0,1:T(8,128)(2,1)S(1)}, bf16[384,192]{0,1:T(8,128)(2,1)}, u32[]{:S(2)}) copy-start(bf16[384,192]{0,1:T(8,128)(2,1)} %param.10) | copy-start | bytes 442372
  78.2 18.5 %all-to-all-start.3 = ((bf16[128,16,128]{2,1,0:T(8,128)(2,1)}), bf16[128,16,128]{2,1,0:T(8,128)(2,1)S(1)}, u32[]{:S(2)}, u32[]{:S(2)}) async-start(bf16[128,16,128]{2,1,0:T(8,128)(2,1)} %shard_map.98), calls=%async_computation.3 | async-start | bytes 1048576 | tf_op jit(solution)/shard_map/all_to_all | solution.py:331
  82.7 6.6 %collective-permute-start.7 = (bf16[64,384]{1,0:T(8,128)(2,1)S(1)}, bf16[64,384]{1,0:T(8,128)(2,1)S(1)}, u32[]{:S(2)}, u32[]{:S(2)}) collective-permute-start(bf16[64,384]{1,0:T(8,128)(2,1)S(1)} %get-tuple-element.35), channel_id=1, source_target_pairs={{0,16},{16,0},{32,48},{48,32},{64,80},{80,64},{96,112},{112,96},{1... | collective-permute-start | bytes 147464 | tf_op jit(solution)/shard_map/ppermute | solution.py:286
  84.0 7.9 %collective-permute-start.8 = (bf16[64,384]{1,0:T(8,128)(2,1)S(1)}, bf16[64,384]{1,0:T(8,128)(2,1)S(1)}, u32[]{:S(2)}, u32[]{:S(2)}) collective-permute-start(bf16[64,384]{1,0:T(8,128)(2,1)S(1)} %get-tuple-element.36), channel_id=1, source_target_pairs={{0,32},{16,48},{32,64},{48,80},{64,96},{80,112},{96,0},{112,16},{1... | collective-permute-start | bytes 147464 | tf_op jit(solution)/shard_map/ppermute | solution.py:286
  84.5 9.0 %collective-permute-start.9 = (bf16[64,384]{1,0:T(8,128)(2,1)S(1)}, bf16[64,384]{1,0:T(8,128)(2,1)S(1)}, u32[]{:S(2)}, u32[]{:S(2)}) collective-permute-start(bf16[64,384]{1,0:T(8,128)(2,1)S(1)} %get-tuple-element.37), channel_id=1, source_target_pairs={{0,48},{16,32},{32,80},{48,64},{64,112},{80,96},{96,16},{112,0},{1... | collective-permute-start | bytes 147464 | tf_op jit(solution)/shard_map/ppermute | solution.py:286
  86.0 8.1 %collective-permute-start.10 = (bf16[64,384]{1,0:T(8,128)(2,1)S(1)}, bf16[64,384]{1,0:T(8,128)(2,1)S(1)}, u32[]{:S(2)}, u32[]{:S(2)}) collective-permute-start(bf16[64,384]{1,0:T(8,128)(2,1)S(1)} %get-tuple-element.38), channel_id=1, source_target_pairs={{0,64},{16,80},{32,96},{48,112},{64,0},{80,16},{96,32},{112,48},{1... | collective-permute-start | bytes 147464 | tf_op jit(solution)/shard_map/ppermute | solution.py:286
  88.1 7.6 %collective-permute-start.11 = (bf16[64,384]{1,0:T(8,128)(2,1)S(1)}, bf16[64,384]{1,0:T(8,128)(2,1)S(1)}, u32[]{:S(2)}, u32[]{:S(2)}) collective-permute-start(bf16[64,384]{1,0:T(8,128)(2,1)S(1)} %get-tuple-element.39), channel_id=1, source_target_pairs={{0,80},{16,64},{32,112},{48,96},{64,16},{80,0},{96,48},{112,32},{1... | collective-permute-start | bytes 147464 | tf_op jit(solution)/shard_map/ppermute | solution.py:286
  89.2 6.4 %collective-permute-start.12 = (bf16[64,384]{1,0:T(8,128)(2,1)S(1)}, bf16[64,384]{1,0:T(8,128)(2,1)S(1)}, u32[]{:S(2)}, u32[]{:S(2)}) collective-permute-start(bf16[64,384]{1,0:T(8,128)(2,1)S(1)} %get-tuple-element.40), channel_id=1, source_target_pairs={{0,96},{16,112},{32,0},{48,16},{64,32},{80,48},{96,64},{112,80},{1... | collective-permute-start | bytes 147464 | tf_op jit(solution)/shard_map/ppermute | solution.py:286
  91.9 4.0 %collective-permute-start.13 = (bf16[64,384]{1,0:T(8,128)(2,1)S(1)}, bf16[64,384]{1,0:T(8,128)(2,1)S(1)}, u32[]{:S(2)}, u32[]{:S(2)}) collective-permute-start(bf16[64,384]{1,0:T(8,128)(2,1)S(1)} %get-tuple-element.41), channel_id=1, source_target_pairs={{0,112},{16,96},{32,16},{48,0},{64,48},{80,32},{96,80},{112,64},{1... | collective-permute-start | bytes 147464 | tf_op jit(solution)/shard_map/ppermute | solution.py:286

commit v4 on v3

--- a/solution.py
+++ b/solution.py
@@ -30,12 +30,16 @@
     return lax.dot_general(a, b, (((0,), (0,)), ((), ())), preferred_element_type=F32)
 
 
+def column_of(place):
+    return (place % 8) * 32 + place // 8
+
+
 HALVES = (slice(0, GROUP), slice(GROUP, TOK))
 
 
 def prepare_scan(aux, by_row, forward):
     token = iota((TOK, 128), 0)
-    chunk = token // 64 if by_row else (token // GROUP) * 4 + token % 4
+    chunk = (token // GROUP) * 4 + (token % 8) // 2 if by_row else token // 64
     member = (iota((TOK, 128), 1) // 16 == chunk).astype(F32)
     lane = iota((256, 640), 1)
     wanted = jnp.where(lane < 128, 192 + lane % 16, 208 + lane % 16)
@@ -45,7 +49,9 @@
     c_part = (spread[:, 128:256] * member).astype(BF)
     log_step = spread[:, 256:].astype(BF)
     here, there = iota((GROUP, GROUP), 0), iota((GROUP, GROUP), 1)
-    same = (here // 64 == there // 64) if by_row else (here % 4 == there % 4)
+    if by_row:
+        here, there = column_of(here), column_of(there)
+    same = here // 64 == there // 64
     if forward:
         order, counted, src, out = there <= here, there <= here, b_part, c_part
     else:
@@ -67,7 +73,7 @@
     if by_row:
         steps = [(k, k + 1) for k in range(7)] if forward else [(k, k - 1) for k in range(7, 0, -1)]
     else:
-        steps = [(j, j + 4) for j in range(4)] if forward else [(j + 4, j) for j in range(4)]
+        steps = [(2 * j, 2 * j + 1) if forward else (2 * j + 1, 2 * j) for j in range(4)]
     for old, new in steps:
         carried[new] = part(decay, old) * (carried[old] + part(states, old))
     coming = jnp.concatenate(carried, axis=0).astype(BF)
@@ -79,13 +85,25 @@
     return apply_scan(prepare_scan(aux, by_row, forward), values, by_row, forward)
 
 
-def to_columns(scratch, slot, token_rows):
-    for l in range(CHAN // 128):
+def lane_tile(l):
+    return slice(128 * l, 128 * l + 128)
+
+
+def row_places():
+    for g in range(2):
         for r in range(8):
             for j in range(4):
-                scratch[l, pl.ds(r * 128 + slot + j, 16, stride=8), :] = token_rows[
-                    l, pl.ds(4 * r + j, 16, stride=32), :
-                ]
+                yield g * GROUP + (r * 4 + j) * 8, (r * 16 + g * 8) * 8 + j
+
+
+def to_columns(scratch, value):
+    for l in range(CHAN // 128):
+        for place, row in row_places():
+            scratch[l, pl.ds(row, 8, stride=8), :] = value[place : place + 8, lane_tile(l)]
+
+
+def by_column(scratch, l):
+    return jnp.concatenate([scratch[l, pl.ds(j, 128, stride=8), :] for j in range(4)], axis=0)
 
 
 def split_lanes(ref, value):
@@ -119,7 +137,7 @@
 
 def pack_columns_kernel(place, feat, cot, sel, log, *outs):
     slot = iota((TOK, 1), 0)
-    row, j = (slot % 64) // 4, slot % 4
+    row, j = slot % 16, (slot % 64) // 16
     dest = peers(place, slot // 64)
     choose = ((row * 32 + 4 * dest + j) == iota((TOK, TOK), 1)).astype(F32).astype(BF)
     left = mm(choose, feat[:, 0:128]).astype(BF)
@@ -133,8 +151,11 @@
         outs[k][:, 256 + MODEL :] = jnp.zeros((128, 64), BF)
 
 
-def row_forward_kernel(packed, w_in, out):
-    aux = packed[...]
+def row_forward_kernel(packed, w_in, out, turned):
+    move = (column_of(iota((GROUP, GROUP), 0)) == iota((GROUP, GROUP), 1)).astype(F32).astype(BF)
+    for h in HALVES:
+        turned[h, :] = mm(move, packed[h, :]).astype(BF)
+    aux = turned[...]
     values = mm(aux[:, :MODEL], w_in[:, :CHAN]).astype(BF).astype(F32)
     out[...] = scan_tokens(aux, values, True, True).astype(BF)
 
@@ -151,32 +172,37 @@
 
 
 def col_adjoint_kernel(place, row_out, w_in, w_out, *refs):
-    pieces, (out, whole, tokens, scratch) = refs[:8], refs[8:]
+    pieces, (out, whole, scratch) = refs[:8], refs[8:]
     for k in range(8):
         half, first = k % 2, 64 * (k % 2)
-        rows = pl.ds(pl.multiple_of(sender(place, k) * 64, 64), 64)
-        whole[rows, :] = pieces[4 * half + k // 2][first : first + 64, :]
+        source = sender(place, k)
+        for j in range(4):
+            rows = pl.ds(pl.multiple_of(128 * j + source * 16, 16), 16)
+            whole[rows, :] = pieces[4 * half + k // 2][first + 16 * j : first + 16 * j + 16, :]
     aux = whole[:, :256]
     cot = whole[:, 256 : 256 + MODEL]
     gate, sig, hidden_grad = gate_terms(aux, cot, w_in, w_out)
     col_grad = (hidden_grad * gate * sig).astype(BF).astype(F32)
     row_grad = scan_tokens(aux, col_grad, False, False)
-    split_lanes(tokens, row_out[...].astype(F32))
-    to_columns(scratch, 0, tokens)
-    split_lanes(tokens, row_grad)
+    to_columns(scratch, row_out[...].astype(F32))
     for l in range(3):
         for j in range(4):
-            scratch[l, pl.ds(4 + j, 128, stride=8), :] = tokens[l, pl.ds(j, 128, stride=4), :]
-    for l in range(3):
-        out[:, 128 * l : 128 * l + 128] = scratch[l].astype(BF)
-
-
-def second_kernel(came, whole, packed, w_in, w_out, block, partial, out, tokens, scratch):
+            rows = slice(128 * j, 128 * j + 128)
+            scratch[l, pl.ds(4 + j, 128, stride=8), :] = row_grad[rows, lane_tile(l)]
+    for l in range(3):
+        out[:, lane_tile(l)] = scratch[l].astype(BF)
+
+
+def second_kernel(came, whole, packed, w_in, w_out, block, partial, out, scratch):
     split_lanes(scratch, came[...].astype(F32))
-    for l in range(3):
-        for j in range(4):
-            tokens[l, pl.ds(j, 128, stride=4), :] = scratch[l, pl.ds(j, 128, stride=8), :]
-    row_out = jnp.concatenate([tokens[l] for l in range(3)], axis=1)
+    row_out = jnp.concatenate([by_column(scratch, l) for l in range(3)], axis=1)
+    row_grad = [
+        jnp.concatenate(
+            [scratch[l, pl.ds(row + 4, 8, stride=8), :] for _, row in row_places()], axis=0
+        )
+        for l in range(3)
+    ]
+    row_grad = jnp.concatenate(row_grad, axis=1)
     feat = whole[:, :MODEL]
     cot = whole[:, 256 : 256 + MODEL]
     col_out = scan_tokens(whole[:, :256], row_out, False, True).astype(BF).astype(F32)
@@ -189,20 +215,12 @@
     out_part = t_mm(hidden, shifted)
     gate_part = t_mm(feat, gate_grad)
 
-    for l in range(3):
-        for r in range(8):
-            for j in range(4):
-                tokens[l, pl.ds(4 * r + j, 16, stride=32), :] = scratch[
-                    l, pl.ds(r * 128 + 4 + j, 16, stride=8), :
-                ]
-    row_grad = jnp.concatenate([tokens[l] for l in range(3)], axis=1)
     value_grad = scan_tokens(packed[...], row_grad, True, False).astype(BF)
     pull = mm_t(value_grad, w_in[:, :CHAN])
     pull = jnp.concatenate([pull, jnp.zeros((TOK, MODEL), F32)], axis=1)
     value_part = t_mm(packed[:, :MODEL], value_grad)
 
-    split_lanes(tokens, pull)
-    to_columns(scratch, 0, tokens)
+    to_columns(scratch, pull)
     in_part = jnp.concatenate([value_part, gate_part], axis=0)
     for l in range(3):
         lanes = slice(128 * l, 128 * l + 128)
@@ -226,21 +244,20 @@
 
 
 def return_kernel(place, came, partial, block, *refs):
-    outs, (scratch, grad, whole) = refs[:8], refs[8:]
+    outs, (scratch, whole) = refs[:8], refs[8:]
     for l in range(2):
         scratch[l] = came[:, :, 128 * l : 128 * l + 128].astype(F32).reshape(1024, 128)
-    for l in range(2):
-        for j in range(4):
-            grad[l, pl.ds(j, 128, stride=4), :] = scratch[l, pl.ds(j, 128, stride=8), :]
-    pull = jnp.concatenate([grad[0], grad[1][:, :64]], axis=1)
+    pull = jnp.concatenate([by_column(scratch, 0), by_column(scratch, 1)[:, :64]], axis=1)
     whole[...] = jnp.concatenate([block[...], partial[...] + pull], axis=1).astype(BF)
     for k in range(8):
-        rows = pl.ds(pl.multiple_of(peers(place, k) * 64, 64), 64)
-        outs[k][...] = whole[rows, :]
+        dest = peers(place, k)
+        for j in range(4):
+            rows = pl.ds(pl.multiple_of(128 * j + dest * 16, 16), 16)
+            outs[k][16 * j : 16 * j + 16, :] = whole[rows, :]
 
 
 def last_kernel(place, sums, *refs):
-    pieces, (block, grad, in_grad, out_grad, part, whole, weights) = refs[:8], refs[8:]
+    pieces, (block, grad, in_grad, out_grad, whole, weights) = refs[:8], refs[8:]
     weights[...] = sums[...].astype(F32)
     strided = lambda first: weights[pl.ds(first, 128, stride=16), :]
     for l in range(3):
@@ -257,10 +274,11 @@
         out_grad[64:192, lanes] = strided(10 + 2 * k).T
     for k in range(8):
         first = 4 * sender(place, k)
-        split_lanes(part.at[k], pieces[k][...].astype(F32))
+        value = pieces[k][...].astype(F32)
         for l in range(3):
             for j in range(4):
-                whole[l, pl.ds(first + j, 16, stride=32), :] = part[k, l, pl.ds(j, 16, stride=4), :]
+                rows = slice(16 * j, 16 * j + 16)
+                whole[l, pl.ds(first + j, 16, stride=32), :] = value[rows, lane_tile(l)]
     middle = whole[1]
     block[...] = jnp.concatenate([whole[0], middle[:, :64]], axis=1).astype(BF)
     grad[...] = jnp.concatenate([middle[:, 64:], whole[2]], axis=1).astype(BF)
@@ -299,7 +317,6 @@
     sel = selectors.transpose(0, 2, 3, 1).reshape(16, 64, 32)
     log = log_decay.transpose(0, 3, 2, 1)
     wide = ((3, 1024, 128), F32)
-    tall = ((3, TOK, 128), F32)
     (row_packed,) = call(
         pack_rows_kernel, [((TOK, 256), BF)], [feat, sel, log], vmem=60 * 1024 * 1024
     )
@@ -310,21 +327,24 @@
         [place, feat, cotangent.reshape(TOK, MODEL), sel, log],
     )
     pieces = swap_rows_in_steps(pieces)
-    (row_out,) = call(
-        row_forward_kernel, [((TOK, CHAN), BF)], [row_packed, in_weight], flops=3 * 10**10
+    row_out, row_packed = call(
+        row_forward_kernel,
+        [((TOK, CHAN), BF), ((TOK, 256), BF)],
+        [row_packed, in_weight],
+        flops=3 * 10**10,
     )
     sent, whole = call(
         col_adjoint_kernel,
         [((1024, CHAN), BF), ((TOK, 512), BF)],
         [place, row_out, in_weight, out_turned, *pieces],
-        [tall, wide],
+        [wide],
     )
     came = lax.all_to_all(sent.reshape(128, 8, CHAN), ("row", "col"), 0, 0)
     block, partial, sent = call(
         second_kernel,
         [((TOK, MODEL), F32), ((TOK, MODEL), F32), ((1024, CHAN), BF)],
         [came.reshape(1024, CHAN), whole, row_packed, in_weight, out_turned],
-        [tall, wide],
+        [wide],
     )
     came = lax.all_to_all(sent.reshape(128, 8, CHAN), ("row", "col"), 0, 0)
     (sums,) = call(sum_kernel, [((128, 16, 128), BF)], [came])
@@ -333,13 +353,13 @@
         return_kernel,
         [((64, CHAN), BF)] * 8,
         [place, came, partial, block],
-        [((2, 1024, 128), F32), ((2, TOK, 128), F32), ((TOK, CHAN), BF)],
+        [((2, 1024, 128), F32), ((TOK, CHAN), BF)],
     )
     block, grad, in_grad, out_grad = call(
         last_kernel,
         [((TOK, MODEL), BF)] * 2 + [((MODEL, 2 * CHAN), F32), ((MODEL, CHAN), F32)],
         [place, sums, *swap_rows(pieces)],
-        [((8, 3, 64, 128), F32), tall, ((2048, 128), F32)],
+        [((3, TOK, 128), F32), ((2048, 128), F32)],
     )
     return (block.reshape(16, 32, MODEL), grad.reshape(16, 32, MODEL), in_grad, out_grad.T)
 

time: 99.1 us -> 97.7 us (0.986)
  Pallas kernels: 14.5 us -> 13 us
    pallas_call x8, Pallas kernels: 14.5 us -> 13 us  [call(): pl.pallas_call(kernel, out_shape=[jax.ShapeDtypeStruct(shape, dtype) for...]
  transfers between devices with their start and end apart: 16 -> 16, of which waited for: 7 -> 6; matrix products, arithmetic and copies ran while one was open for 0% -> 0% of each run, Pallas kernels for 2% -> 3%
where the time goes in v4:
time: 97.7 us; the launch traced here: 97.4 us
  blocking collectives  45.5 us (47%)
  starting transfers between devices  32.6 us (33%)
  Pallas kernels  13 us (13%)
  waiting for transfers between devices  5.48 us (6%)
    all_to_all x2, blocking collectives, on_device(): came = lax.all_to_all(sent.reshape(128, 8, CHAN), ('row', 'col'), 0, 0)  45.5 us
    pallas_call x8, Pallas kernels, call(): pl.pallas_call(kernel, out_shape=[jax.ShapeDtypeStruct(shape, dtype) for...  13 us
    ppermute x7, starting transfers between devices, swap_rows(): lax.ppermute(pieces[k], 'row', pairs(k))  9.7 us
    all_to_all x1, starting transfers between devices, on_device(): lax.all_to_all(row_packed.reshape(16, 32, 256), 'col', 0, 0)  8.73 us
    ppermute x4, starting transfers between devices, swap_rows_in_steps(): lax.ppermute(piece, 'row', [(i, i ^ 1) for i in range(8)])  4.97 us
    ppermute x3, starting transfers between devices, swap_rows_in_steps(): lax.ppermute(pieces[s], 'row', along(s))  4.88 us
    all_to_all x1, starting transfers between devices, on_device(): sums = lax.all_to_all(sums, ('row', 'col'), 0, 0).reshape(2048, 128)  4.33 us
    ppermute x7, waiting for transfers between devices, swap_rows(): lax.ppermute(pieces[k], 'row', pairs(k))  3.56 us
  transfers between devices with their start and end apart: 16, of which 6 were waited for; matrix products, arithmetic and copies ran while one was open for 0% of the time, Pallas kernels for 3%

profile of v4, /device:TPU:1, one launch (start us, length us, event | category | flops | bytes accessed | tf_op | source)
XLA Modules:
  0.0 97.4 jit_solution(11891518621735024830)
XLA Ops:
  0.6 0.0 copy-start.4
  0.6 0.0 copy-start.5
  0.7 2.0 %shard_map.93 = bf16[512,256]{1,0:T(8,128)(2,1)} custom-call(bf16[512,192]{1,0:T(8,128)(2,1)} %bitcast.19, bf16[16,64,32]{2,1,0:T(8,128)(2,1)} %bitcast.21, bf16[16,6,2,32]{3,2,1,0:T(2,128)(2,1)} %bitcast.29), custom_call_target="tpu_custom_call" | custom-call | flops 100000000 | bytes 1000000 | tf_op jit(solution)/shard_map/pallas_call | solution.py:291
  2.7 8.7 %all-to-all-start = ((bf16[16,32,256]{2,1,0:T(8,128)(2,1)}), bf16[16,32,256]{2,1,0:T(8,128)(2,1)S(1)}, u32[]{:S(2)}, u32[]{:S(2)}) async-start(bf16[16,32,256]{2,1,0:T(8,128)(2,1)} %bitcast.31), calls=%async_computation | async-start | bytes 524288 | tf_op jit(solution)/shard_map/all_to_all | solution.py:323
  11.4 0.0 copy-done.4
  11.5 0.0 copy-start
  11.5 0.9 shard_map.95
  12.4 1.3 %collective-permute-start = (bf16[128,512]{1,0:T(8,128)(2,1)S(1)}, bf16[128,512]{1,0:T(8,128)(2,1)S(1)}, u32[]{:S(2)}, u32[]{:S(2)}) collective-permute-start(bf16[128,512]{1,0:T(8,128)(2,1)S(1)} %get-tuple-element.29), channel_id=1, source_target_pairs={{0,32},{16,48},{32,64},{48,80},{64,96},{80,112},{96,0},{112,16},{1... | collective-permute-start | bytes 393224 | tf_op jit(solution)/shard_map/ppermute | solution.py:309
  13.7 2.5 %collective-permute-start.1 = (bf16[128,512]{1,0:T(8,128)(2,1)S(1)}, bf16[128,512]{1,0:T(8,128)(2,1)S(1)}, u32[]{:S(2)}, u32[]{:S(2)}) collective-permute-start(bf16[128,512]{1,0:T(8,128)(2,1)S(1)} %get-tuple-element.30), channel_id=1, source_target_pairs={{0,64},{16,80},{32,96},{48,112},{64,0},{80,16},{96,32},{112,48},{1... | collective-permute-start | bytes 393224 | tf_op jit(solution)/shard_map/ppermute | solution.py:309
  16.2 1.2 %collective-permute-start.2 = (bf16[128,512]{1,0:T(8,128)(2,1)S(1)}, bf16[128,512]{1,0:T(8,128)(2,1)S(1)}, u32[]{:S(2)}, u32[]{:S(2)}) collective-permute-start(bf16[128,512]{1,0:T(8,128)(2,1)S(1)} %get-tuple-element.31), channel_id=1, source_target_pairs={{0,96},{16,112},{32,0},{48,16},{64,32},{80,48},{96,64},{112,80},{1... | collective-permute-start | bytes 393224 | tf_op jit(solution)/shard_map/ppermute | solution.py:309
  17.3 1.8 %collective-permute-start.3 = (bf16[128,512]{1,0:T(8,128)(2,1)S(1)}, bf16[128,512]{1,0:T(8,128)(2,1)S(1)}, u32[]{:S(2)}, u32[]{:S(2)}) collective-permute-start(bf16[128,512]{1,0:T(8,128)(2,1)S(1)} %get-tuple-element.28.refs_0_), channel_id=1, source_target_pairs={{0,16},{16,0},{32,48},{48,32},{64,80},{80,64},{96,112},{112,96},{1... | collective-permute-start | bytes 393224 | tf_op jit(solution)/shard_map/ppermute | solution.py:310
  19.1 0.0 collective-permute-done.refs_1_
  19.1 1.0 %collective-permute-start.4 = (bf16[128,512]{1,0:T(8,128)(2,1)S(1)}, bf16[128,512]{1,0:T(8,128)(2,1)S(1)}, u32[]{:S(2)}, u32[]{:S(2)}) collective-permute-start(bf16[128,512]{1,0:T(8,128)(2,1)S(1)} %collective-permute-done.refs_1_), channel_id=1, source_target_pairs={{0,16},{16,0},{32,48},{48,32},{64,80},{80,64},{96,112},{112,96},{1... | collective-permute-start | bytes 393224 | tf_op jit(solution)/shard_map/ppermute | solution.py:310
  20.1 1.1 %collective-permute-done.1.refs_2_ = bf16[128,512]{1,0:T(8,128)(2,1)S(1)} collective-permute-done((bf16[128,512]{1,0:T(8,128)(2,1)S(1)}, bf16[128,512]{1,0:T(8,128)(2,1)S(1)}, u32[]{:S(2)}, u32[]{:S(2)}) %collective-permute-start.1) | collective-permute-done | bytes 131104 | tf_op jit(solution)/shard_map/ppermute | solution.py:309
  21.2 2.2 %collective-permute-start.5 = (bf16[128,512]{1,0:T(8,128)(2,1)S(1)}, bf16[128,512]{1,0:T(8,128)(2,1)S(1)}, u32[]{:S(2)}, u32[]{:S(2)}) collective-permute-start(bf16[128,512]{1,0:T(8,128)(2,1)S(1)} %collective-permute-done.1.refs_2_), channel_id=1, source_target_pairs={{0,16},{16,0},{32,48},{48,32},{64,80},{80,64},{96,112},{112,96},{1... | collective-permute-start | bytes 393224 | tf_op jit(solution)/shard_map/ppermute | solution.py:310
  23.4 0.0 collective-permute-done.2.refs_3_
  23.4 0.0 collective-permute-start.6
  23.4 0.0 all-to-all-done
  23.4 0.0 copy-done
  23.4 0.0 copy-start.3
  23.4 1.3 %shard_map.94 = (bf16[512,384]{1,0:T(8,128)(2,1)S(1)}, bf16[512,256]{1,0:T(8,128)(2,1)S(1)}) custom-call(bf16[512,256]{1,0:T(8,128)(2,1)S(1)} %bitcast.28, bf16[192,768]{1,0:T(8,128)(2,1)S(1)} %copy-done), custom_call_target="tpu_custom_call" | custom-call | flops 30000001024 | bytes 1000000 | tf_op jit(solution)/shard_map/pallas_call | solution.py:291
  24.8 0.0 collective-permute-done.3.refs_4_
  24.8 0.0 collective-permute-done.4.refs_5_
  24.8 0.0 collective-permute-done.5.refs_6_
  24.8 0.0 collective-permute-done.6.refs_7_
  24.8 1.6 %shard_map.96 = (bf16[1024,384]{1,0:T(8,128)(2,1)S(1)}, bf16[512,512]{1,0:T(8,128)(2,1)S(1)}) custom-call(s32[1]{0:T(128)} %bitcast.place, bf16[512,384]{1,0:T(8,128)(2,1)S(1)} %get-tuple-element.27.row_out, bf16[192,768]{1,0:T(8,128)(2,1)S(1)} %copy-done, bf16[192,384]{1,0:T(8,128)(2,1)S(1)} %bitcast.25, bf16[128,512]{1,0:T(8,128)(2,1)S(1)} %get-tuple-element.28.refs_0_, ...), custom_call_target="tpu_custom_call" | custom-call | flops 100000000 | bytes 1000000 | tf_op jit(solution)/shard_map/pallas_call | solution.py:291
  26.5 25.1 %all_to_all.20 = bf16[128,8,384]{2,1,0:T(8,128)(2,1)S(1)} all-to-all(bf16[128,8,384]{2,1,0:T(8,128)(2,1)S(1)} %bitcast.23), channel_id=1, replica_groups=mesh['row'=8,'col'=16] {'row','col'}, dimensions={0} | all-to-all | bytes 1572864 | tf_op jit(solution)/shard_map/all_to_all | solution.py:342
  51.6 3.7 %shard_map.97 = (f32[512,192]{1,0:T(8,128)S(1)}, f32[512,192]{1,0:T(8,128)S(1)}, bf16[1024,384]{1,0:T(8,128)(2,1)S(1)}) custom-call(bf16[1024,384]{1,0:T(8,128)(2,1)S(1)} %bitcast.17, bf16[512,512]{1,0:T(8,128)(2,1)S(1)} %get-tuple-element.33.whole, bf16[512,256]{1,0:T(8,128)(2,1)S(1)} %get-tuple-element.34.packed, bf16[192,768]{1,0:T(8,128)(2,1)S(1)} %copy-done, ...), custom_call_target="tpu_custom_call" | custom-call | flops 100000000 | bytes 1000000 | tf_op jit(solution)/shard_map/pallas_call | solution.py:291
  55.3 20.4 %all_to_all.21.came = bf16[128,8,384]{2,1,0:T(8,128)(2,1)S(1)} all-to-all(bf16[128,8,384]{2,1,0:T(8,128)(2,1)S(1)} %bitcast.24), channel_id=1, replica_groups=mesh['row'=8,'col'=16] {'row','col'}, dimensions={0} | all-to-all | bytes 1572864 | tf_op jit(solution)/shard_map/all_to_all | solution.py:349
  75.6 1.0 shard_map.98
  76.6 4.3 %all-to-all-start.3 = ((bf16[128,16,128]{2,1,0:T(8,128)(2,1)}), bf16[128,16,128]{2,1,0:T(8,128)(2,1)S(1)}, u32[]{:S(2)}, u32[]{:S(2)}) async-start(bf16[128,16,128]{2,1,0:T(8,128)(2,1)} %shard_map.98), calls=%async_computation.3 | async-start | bytes 1048576 | tf_op jit(solution)/shard_map/all_to_all | solution.py:351
  81.0 0.3 shard_map.99
  81.3 1.3 %collective-permute-start.7 = (bf16[64,384]{1,0:T(8,128)(2,1)S(1)}, bf16[64,384]{1,0:T(8,128)(2,1)S(1)}, u32[]{:S(2)}, u32[]{:S(2)}) collective-permute-start(bf16[64,384]{1,0:T(8,128)(2,1)S(1)} %get-tuple-element.39), channel_id=1, source_target_pairs={{0,16},{16,0},{32,48},{48,32},{64,80},{80,64},{96,112},{112,96},{1... | collective-permute-start | bytes 147464 | tf_op jit(solution)/shard_map/ppermute | solution.py:304
  82.5 0.5 collective-permute-start.8
  83.1 1.5 %collective-permute-start.9 = (bf16[64,384]{1,0:T(8,128)(2,1)S(1)}, bf16[64,384]{1,0:T(8,128)(2,1)S(1)}, u32[]{:S(2)}, u32[]{:S(2)}) collective-permute-start(bf16[64,384]{1,0:T(8,128)(2,1)S(1)} %get-tuple-element.41), channel_id=1, source_target_pairs={{0,48},{16,32},{32,80},{48,64},{64,112},{80,96},{96,16},{112,0},{1... | collective-permute-start | bytes 147464 | tf_op jit(solution)/shard_map/ppermute | solution.py:304
  84.6 2.0 %collective-permute-start.10 = (bf16[64,384]{1,0:T(8,128)(2,1)S(1)}, bf16[64,384]{1,0:T(8,128)(2,1)S(1)}, u32[]{:S(2)}, u32[]{:S(2)}) collective-permute-start(bf16[64,384]{1,0:T(8,128)(2,1)S(1)} %get-tuple-element.42), channel_id=1, source_target_pairs={{0,64},{16,80},{32,96},{48,112},{64,0},{80,16},{96,32},{112,48},{1... | collective-permute-start | bytes 147464 | tf_op jit(solution)/shard_map/ppermute | solution.py:304
  86.7 1.2 %collective-permute-start.11 = (bf16[64,384]{1,0:T(8,128)(2,1)S(1)}, bf16[64,384]{1,0:T(8,128)(2,1)S(1)}, u32[]{:S(2)}, u32[]{:S(2)}) collective-permute-start(bf16[64,384]{1,0:T(8,128)(2,1)S(1)} %get-tuple-element.43), channel_id=1, source_target_pairs={{0,80},{16,64},{32,112},{48,96},{64,16},{80,0},{96,48},{112,32},{1... | collective-permute-start | bytes 147464 | tf_op jit(solution)/shard_map/ppermute | solution.py:304
  87.8 0.0 collective-permute-done.7.refs_1_
  87.8 1.5 %collective-permute-start.12 = (bf16[64,384]{1,0:T(8,128)(2,1)S(1)}, bf16[64,384]{1,0:T(8,128)(2,1)S(1)}, u32[]{:S(2)}, u32[]{:S(2)}) collective-permute-start(bf16[64,384]{1,0:T(8,128)(2,1)S(1)} %get-tuple-element.44), channel_id=1, source_target_pairs={{0,96},{16,112},{32,0},{48,16},{64,32},{80,48},{96,64},{112,80},{1... | collective-permute-start | bytes 147464 | tf_op jit(solution)/shard_map/ppermute | solution.py:304
  89.3 1.2 %collective-permute-done.8.refs_2_ = bf16[64,384]{1,0:T(8,128)(2,1)S(1)} collective-permute-done((bf16[64,384]{1,0:T(8,128)(2,1)S(1)}, bf16[64,384]{1,0:T(8,128)(2,1)S(1)}, u32[]{:S(2)}, u32[]{:S(2)}) %collective-permute-start.8) | collective-permute-done | bytes 49184 | tf_op jit(solution)/shard_map/ppermute | solution.py:304
  90.5 1.7 %collective-permute-start.13 = (bf16[64,384]{1,0:T(8,128)(2,1)S(1)}, bf16[64,384]{1,0:T(8,128)(2,1)S(1)}, u32[]{:S(2)}, u32[]{:S(2)}) collective-permute-start(bf16[64,384]{1,0:T(8,128)(2,1)S(1)} %get-tuple-element.45), channel_id=1, source_target_pairs={{0,112},{16,96},{32,16},{48,0},{64,48},{80,32},{96,80},{112,64},{1... | collective-permute-start | bytes 147464 | tf_op jit(solution)/shard_map/ppermute | solution.py:304
  92.2 0.0 collective-permute-done.9.refs_3_
  92.2 0.6 collective-permute-done.10.refs_4_
  92.8 1.5 %collective-permute-done.11.refs_5_ = bf16[64,384]{1,0:T(8,128)(2,1)S(1)} collective-permute-done((bf16[64,384]{1,0:T(8,128)(2,1)S(1)}, bf16[64,384]{1,0:T(8,128)(2,1)S(1)}, u32[]{:S(2)}, u32[]{:S(2)}) %collective-permute-start.11) | collective-permute-done | bytes 49184 | tf_op jit(solution)/shard_map/ppermute | solution.py:304
  94.3 0.0 collective-permute-done.12.refs_6_
  94.3 0.2 collective-permute-done.13.refs_7_
  94.5 0.8 all-to-all-done.3
  95.3 2.1 %shard_map.100 = (bf16[512,192]{1,0:T(8,128)(2,1)}, bf16[512,192]{1,0:T(8,128)(2,1)}, f32[192,768]{1,0:T(8,128)}, f32[192,384]{1,0:T(8,128)}) custom-call(s32[1]{0:T(128)} %bitcast.place, bf16[2048,128]{1,0:T(8,128)(2,1)S(1)} %bitcast.18, bf16[64,384]{1,0:T(8,128)(2,1)S(1)} %get-tuple-element.38.refs_0_, bf16[64,384]{1,0:T(8,128)(2,1)S(1)} %collective-permute-done.7.refs_1_, ...), custom_call_target="tpu_custom_call" | custom-call | flops 100000000 | bytes 1000000 | tf_op jit(solution)/shard_map/pallas_call | solution.py:291
  (6 shorter events, 0.0 us)
Async XLA Ops:
  0.6 10.8 %copy-start.4 = (bf16[16,32,192]{2,1,0:T(8,128)(2,1)S(1)}, bf16[16,32,192]{2,1,0:T(8,128)(2,1)}, u32[]{:S(2)}) copy-start(bf16[16,32,192]{2,1,0:T(8,128)(2,1)} %param.11) | copy-start | bytes 589828
  0.6 10.8 %copy-start.5 = (bf16[16,32,2,6]{1,2,3,0:T(2,128)(2,1)S(1)}, bf16[16,32,2,6]{1,2,3,0:T(2,128)(2,1)}, u32[]{:S(2)}) copy-start(bf16[16,32,2,6]{1,2,3,0:T(2,128)(2,1)} %param.8) | copy-start | bytes 36868
  2.7 8.8 %copy-start.1 = (bf16[16,32,192]{2,1,0:T(8,128)(2,1)S(1)}, bf16[16,32,192]{2,1,0:T(8,128)(2,1)}, u32[]{:S(2)}) copy-start(bf16[16,32,192]{2,1,0:T(8,128)(2,1)} %param.6) | copy-start | bytes 589828
  2.7 8.8 %copy-start.2 = (bf16[16,32,4,16]{1,3,2,0:T(8,128)(2,1)S(1)}, bf16[16,32,4,16]{1,3,2,0:T(8,128)(2,1)}, u32[]{:S(2)}) copy-start(bf16[16,32,4,16]{1,3,2,0:T(8,128)(2,1)} %param.7) | copy-start | bytes 196612
  2.7 20.7 %all-to-all-start = ((bf16[16,32,256]{2,1,0:T(8,128)(2,1)}), bf16[16,32,256]{2,1,0:T(8,128)(2,1)S(1)}, u32[]{:S(2)}, u32[]{:S(2)}) async-start(bf16[16,32,256]{2,1,0:T(8,128)(2,1)} %bitcast.31), calls=%async_computation | async-start | bytes 524288 | tf_op jit(solution)/shard_map/all_to_all | solution.py:323
  11.5 12.0 %copy-start = (bf16[192,768]{1,0:T(8,128)(2,1)S(1)}, bf16[192,768]{1,0:T(8,128)(2,1)}, u32[]{:S(2)}) copy-start(bf16[192,768]{1,0:T(8,128)(2,1)} %w_in.5) | copy-start | bytes 884740
  12.4 6.7 %collective-permute-start = (bf16[128,512]{1,0:T(8,128)(2,1)S(1)}, bf16[128,512]{1,0:T(8,128)(2,1)S(1)}, u32[]{:S(2)}, u32[]{:S(2)}) collective-permute-start(bf16[128,512]{1,0:T(8,128)(2,1)S(1)} %get-tuple-element.29), channel_id=1, source_target_pairs={{0,32},{16,48},{32,64},{48,80},{64,96},{80,112},{96,0},{112,16},{1... | collective-permute-start | bytes 393224 | tf_op jit(solution)/shard_map/ppermute | solution.py:309
  13.7 7.5 %collective-permute-start.1 = (bf16[128,512]{1,0:T(8,128)(2,1)S(1)}, bf16[128,512]{1,0:T(8,128)(2,1)S(1)}, u32[]{:S(2)}, u32[]{:S(2)}) collective-permute-start(bf16[128,512]{1,0:T(8,128)(2,1)S(1)} %get-tuple-element.30), channel_id=1, source_target_pairs={{0,64},{16,80},{32,96},{48,112},{64,0},{80,16},{96,32},{112,48},{1... | collective-permute-start | bytes 393224 | tf_op jit(solution)/shard_map/ppermute | solution.py:309
  16.2 7.3 %collective-permute-start.2 = (bf16[128,512]{1,0:T(8,128)(2,1)S(1)}, bf16[128,512]{1,0:T(8,128)(2,1)S(1)}, u32[]{:S(2)}, u32[]{:S(2)}) collective-permute-start(bf16[128,512]{1,0:T(8,128)(2,1)S(1)} %get-tuple-element.31), channel_id=1, source_target_pairs={{0,96},{16,112},{32,0},{48,16},{64,32},{80,48},{96,64},{112,80},{1... | collective-permute-start | bytes 393224 | tf_op jit(solution)/shard_map/ppermute | solution.py:309
  17.3 7.5 %collective-permute-start.3 = (bf16[128,512]{1,0:T(8,128)(2,1)S(1)}, bf16[128,512]{1,0:T(8,128)(2,1)S(1)}, u32[]{:S(2)}, u32[]{:S(2)}) collective-permute-start(bf16[128,512]{1,0:T(8,128)(2,1)S(1)} %get-tuple-element.28.refs_0_), channel_id=1, source_target_pairs={{0,16},{16,0},{32,48},{48,32},{64,80},{80,64},{96,112},{112,96},{1... | collective-permute-start | bytes 393224 | tf_op jit(solution)/shard_map/ppermute | solution.py:310
  19.1 5.7 %collective-permute-start.4 = (bf16[128,512]{1,0:T(8,128)(2,1)S(1)}, bf16[128,512]{1,0:T(8,128)(2,1)S(1)}, u32[]{:S(2)}, u32[]{:S(2)}) collective-permute-start(bf16[128,512]{1,0:T(8,128)(2,1)S(1)} %collective-permute-done.refs_1_), channel_id=1, source_target_pairs={{0,16},{16,0},{32,48},{48,32},{64,80},{80,64},{96,112},{112,96},{1... | collective-permute-start | bytes 393224 | tf_op jit(solution)/shard_map/ppermute | solution.py:310
  21.2 3.5 %collective-permute-start.5 = (bf16[128,512]{1,0:T(8,128)(2,1)S(1)}, bf16[128,512]{1,0:T(8,128)(2,1)S(1)}, u32[]{:S(2)}, u32[]{:S(2)}) collective-permute-start(bf16[128,512]{1,0:T(8,128)(2,1)S(1)} %collective-permute-done.1.refs_2_), channel_id=1, source_target_pairs={{0,16},{16,0},{32,48},{48,32},{64,80},{80,64},{96,112},{112,96},{1... | collective-permute-start | bytes 393224 | tf_op jit(solution)/shard_map/ppermute | solution.py:310
  23.4 1.4 %collective-permute-start.6 = (bf16[128,512]{1,0:T(8,128)(2,1)S(1)}, bf16[128,512]{1,0:T(8,128)(2,1)S(1)}, u32[]{:S(2)}, u32[]{:S(2)}) collective-permute-start(bf16[128,512]{1,0:T(8,128)(2,1)S(1)} %collective-permute-done.2.refs_3_), channel_id=1, source_target_pairs={{0,16},{16,0},{32,48},{48,32},{64,80},{80,64},{96,112},{112,96},{1... | collective-permute-start | bytes 393224 | tf_op jit(solution)/shard_map/ppermute | solution.py:310
  23.4 1.4 %copy-start.3 = (bf16[384,192]{0,1:T(8,128)(2,1)S(1)}, bf16[384,192]{0,1:T(8,128)(2,1)}, u32[]{:S(2)}) copy-start(bf16[384,192]{0,1:T(8,128)(2,1)} %param.10) | copy-start | bytes 442372
  76.6 18.7 %all-to-all-start.3 = ((bf16[128,16,128]{2,1,0:T(8,128)(2,1)}), bf16[128,16,128]{2,1,0:T(8,128)(2,1)S(1)}, u32[]{:S(2)}, u32[]{:S(2)}) async-start(bf16[128,16,128]{2,1,0:T(8,128)(2,1)} %shard_map.98), calls=%async_computation.3 | async-start | bytes 1048576 | tf_op jit(solution)/shard_map/all_to_all | solution.py:351
  81.3 6.6 %collective-permute-start.7 = (bf16[64,384]{1,0:T(8,128)(2,1)S(1)}, bf16[64,384]{1,0:T(8,128)(2,1)S(1)}, u32[]{:S(2)}, u32[]{:S(2)}) collective-permute-start(bf16[64,384]{1,0:T(8,128)(2,1)S(1)} %get-tuple-element.39), channel_id=1, source_target_pairs={{0,16},{16,0},{32,48},{48,32},{64,80},{80,64},{96,112},{112,96},{1... | collective-permute-start | bytes 147464 | tf_op jit(solution)/shard_map/ppermute | solution.py:304
  82.5 8.0 %collective-permute-start.8 = (bf16[64,384]{1,0:T(8,128)(2,1)S(1)}, bf16[64,384]{1,0:T(8,128)(2,1)S(1)}, u32[]{:S(2)}, u32[]{:S(2)}) collective-permute-start(bf16[64,384]{1,0:T(8,128)(2,1)S(1)} %get-tuple-element.40), channel_id=1, source_target_pairs={{0,32},{16,48},{32,64},{48,80},{64,96},{80,112},{96,0},{112,16},{1... | collective-permute-start | bytes 147464 | tf_op jit(solution)/shard_map/ppermute | solution.py:304
  83.1 9.1 %collective-permute-start.9 = (bf16[64,384]{1,0:T(8,128)(2,1)S(1)}, bf16[64,384]{1,0:T(8,128)(2,1)S(1)}, u32[]{:S(2)}, u32[]{:S(2)}) collective-permute-start(bf16[64,384]{1,0:T(8,128)(2,1)S(1)} %get-tuple-element.41), channel_id=1, source_target_pairs={{0,48},{16,32},{32,80},{48,64},{64,112},{80,96},{96,16},{112,0},{1... | collective-permute-start | bytes 147464 | tf_op jit(solution)/shard_map/ppermute | solution.py:304
  84.6 8.1 %collective-permute-start.10 = (bf16[64,384]{1,0:T(8,128)(2,1)S(1)}, bf16[64,384]{1,0:T(8,128)(2,1)S(1)}, u32[]{:S(2)}, u32[]{:S(2)}) collective-permute-start(bf16[64,384]{1,0:T(8,128)(2,1)S(1)} %get-tuple-element.42), channel_id=1, source_target_pairs={{0,64},{16,80},{32,96},{48,112},{64,0},{80,16},{96,32},{112,48},{1... | collective-permute-start | bytes 147464 | tf_op jit(solution)/shard_map/ppermute | solution.py:304
  86.7 7.6 %collective-permute-start.11 = (bf16[64,384]{1,0:T(8,128)(2,1)S(1)}, bf16[64,384]{1,0:T(8,128)(2,1)S(1)}, u32[]{:S(2)}, u32[]{:S(2)}) collective-permute-start(bf16[64,384]{1,0:T(8,128)(2,1)S(1)} %get-tuple-element.43), channel_id=1, source_target_pairs={{0,80},{16,64},{32,112},{48,96},{64,16},{80,0},{96,48},{112,32},{1... | collective-permute-start | bytes 147464 | tf_op jit(solution)/shard_map/ppermute | solution.py:304
  87.8 6.5 %collective-permute-start.12 = (bf16[64,384]{1,0:T(8,128)(2,1)S(1)}, bf16[64,384]{1,0:T(8,128)(2,1)S(1)}, u32[]{:S(2)}, u32[]{:S(2)}) collective-permute-start(bf16[64,384]{1,0:T(8,128)(2,1)S(1)} %get-tuple-element.44), channel_id=1, source_target_pairs={{0,96},{16,112},{32,0},{48,16},{64,32},{80,48},{96,64},{112,80},{1... | collective-permute-start | bytes 147464 | tf_op jit(solution)/shard_map/ppermute | solution.py:304
  90.5 4.0 %collective-permute-start.13 = (bf16[64,384]{1,0:T(8,128)(2,1)S(1)}, bf16[64,384]{1,0:T(8,128)(2,1)S(1)}, u32[]{:S(2)}, u32[]{:S(2)}) collective-permute-start(bf16[64,384]{1,0:T(8,128)(2,1)S(1)} %get-tuple-element.45), channel_id=1, source_target_pairs={{0,112},{16,96},{32,16},{48,0},{64,48},{80,32},{96,80},{112,64},{1... | collective-permute-start | bytes 147464 | tf_op jit(solution)/shard_map/ppermute | solution.py:304

commit v5 on v4

--- a/solution.py
+++ b/solution.py
@@ -256,6 +256,9 @@
             outs[k][16 * j : 16 * j + 16, :] = whole[rows, :]
 
 
+SENT = (0, 4, 5, 2, 3, 6, 7, 1)
+
+
 def last_kernel(place, sums, *refs):
     pieces, (block, grad, in_grad, out_grad, whole, weights) = refs[:8], refs[8:]
     weights[...] = sums[...].astype(F32)
@@ -274,7 +277,7 @@
         out_grad[64:192, lanes] = strided(10 + 2 * k).T
     for k in range(8):
         first = 4 * sender(place, k)
-        value = pieces[k][...].astype(F32)
+        value = pieces[SENT.index(k)][...].astype(F32)
         for l in range(3):
             for j in range(4):
                 rows = slice(16 * j, 16 * j + 16)
@@ -301,7 +304,10 @@
 
 def swap_rows(pieces):
     pairs = lambda k: [(i, ((i // 2 + k // 2) % 4) * 2 + (i + k) % 2) for i in range(8)]
-    return [pieces[0]] + [lax.ppermute(pieces[k], "row", pairs(k)) for k in range(1, 8)]
+    came = {0: pieces[0]}
+    for k in SENT[1:]:
+        came[k] = lax.ppermute(pieces[k], "row", pairs(k))
+    return [came[k] for k in SENT]
 
 
 def swap_rows_in_steps(pieces):

time: 97.7 us -> 97.9 us (level)
  no operation moved by 1% of the time
where the time goes in v5:
time: 97.9 us; the launch traced here: 97.6 us
  blocking collectives  45.5 us (46%)
  starting transfers between devices  32.7 us (33%)
  Pallas kernels  13 us (13%)
  waiting for transfers between devices  5.55 us (6%)
    all_to_all x2, blocking collectives, on_device(): came = lax.all_to_all(sent.reshape(128, 8, CHAN), ('row', 'col'), 0, 0)  45.5 us
    pallas_call x8, Pallas kernels, call(): pl.pallas_call(kernel, out_shape=[jax.ShapeDtypeStruct(shape, dtype) for...  13 us
    ppermute x7, starting transfers between devices, swap_rows(): came[k] = lax.ppermute(pieces[k], 'row', pairs(k))  9.8 us
    all_to_all x1, starting transfers between devices, on_device(): lax.all_to_all(row_packed.reshape(16, 32, 256), 'col', 0, 0)  8.73 us
    ppermute x4, starting transfers between devices, swap_rows_in_steps(): lax.ppermute(piece, 'row', [(i, i ^ 1) for i in range(8)])  4.97 us
    ppermute x3, starting transfers between devices, swap_rows_in_steps(): lax.ppermute(pieces[s], 'row', along(s))  4.88 us
    all_to_all x1, starting transfers between devices, on_device(): sums = lax.all_to_all(sums, ('row', 'col'), 0, 0).reshape(2048, 128)  4.33 us
    ppermute x7, waiting for transfers between devices, swap_rows(): came[k] = lax.ppermute(pieces[k], 'row', pairs(k))  3.39 us
  transfers between devices with their start and end apart: 16, of which 6 were waited for; matrix products, arithmetic and copies ran while one was open for 0% of the time, Pallas kernels for 3%

profile of v5, /device:TPU:1, one launch (start us, length us, event | category | flops | bytes accessed | tf_op | source)
XLA Modules:
  0.0 97.6 jit_solution(9299361747020318758)
XLA Ops:
  0.7 2.0 %shard_map.93 = bf16[512,256]{1,0:T(8,128)(2,1)} custom-call(bf16[512,192]{1,0:T(8,128)(2,1)} %bitcast.19, bf16[16,64,32]{2,1,0:T(8,128)(2,1)} %bitcast.21, bf16[16,6,2,32]{3,2,1,0:T(2,128)(2,1)} %bitcast.29), custom_call_target="tpu_custom_call" | custom-call | flops 100000000 | bytes 1000000 | tf_op jit(solution)/shard_map/pallas_call | solution.py:294
  2.7 8.7 %all-to-all-start = ((bf16[16,32,256]{2,1,0:T(8,128)(2,1)}), bf16[16,32,256]{2,1,0:T(8,128)(2,1)S(1)}, u32[]{:S(2)}, u32[]{:S(2)}) async-start(bf16[16,32,256]{2,1,0:T(8,128)(2,1)} %bitcast.31), calls=%async_computation | async-start | bytes 524288 | tf_op jit(solution)/shard_map/all_to_all | solution.py:329
  11.4 0.0 copy-done.4
  11.4 0.0 copy-done.5
  11.4 0.0 copy-done.1
  11.4 0.0 copy-done.2
  11.5 0.0 copy-start
  11.5 0.9 shard_map.95
  12.4 1.3 %collective-permute-start = (bf16[128,512]{1,0:T(8,128)(2,1)S(1)}, bf16[128,512]{1,0:T(8,128)(2,1)S(1)}, u32[]{:S(2)}, u32[]{:S(2)}) collective-permute-start(bf16[128,512]{1,0:T(8,128)(2,1)S(1)} %get-tuple-element.29), channel_id=1, source_target_pairs={{0,32},{16,48},{32,64},{48,80},{64,96},{80,112},{96,0},{112,16},{1... | collective-permute-start | bytes 393224 | tf_op jit(solution)/shard_map/ppermute | solution.py:315
  13.7 2.5 %collective-permute-start.1 = (bf16[128,512]{1,0:T(8,128)(2,1)S(1)}, bf16[128,512]{1,0:T(8,128)(2,1)S(1)}, u32[]{:S(2)}, u32[]{:S(2)}) collective-permute-start(bf16[128,512]{1,0:T(8,128)(2,1)S(1)} %get-tuple-element.30), channel_id=1, source_target_pairs={{0,64},{16,80},{32,96},{48,112},{64,0},{80,16},{96,32},{112,48},{1... | collective-permute-start | bytes 393224 | tf_op jit(solution)/shard_map/ppermute | solution.py:315
  16.2 1.2 %collective-permute-start.2 = (bf16[128,512]{1,0:T(8,128)(2,1)S(1)}, bf16[128,512]{1,0:T(8,128)(2,1)S(1)}, u32[]{:S(2)}, u32[]{:S(2)}) collective-permute-start(bf16[128,512]{1,0:T(8,128)(2,1)S(1)} %get-tuple-element.31), channel_id=1, source_target_pairs={{0,96},{16,112},{32,0},{48,16},{64,32},{80,48},{96,64},{112,80},{1... | collective-permute-start | bytes 393224 | tf_op jit(solution)/shard_map/ppermute | solution.py:315
  17.3 1.8 %collective-permute-start.3 = (bf16[128,512]{1,0:T(8,128)(2,1)S(1)}, bf16[128,512]{1,0:T(8,128)(2,1)S(1)}, u32[]{:S(2)}, u32[]{:S(2)}) collective-permute-start(bf16[128,512]{1,0:T(8,128)(2,1)S(1)} %get-tuple-element.28.refs_0_), channel_id=1, source_target_pairs={{0,16},{16,0},{32,48},{48,32},{64,80},{80,64},{96,112},{112,96},{1... | collective-permute-start | bytes 393224 | tf_op jit(solution)/shard_map/ppermute | solution.py:316
  19.1 0.0 collective-permute-done.refs_1_
  19.1 1.0 %collective-permute-start.4 = (bf16[128,512]{1,0:T(8,128)(2,1)S(1)}, bf16[128,512]{1,0:T(8,128)(2,1)S(1)}, u32[]{:S(2)}, u32[]{:S(2)}) collective-permute-start(bf16[128,512]{1,0:T(8,128)(2,1)S(1)} %collective-permute-done.refs_1_), channel_id=1, source_target_pairs={{0,16},{16,0},{32,48},{48,32},{64,80},{80,64},{96,112},{112,96},{1... | collective-permute-start | bytes 393224 | tf_op jit(solution)/shard_map/ppermute | solution.py:316
  20.1 1.1 %collective-permute-done.1.refs_2_ = bf16[128,512]{1,0:T(8,128)(2,1)S(1)} collective-permute-done((bf16[128,512]{1,0:T(8,128)(2,1)S(1)}, bf16[128,512]{1,0:T(8,128)(2,1)S(1)}, u32[]{:S(2)}, u32[]{:S(2)}) %collective-permute-start.1) | collective-permute-done | bytes 131104 | tf_op jit(solution)/shard_map/ppermute | solution.py:315
  21.2 2.2 %collective-permute-start.5 = (bf16[128,512]{1,0:T(8,128)(2,1)S(1)}, bf16[128,512]{1,0:T(8,128)(2,1)S(1)}, u32[]{:S(2)}, u32[]{:S(2)}) collective-permute-start(bf16[128,512]{1,0:T(8,128)(2,1)S(1)} %collective-permute-done.1.refs_2_), channel_id=1, source_target_pairs={{0,16},{16,0},{32,48},{48,32},{64,80},{80,64},{96,112},{112,96},{1... | collective-permute-start | bytes 393224 | tf_op jit(solution)/shard_map/ppermute | solution.py:316
  23.4 0.0 collective-permute-done.2.refs_3_
  23.4 0.0 collective-permute-start.6
  23.4 0.0 all-to-all-done
  23.4 0.0 copy-start.3
  23.4 1.3 %shard_map.94 = (bf16[512,384]{1,0:T(8,128)(2,1)S(1)}, bf16[512,256]{1,0:T(8,128)(2,1)S(1)}) custom-call(bf16[512,256]{1,0:T(8,128)(2,1)S(1)} %bitcast.28, bf16[192,768]{1,0:T(8,128)(2,1)S(1)} %copy-done), custom_call_target="tpu_custom_call" | custom-call | flops 30000001024 | bytes 1000000 | tf_op jit(solution)/shard_map/pallas_call | solution.py:294
  24.8 0.0 collective-permute-done.3.refs_4_
  24.8 0.0 collective-permute-done.4.refs_5_
  24.8 0.0 collective-permute-done.5.refs_6_
  24.8 0.0 collective-permute-done.6.refs_7_
  24.8 1.6 %shard_map.96 = (bf16[1024,384]{1,0:T(8,128)(2,1)S(1)}, bf16[512,512]{1,0:T(8,128)(2,1)S(1)}) custom-call(s32[1]{0:T(128)} %bitcast.place, bf16[512,384]{1,0:T(8,128)(2,1)S(1)} %get-tuple-element.27.row_out, bf16[192,768]{1,0:T(8,128)(2,1)S(1)} %copy-done, bf16[192,384]{1,0:T(8,128)(2,1)S(1)} %bitcast.25, bf16[128,512]{1,0:T(8,128)(2,1)S(1)} %get-tuple-element.28.refs_0_, ...), custom_call_target="tpu_custom_call" | custom-call | flops 100000000 | bytes 1000000 | tf_op jit(solution)/shard_map/pallas_call | solution.py:294
  26.5 25.1 %all_to_all.20 = bf16[128,8,384]{2,1,0:T(8,128)(2,1)S(1)} all-to-all(bf16[128,8,384]{2,1,0:T(8,128)(2,1)S(1)} %bitcast.23), channel_id=1, replica_groups=mesh['row'=8,'col'=16] {'row','col'}, dimensions={0} | all-to-all | bytes 1572864 | tf_op jit(solution)/shard_map/all_to_all | solution.py:348
  51.6 3.7 %shard_map.97 = (f32[512,192]{1,0:T(8,128)S(1)}, f32[512,192]{1,0:T(8,128)S(1)}, bf16[1024,384]{1,0:T(8,128)(2,1)S(1)}) custom-call(bf16[1024,384]{1,0:T(8,128)(2,1)S(1)} %bitcast.17, bf16[512,512]{1,0:T(8,128)(2,1)S(1)} %get-tuple-element.33.whole, bf16[512,256]{1,0:T(8,128)(2,1)S(1)} %get-tuple-element.34.packed, bf16[192,768]{1,0:T(8,128)(2,1)S(1)} %copy-done, ...), custom_call_target="tpu_custom_call" | custom-call | flops 100000000 | bytes 1000000 | tf_op jit(solution)/shard_map/pallas_call | solution.py:294
  55.3 20.4 %all_to_all.21.came = bf16[128,8,384]{2,1,0:T(8,128)(2,1)S(1)} all-to-all(bf16[128,8,384]{2,1,0:T(8,128)(2,1)S(1)} %bitcast.24), channel_id=1, replica_groups=mesh['row'=8,'col'=16] {'row','col'}, dimensions={0} | all-to-all | bytes 1572864 | tf_op jit(solution)/shard_map/all_to_all | solution.py:355
  75.6 1.0 shard_map.98
  76.6 4.3 %all-to-all-start.3 = ((bf16[128,16,128]{2,1,0:T(8,128)(2,1)}), bf16[128,16,128]{2,1,0:T(8,128)(2,1)S(1)}, u32[]{:S(2)}, u32[]{:S(2)}) async-start(bf16[128,16,128]{2,1,0:T(8,128)(2,1)} %shard_map.98), calls=%async_computation.3 | async-start | bytes 1048576 | tf_op jit(solution)/shard_map/all_to_all | solution.py:357
  81.0 0.3 shard_map.99
  81.3 3.0 %collective-permute-start.7 = (bf16[64,384]{1,0:T(8,128)(2,1)S(1)}, bf16[64,384]{1,0:T(8,128)(2,1)S(1)}, u32[]{:S(2)}, u32[]{:S(2)}) collective-permute-start(bf16[64,384]{1,0:T(8,128)(2,1)S(1)} %get-tuple-element.39), channel_id=1, source_target_pairs={{0,64},{16,80},{32,96},{48,112},{64,0},{80,16},{96,32},{112,48},{1... | collective-permute-start | bytes 147464 | tf_op jit(solution)/shard_map/ppermute | solution.py:309
  84.3 1.4 %collective-permute-start.8 = (bf16[64,384]{1,0:T(8,128)(2,1)S(1)}, bf16[64,384]{1,0:T(8,128)(2,1)S(1)}, u32[]{:S(2)}, u32[]{:S(2)}) collective-permute-start(bf16[64,384]{1,0:T(8,128)(2,1)S(1)} %get-tuple-element.40), channel_id=1, source_target_pairs={{0,80},{16,64},{32,112},{48,96},{64,16},{80,0},{96,48},{112,32},{1... | collective-permute-start | bytes 147464 | tf_op jit(solution)/shard_map/ppermute | solution.py:309
  85.7 0.5 collective-permute-start.9
  86.2 1.2 %collective-permute-start.10 = (bf16[64,384]{1,0:T(8,128)(2,1)S(1)}, bf16[64,384]{1,0:T(8,128)(2,1)S(1)}, u32[]{:S(2)}, u32[]{:S(2)}) collective-permute-start(bf16[64,384]{1,0:T(8,128)(2,1)S(1)} %get-tuple-element.42), channel_id=1, source_target_pairs={{0,48},{16,32},{32,80},{48,64},{64,112},{80,96},{96,16},{112,0},{1... | collective-permute-start | bytes 147464 | tf_op jit(solution)/shard_map/ppermute | solution.py:309
  87.5 1.5 %collective-permute-start.11 = (bf16[64,384]{1,0:T(8,128)(2,1)S(1)}, bf16[64,384]{1,0:T(8,128)(2,1)S(1)}, u32[]{:S(2)}, u32[]{:S(2)}) collective-permute-start(bf16[64,384]{1,0:T(8,128)(2,1)S(1)} %get-tuple-element.43), channel_id=1, source_target_pairs={{0,96},{16,112},{32,0},{48,16},{64,32},{80,48},{96,64},{112,80},{1... | collective-permute-start | bytes 147464 | tf_op jit(solution)/shard_map/ppermute | solution.py:309
  89.0 1.7 %collective-permute-done.7.refs_1_ = bf16[64,384]{1,0:T(8,128)(2,1)S(1)} collective-permute-done((bf16[64,384]{1,0:T(8,128)(2,1)S(1)}, bf16[64,384]{1,0:T(8,128)(2,1)S(1)}, u32[]{:S(2)}, u32[]{:S(2)}) %collective-permute-start.7) | collective-permute-done | bytes 49184 | tf_op jit(solution)/shard_map/ppermute | solution.py:309
  90.6 2.1 %collective-permute-start.12 = (bf16[64,384]{1,0:T(8,128)(2,1)S(1)}, bf16[64,384]{1,0:T(8,128)(2,1)S(1)}, u32[]{:S(2)}, u32[]{:S(2)}) collective-permute-start(bf16[64,384]{1,0:T(8,128)(2,1)S(1)} %get-tuple-element.44), channel_id=1, source_target_pairs={{0,112},{16,96},{32,16},{48,0},{64,48},{80,32},{96,80},{112,64},{1... | collective-permute-start | bytes 147464 | tf_op jit(solution)/shard_map/ppermute | solution.py:309
  92.7 0.0 collective-permute-done.8.refs_2_
  92.7 0.0 collective-permute-start.13
  92.8 0.3 collective-permute-done.9.refs_3_
  93.1 0.8 collective-permute-done.10.refs_4_
  93.9 0.0 collective-permute-done.11.refs_5_
  93.9 0.6 collective-permute-done.12.refs_6_
  94.5 0.0 collective-permute-done.13.refs_7_
  94.5 1.0 %all-to-all-done.3 = bf16[128,16,128]{2,1,0:T(8,128)(2,1)S(1)} async-done(((bf16[128,16,128]{2,1,0:T(8,128)(2,1)}), bf16[128,16,128]{2,1,0:T(8,128)(2,1)S(1)}, u32[]{:S(2)}, u32[]{:S(2)}) %all-to-all-start.3) | async-done | bytes 524320 | tf_op jit(solution)/shard_map/all_to_all | solution.py:357
  95.5 2.1 %shard_map.100 = (bf16[512,192]{1,0:T(8,128)(2,1)}, bf16[512,192]{1,0:T(8,128)(2,1)}, f32[192,768]{1,0:T(8,128)}, f32[192,384]{1,0:T(8,128)}) custom-call(s32[1]{0:T(128)} %bitcast.place, bf16[2048,128]{1,0:T(8,128)(2,1)S(1)} %bitcast.18, bf16[64,384]{1,0:T(8,128)(2,1)S(1)} %get-tuple-element.38.refs_0_, bf16[64,384]{1,0:T(8,128)(2,1)S(1)} %collective-permute-done.7.refs_1_, ...), custom_call_target="tpu_custom_call" | custom-call | flops 100000000 | bytes 1000000 | tf_op jit(solution)/shard_map/pallas_call | solution.py:294
  (6 shorter events, 0.0 us)
Async XLA Ops:
  0.6 10.8 %copy-start.4 = (bf16[16,32,192]{2,1,0:T(8,128)(2,1)S(1)}, bf16[16,32,192]{2,1,0:T(8,128)(2,1)}, u32[]{:S(2)}) copy-start(bf16[16,32,192]{2,1,0:T(8,128)(2,1)} %param.11) | copy-start | bytes 589828
  0.6 10.8 %copy-start.5 = (bf16[16,32,2,6]{1,2,3,0:T(2,128)(2,1)S(1)}, bf16[16,32,2,6]{1,2,3,0:T(2,128)(2,1)}, u32[]{:S(2)}) copy-start(bf16[16,32,2,6]{1,2,3,0:T(2,128)(2,1)} %param.8) | copy-start | bytes 36868
  2.7 8.8 %copy-start.1 = (bf16[16,32,192]{2,1,0:T(8,128)(2,1)S(1)}, bf16[16,32,192]{2,1,0:T(8,128)(2,1)}, u32[]{:S(2)}) copy-start(bf16[16,32,192]{2,1,0:T(8,128)(2,1)} %param.6) | copy-start | bytes 589828
  2.7 8.8 %copy-start.2 = (bf16[16,32,4,16]{1,3,2,0:T(8,128)(2,1)S(1)}, bf16[16,32,4,16]{1,3,2,0:T(8,128)(2,1)}, u32[]{:S(2)}) copy-start(bf16[16,32,4,16]{1,3,2,0:T(8,128)(2,1)} %param.7) | copy-start | bytes 196612
  2.7 20.7 %all-to-all-start = ((bf16[16,32,256]{2,1,0:T(8,128)(2,1)}), bf16[16,32,256]{2,1,0:T(8,128)(2,1)S(1)}, u32[]{:S(2)}, u32[]{:S(2)}) async-start(bf16[16,32,256]{2,1,0:T(8,128)(2,1)} %bitcast.31), calls=%async_computation | async-start | bytes 524288 | tf_op jit(solution)/shard_map/all_to_all | solution.py:329
  11.5 12.0 %copy-start = (bf16[192,768]{1,0:T(8,128)(2,1)S(1)}, bf16[192,768]{1,0:T(8,128)(2,1)}, u32[]{:S(2)}) copy-start(bf16[192,768]{1,0:T(8,128)(2,1)} %w_in.5) | copy-start | bytes 884740
  12.4 6.7 %collective-permute-start = (bf16[128,512]{1,0:T(8,128)(2,1)S(1)}, bf16[128,512]{1,0:T(8,128)(2,1)S(1)}, u32[]{:S(2)}, u32[]{:S(2)}) collective-permute-start(bf16[128,512]{1,0:T(8,128)(2,1)S(1)} %get-tuple-element.29), channel_id=1, source_target_pairs={{0,32},{16,48},{32,64},{48,80},{64,96},{80,112},{96,0},{112,16},{1... | collective-permute-start | bytes 393224 | tf_op jit(solution)/shard_map/ppermute | solution.py:315
  13.7 7.5 %collective-permute-start.1 = (bf16[128,512]{1,0:T(8,128)(2,1)S(1)}, bf16[128,512]{1,0:T(8,128)(2,1)S(1)}, u32[]{:S(2)}, u32[]{:S(2)}) collective-permute-start(bf16[128,512]{1,0:T(8,128)(2,1)S(1)} %get-tuple-element.30), channel_id=1, source_target_pairs={{0,64},{16,80},{32,96},{48,112},{64,0},{80,16},{96,32},{112,48},{1... | collective-permute-start | bytes 393224 | tf_op jit(solution)/shard_map/ppermute | solution.py:315
  16.2 7.3 %collective-permute-start.2 = (bf16[128,512]{1,0:T(8,128)(2,1)S(1)}, bf16[128,512]{1,0:T(8,128)(2,1)S(1)}, u32[]{:S(2)}, u32[]{:S(2)}) collective-permute-start(bf16[128,512]{1,0:T(8,128)(2,1)S(1)} %get-tuple-element.31), channel_id=1, source_target_pairs={{0,96},{16,112},{32,0},{48,16},{64,32},{80,48},{96,64},{112,80},{1... | collective-permute-start | bytes 393224 | tf_op jit(solution)/shard_map/ppermute | solution.py:315
  17.3 7.5 %collective-permute-start.3 = (bf16[128,512]{1,0:T(8,128)(2,1)S(1)}, bf16[128,512]{1,0:T(8,128)(2,1)S(1)}, u32[]{:S(2)}, u32[]{:S(2)}) collective-permute-start(bf16[128,512]{1,0:T(8,128)(2,1)S(1)} %get-tuple-element.28.refs_0_), channel_id=1, source_target_pairs={{0,16},{16,0},{32,48},{48,32},{64,80},{80,64},{96,112},{112,96},{1... | collective-permute-start | bytes 393224 | tf_op jit(solution)/shard_map/ppermute | solution.py:316
  19.1 5.7 %collective-permute-start.4 = (bf16[128,512]{1,0:T(8,128)(2,1)S(1)}, bf16[128,512]{1,0:T(8,128)(2,1)S(1)}, u32[]{:S(2)}, u32[]{:S(2)}) collective-permute-start(bf16[128,512]{1,0:T(8,128)(2,1)S(1)} %collective-permute-done.refs_1_), channel_id=1, source_target_pairs={{0,16},{16,0},{32,48},{48,32},{64,80},{80,64},{96,112},{112,96},{1... | collective-permute-start | bytes 393224 | tf_op jit(solution)/shard_map/ppermute | solution.py:316
  21.2 3.5 %collective-permute-start.5 = (bf16[128,512]{1,0:T(8,128)(2,1)S(1)}, bf16[128,512]{1,0:T(8,128)(2,1)S(1)}, u32[]{:S(2)}, u32[]{:S(2)}) collective-permute-start(bf16[128,512]{1,0:T(8,128)(2,1)S(1)} %collective-permute-done.1.refs_2_), channel_id=1, source_target_pairs={{0,16},{16,0},{32,48},{48,32},{64,80},{80,64},{96,112},{112,96},{1... | collective-permute-start | bytes 393224 | tf_op jit(solution)/shard_map/ppermute | solution.py:316
  23.4 1.4 %collective-permute-start.6 = (bf16[128,512]{1,0:T(8,128)(2,1)S(1)}, bf16[128,512]{1,0:T(8,128)(2,1)S(1)}, u32[]{:S(2)}, u32[]{:S(2)}) collective-permute-start(bf16[128,512]{1,0:T(8,128)(2,1)S(1)} %collective-permute-done.2.refs_3_), channel_id=1, source_target_pairs={{0,16},{16,0},{32,48},{48,32},{64,80},{80,64},{96,112},{112,96},{1... | collective-permute-start | bytes 393224 | tf_op jit(solution)/shard_map/ppermute | solution.py:316
  23.4 1.4 %copy-start.3 = (bf16[384,192]{0,1:T(8,128)(2,1)S(1)}, bf16[384,192]{0,1:T(8,128)(2,1)}, u32[]{:S(2)}) copy-start(bf16[384,192]{0,1:T(8,128)(2,1)} %param.10) | copy-start | bytes 442372
  76.6 18.8 %all-to-all-start.3 = ((bf16[128,16,128]{2,1,0:T(8,128)(2,1)}), bf16[128,16,128]{2,1,0:T(8,128)(2,1)S(1)}, u32[]{:S(2)}, u32[]{:S(2)}) async-start(bf16[128,16,128]{2,1,0:T(8,128)(2,1)} %shard_map.98), calls=%async_computation.3 | async-start | bytes 1048576 | tf_op jit(solution)/shard_map/all_to_all | solution.py:357
  81.3 9.4 %collective-permute-start.7 = (bf16[64,384]{1,0:T(8,128)(2,1)S(1)}, bf16[64,384]{1,0:T(8,128)(2,1)S(1)}, u32[]{:S(2)}, u32[]{:S(2)}) collective-permute-start(bf16[64,384]{1,0:T(8,128)(2,1)S(1)} %get-tuple-element.39), channel_id=1, source_target_pairs={{0,64},{16,80},{32,96},{48,112},{64,0},{80,16},{96,32},{112,48},{1... | collective-permute-start | bytes 147464 | tf_op jit(solution)/shard_map/ppermute | solution.py:309
  84.3 8.5 %collective-permute-start.8 = (bf16[64,384]{1,0:T(8,128)(2,1)S(1)}, bf16[64,384]{1,0:T(8,128)(2,1)S(1)}, u32[]{:S(2)}, u32[]{:S(2)}) collective-permute-start(bf16[64,384]{1,0:T(8,128)(2,1)S(1)} %get-tuple-element.40), channel_id=1, source_target_pairs={{0,80},{16,64},{32,112},{48,96},{64,16},{80,0},{96,48},{112,32},{1... | collective-permute-start | bytes 147464 | tf_op jit(solution)/shard_map/ppermute | solution.py:309
  85.7 7.4 %collective-permute-start.9 = (bf16[64,384]{1,0:T(8,128)(2,1)S(1)}, bf16[64,384]{1,0:T(8,128)(2,1)S(1)}, u32[]{:S(2)}, u32[]{:S(2)}) collective-permute-start(bf16[64,384]{1,0:T(8,128)(2,1)S(1)} %get-tuple-element.41), channel_id=1, source_target_pairs={{0,32},{16,48},{32,64},{48,80},{64,96},{80,112},{96,0},{112,16},{1... | collective-permute-start | bytes 147464 | tf_op jit(solution)/shard_map/ppermute | solution.py:309
  86.2 7.6 %collective-permute-start.10 = (bf16[64,384]{1,0:T(8,128)(2,1)S(1)}, bf16[64,384]{1,0:T(8,128)(2,1)S(1)}, u32[]{:S(2)}, u32[]{:S(2)}) collective-permute-start(bf16[64,384]{1,0:T(8,128)(2,1)S(1)} %get-tuple-element.42), channel_id=1, source_target_pairs={{0,48},{16,32},{32,80},{48,64},{64,112},{80,96},{96,16},{112,0},{1... | collective-permute-start | bytes 147464 | tf_op jit(solution)/shard_map/ppermute | solution.py:309
  87.5 6.4 %collective-permute-start.11 = (bf16[64,384]{1,0:T(8,128)(2,1)S(1)}, bf16[64,384]{1,0:T(8,128)(2,1)S(1)}, u32[]{:S(2)}, u32[]{:S(2)}) collective-permute-start(bf16[64,384]{1,0:T(8,128)(2,1)S(1)} %get-tuple-element.43), channel_id=1, source_target_pairs={{0,96},{16,112},{32,0},{48,16},{64,32},{80,48},{96,64},{112,80},{1... | collective-permute-start | bytes 147464 | tf_op jit(solution)/shard_map/ppermute | solution.py:309
  90.6 3.8 %collective-permute-start.12 = (bf16[64,384]{1,0:T(8,128)(2,1)S(1)}, bf16[64,384]{1,0:T(8,128)(2,1)S(1)}, u32[]{:S(2)}, u32[]{:S(2)}) collective-permute-start(bf16[64,384]{1,0:T(8,128)(2,1)S(1)} %get-tuple-element.44), channel_id=1, source_target_pairs={{0,112},{16,96},{32,16},{48,0},{64,48},{80,32},{96,80},{112,64},{1... | collective-permute-start | bytes 147464 | tf_op jit(solution)/shard_map/ppermute | solution.py:309
  92.7 1.7 %collective-permute-start.13 = (bf16[64,384]{1,0:T(8,128)(2,1)S(1)}, bf16[64,384]{1,0:T(8,128)(2,1)S(1)}, u32[]{:S(2)}, u32[]{:S(2)}) collective-permute-start(bf16[64,384]{1,0:T(8,128)(2,1)S(1)} %get-tuple-element.45), channel_id=1, source_target_pairs={{0,16},{16,0},{32,48},{48,32},{64,80},{80,64},{96,112},{112,96},{1... | collective-permute-start | bytes 147464 | tf_op jit(solution)/shard_map/ppermute | solution.py:309
